TPU v7x, 128 devices: a whole 4x4x4 slice. The times are simulated.
128 devices in a mesh: dom: 32 (over z, y, core), node: 4 (over x).
Axes of the slice: x: 4, y: 4, z: 4, core: 2. Of those that a mesh axis runs over, the one named last changes fastest.
Arguments:
- features: bfloat16 [65536, 256], P(('dom', 'node')), may hold values from -14 to 14
- w_query: bfloat16 [256, 256], replicated, may hold values from -0.375 to 0.375
- w_key: bfloat16 [256, 256], replicated, may hold values from -0.375 to 0.375
- w_value: bfloat16 [256, 256], replicated, may hold values from -0.375 to 0.375
- w_out: bfloat16 [256, 256], replicated, may hold values from -0.375 to 0.375
- w_expand: bfloat16 [256, 1024], replicated, may hold values from -0.375 to 0.375
- w_reduce: bfloat16 [1024, 256], replicated, may hold values from -0.1875 to 0.1875
- gain_attn: float32 [256], replicated, may hold values from 0.25 to 1.75
- gain_ffn: float32 [256], replicated, may hold values from 0.25 to 1.75
- tile_mask: int32 [65536, 7, 128], P(('dom', 'node')), may hold values 0 or 1
- local_block: int32 [512, 2], P(('dom', 'node')), may hold values from 0 to 15
- remote_slot: int32 [512, 4], P(('dom', 'node')), may hold values from 0 to 63, as said below
- remote_block: int32 [32, 4, 64], P('dom', 'node'), may hold values from 0 to 15
- d_out: bfloat16 [65536, 256], P(('dom', 'node')), may hold values from -6 to 6
Outputs:
- output: bfloat16 [65536, 256], P(('dom', 'node'))
- d_x: bfloat16 [65536, 256], P(('dom', 'node'))
- grad_query: float32 [256, 256], replicated
- grad_key: float32 [256, 256], replicated
- grad_value: float32 [256, 256], replicated
- grad_out: float32 [256, 256], replicated
- grad_expand: float32 [256, 1024], replicated
- grad_reduce: float32 [1024, 256], replicated
Inputs may be any that keep to these rules, and one draw needn't show every extreme that they name: `remote_slot`: within the rows of one device the slots are distinct; slot s asks partition s // 2; on every device some partition is asked for exactly 2 blocks.
All inputs are finite; a program needn't handle non-finite values. No bound on the sum of `tile_mask` on one device may be relied on, other than what follows from the above.
Results may differ from a plain program's by a relative error of at most 0.013.
The roundings to bfloat16 on the way count: a program that leaves them out, or rounds other values in their place, can miss the bound.
Values may be sent and summed in bfloat16 or wider, within the bound.
A program may use at most 192 MiB of HBM per device.

v0:
```python
import math

import jax
import jax.numpy as jnp
from jax import lax
from jax.sharding import PartitionSpec as P

HEADS = 8


EPSILON = 1e-05


def layer_norm(values, gain):
    center = values - jnp.mean(values, -1, keepdims=True)
    spread = jnp.mean(center * center, -1, keepdims=True)
    return center * lax.rsqrt(spread + EPSILON) * gain


def gelu_tanh(values):
    return jax.nn.gelu(values, approximate=True)


def split_heads(query_rows, pair_rows):
    groups, block_len, width = query_rows.shape
    head_dim = width // HEADS
    query_heads = query_rows.reshape(groups, block_len, HEADS, head_dim)
    key_heads = pair_rows[..., :width].reshape(groups, -1, HEADS, head_dim)
    value_heads = pair_rows[..., width:].reshape(groups, -1, HEADS, head_dim)
    return (query_heads, key_heads, value_heads, 1.0 / math.sqrt(head_dim))


def attend(query_rows, pair_rows, allowed):
    groups, block_len, width = query_rows.shape
    query_heads, key_heads, value_heads, score_scale = split_heads(query_rows, pair_rows)
    scores = (
        jnp.einsum("gqhd,gkhd->ghqk", query_heads, key_heads, preferred_element_type=jnp.float32)
        * score_scale
    )
    visible = allowed[:, None]
    row_max = jnp.max(jnp.where(visible, scores, -jnp.inf), -1, keepdims=True)
    weights_raw = jnp.where(visible, jnp.exp(scores - row_max), 0.0)
    row_total = jnp.sum(weights_raw, -1, keepdims=True)
    probs = weights_raw / row_total
    probs_low = probs.astype(jnp.bfloat16)
    mixed = jnp.einsum(
        "ghqk,gkhd->gqhd", probs_low, value_heads, preferred_element_type=jnp.float32
    )
    return (mixed.astype(jnp.bfloat16).reshape(groups, block_len, width), probs, probs_low)


def attend_back(query_rows, pair_rows, probs, probs_low, d_mixed):
    groups, block_len, width = query_rows.shape
    query_heads, key_heads, value_heads, score_scale = split_heads(query_rows, pair_rows)
    d_heads = d_mixed.reshape(groups, block_len, HEADS, -1)
    d_probs = jnp.einsum(
        "gqhd,gkhd->ghqk", d_heads, value_heads, preferred_element_type=jnp.float32
    )
    d_values = jnp.einsum("ghqk,gqhd->gkhd", probs_low, d_heads, preferred_element_type=jnp.float32)
    inner = jnp.sum(probs * d_probs, -1, keepdims=True)
    d_scores = (probs * (d_probs - inner) * score_scale).astype(jnp.bfloat16)
    d_query = jnp.einsum(
        "ghqk,gkhd->gqhd", d_scores, key_heads, preferred_element_type=jnp.float32
    ).reshape(groups, block_len, width)
    d_keys = jnp.einsum(
        "ghqk,gqhd->gkhd", d_scores, query_heads, preferred_element_type=jnp.float32
    )
    d_pairs = jnp.concatenate(
        [d_keys.reshape(groups, -1, width), d_values.reshape(groups, -1, width)], -1
    )
    return (d_query, d_pairs)


def feed_tail(features, mixed_rows, w_out, w_expand, w_reduce, gain_attn, gain_ffn, d_out):
    residual = features.astype(jnp.float32) + jnp.dot(
        mixed_rows, w_out, preferred_element_type=jnp.float32
    )
    first_norm, first_back = jax.vjp(lambda values: layer_norm(values, gain_attn), residual)
    first_low = first_norm.astype(jnp.bfloat16)
    pre_act = jnp.dot(first_low, w_expand, preferred_element_type=jnp.float32)
    activation, gelu_back = jax.vjp(gelu_tanh, pre_act)
    act_low = activation.astype(jnp.bfloat16)
    second_in = first_low.astype(jnp.float32) + jnp.dot(
        act_low, w_reduce, preferred_element_type=jnp.float32
    )
    result, second_back = jax.vjp(lambda values: layer_norm(values, gain_ffn), second_in)
    output = result.astype(jnp.bfloat16)
    d_second = second_back(d_out.astype(jnp.float32))[0]
    d_second_low = d_second.astype(jnp.bfloat16)
    reduce_sum = jnp.dot(act_low.T, d_second_low, preferred_element_type=jnp.float32)
    d_pre = gelu_back(jnp.dot(d_second_low, w_reduce.T, preferred_element_type=jnp.float32))[0]
    d_pre_low = d_pre.astype(jnp.bfloat16)
    expand_sum = jnp.dot(first_low.T, d_pre_low, preferred_element_type=jnp.float32)
    d_first = d_second + jnp.dot(d_pre_low, w_expand.T, preferred_element_type=jnp.float32)
    d_resid = first_back(d_first)[0]
    d_resid_low = d_resid.astype(jnp.bfloat16)
    out_sum = jnp.dot(mixed_rows.T, d_resid_low, preferred_element_type=jnp.float32)
    d_mixed = jnp.dot(d_resid_low, w_out.T, preferred_element_type=jnp.float32).astype(jnp.bfloat16)
    return (output, d_resid, d_mixed, out_sum, expand_sum, reduce_sum)


def on_device(
    features,
    w_query,
    w_key,
    w_value,
    w_out,
    w_expand,
    w_reduce,
    gain_attn,
    gain_ffn,
    tile_mask,
    local_block,
    remote_slot,
    remote_block,
    d_out,
):
    rows, width = features.shape
    tile_count = tile_mask.shape[1]
    block_len = tile_mask.shape[2]
    row_blocks = rows // block_len
    dom_count = lax.axis_size("dom")
    node_count = lax.axis_size("node")
    node_index = lax.axis_index("node")
    part_count = node_count * row_blocks
    slot_count = remote_block.shape[2]
    capacity = slot_count // dom_count
    near_tiles = local_block.shape[1] + 1
    w_pair = jnp.concatenate([w_key, w_value], 1)
    pair_width = 2 * width
    queries = jnp.dot(features, w_query, preferred_element_type=jnp.float32).astype(jnp.bfloat16)
    wanted = lax.all_to_all(
        remote_block.reshape(dom_count, capacity), "dom", split_axis=0, concat_axis=0, tiled=True
    )
    wanted_flat = wanted.reshape(-1)
    own_pairs = jnp.dot(features, w_pair, preferred_element_type=jnp.float32).astype(jnp.bfloat16)
    part_pairs = lax.all_gather(own_pairs, "node", axis=0, tiled=True).reshape(
        part_count, block_len, pair_width
    )
    far_pairs = lax.all_to_all(
        part_pairs[wanted], "dom", split_axis=0, concat_axis=0, tiled=True
    ).reshape(slot_count, block_len, pair_width)
    self_ids = node_index * row_blocks + jnp.arange(row_blocks, dtype=jnp.int32)
    near_ids = jnp.concatenate([self_ids[:, None], local_block], 1)
    diagonal = (jnp.arange(block_len)[:, None] == jnp.arange(block_len)[None, :]).astype(jnp.int32)
    mask_blocks = tile_mask.reshape(row_blocks, block_len, tile_count, block_len)
    own_part = jnp.maximum(mask_blocks[:, :, 0:1, :], diagonal[None, :, None, :])
    mask_blocks = jnp.concatenate([own_part, mask_blocks[:, :, 1:, :]], 2)
    group_size = 4
    group_count = row_blocks // group_size
    query_groups = queries.reshape(group_count, group_size, block_len, width)
    near_groups = near_ids.reshape(group_count, group_size, near_tiles)
    far_groups = remote_slot.reshape(group_count, group_size, tile_count - near_tiles)
    keep_groups = (mask_blocks > 0).reshape(
        group_count, group_size, block_len, tile_count * block_len
    )

    def gather_tiles(near_sel, far_sel):
        tiles_here = jnp.concatenate([part_pairs[near_sel], far_pairs[far_sel]], 1)
        return tiles_here.reshape(group_size, tile_count * block_len, pair_width)

    def forward_group(items):
        query_part, near_sel, far_sel, keep_part = items
        return attend(query_part, gather_tiles(near_sel, far_sel), keep_part)[0]

    mixed_rows = lax.map(
        forward_group, (query_groups, near_groups, far_groups, keep_groups)
    ).reshape(rows, width)
    output, d_resid, d_mixed, out_sum, expand_sum, reduce_sum = feed_tail(
        features, mixed_rows, w_out, w_expand, w_reduce, gain_attn, gain_ffn, d_out
    )
    mixed_groups = d_mixed.reshape(group_count, group_size, block_len, width)

    def backward_group(carry, items):
        near_acc, far_acc = carry
        query_part, near_sel, far_sel, keep_part, grad_part = items
        pair_rows = gather_tiles(near_sel, far_sel)
        unused, probs, probs_low = attend(query_part, pair_rows, keep_part)
        d_query, d_pairs = attend_back(query_part, pair_rows, probs, probs_low, grad_part)
        d_pairs = d_pairs.reshape(group_size, tile_count, block_len, pair_width)
        near_acc = near_acc.at[near_sel.reshape(-1)].add(
            d_pairs[:, :near_tiles].reshape(-1, block_len, pair_width)
        )
        far_acc = far_acc.at[far_sel.reshape(-1)].add(
            d_pairs[:, near_tiles:].reshape(-1, block_len, pair_width)
        )
        return ((near_acc, far_acc), d_query)

    start = (
        jnp.zeros((part_count, block_len, pair_width), jnp.float32),
        jnp.zeros((slot_count, block_len, pair_width), jnp.float32),
    )
    (near_acc, far_acc), query_grads = lax.scan(
        backward_group, start, (query_groups, near_groups, far_groups, keep_groups, mixed_groups)
    )
    d_query = query_grads.reshape(rows, width).astype(jnp.bfloat16)
    query_sum = jnp.dot(features.T, d_query, preferred_element_type=jnp.float32)
    d_rows = d_resid + jnp.dot(d_query, w_query.T, preferred_element_type=jnp.float32)
    pair_full = w_pair.astype(jnp.float32)
    near_low = near_acc.astype(jnp.bfloat16)
    far_low = far_acc.astype(jnp.bfloat16)
    returned = lax.all_to_all(
        far_low.reshape(dom_count, capacity, block_len, pair_width),
        "dom",
        split_axis=0,
        concat_axis=0,
        tiled=True,
    )
    combined = (
        near_low.astype(jnp.float32)
        .at[wanted_flat]
        .add(returned.reshape(slot_count, block_len, pair_width).astype(jnp.float32))
    )
    own_grads = lax.psum_scatter(
        combined.reshape(part_count * block_len, pair_width).astype(jnp.bfloat16),
        "node",
        scatter_dimension=0,
        tiled=True,
    ).astype(jnp.float32)
    pair_sum = jnp.dot(features.astype(jnp.float32).T, own_grads, precision=lax.Precision.HIGHEST)
    d_rows = d_rows + jnp.dot(own_grads, pair_full.T, precision=lax.Precision.HIGHEST)
    totals = lax.psum(
        (query_sum, pair_sum[:, :width], pair_sum[:, width:], out_sum, expand_sum, reduce_sum),
        ("dom", "node"),
    )
    factor = 1.0 / math.sqrt(rows * dom_count * node_count)
    scaled = tuple((summed * factor for summed in totals))
    return (output, d_rows.astype(jnp.bfloat16)) + scaled


def solution(mesh):
    placed = (
        P(("dom", "node"), None),
        P(),
        P(),
        P(),
        P(),
        P(),
        P(),
        P(),
        P(),
        P(("dom", "node"), None, None),
        P(("dom", "node"), None),
        P(("dom", "node"), None),
        P("dom", "node", None),
        P(("dom", "node"), None),
    )
    return jax.shard_map(
        on_device,
        mesh=mesh,
        in_specs=placed,
        out_specs=(
            P(("dom", "node"), None),
            P(("dom", "node"), None),
            P(),
            P(),
            P(),
            P(),
            P(),
            P(),
        ),
        check_vma=False,
    )
```

profile of v0, /device:TPU:0, one launch (start us, length us, event | category | flops | bytes accessed | tf_op | source)
XLA Modules:
  0.0 681.7 jit_solution(8670200628323994540)
XLA Ops:
  14.5 8.4 %all-to-all-start = ((s32[32,1,2]{2,1,0:T(1,128)}), s32[32,1,2]{2,1,0:T(1,128)S(1)}, u32[]{:S(2)}, u32[]{:S(2)}) async-start(s32[32,1,2]{2,1,0:T(1,128)} %bitcast.5), calls=%async_computation | async-start | bytes 32768 | tf_op jit(solution)/shard_map/all_to_all | solution.py:132
  23.8 6.4 all-to-all-done
  31.1 14.3 %all-gather.2.cloned.1.call-done = bf16[2048,512]{0,1:T(8,128)(2,1)} async-done(((bf16[512,512]{0,1:T(8,128)(2,1)}), bf16[2048,512]{0,1:T(8,128)(2,1)}) %all-gather.2.cloned.1.call-update) | async-done | bytes 2097168 | tf_op jit(solution)/shard_map/all_gather | solution.py:137
  48.2 5.5 gather_fusion.1
  53.8 7.5 %all-to-all-start.1 = ((bf16[32,2,128,512]{3,2,1,0:T(8,128)(2,1)}), bf16[32,2,128,512]{3,2,1,0:T(8,128)(2,1)}, u32[]{:S(2)}, u32[]{:S(2)}) async-start(bf16[32,2,128,512]{3,2,1,0:T(8,128)(2,1)} %bitcast.109), calls=%async_computation.1 | async-start | bytes 16777216 | tf_op jit(solution)/shard_map/all_to_all | solution.py:140
  74.2 93.0 %all-to-all-done.1 = bf16[32,2,128,512]{3,2,1,0:T(8,128)(2,1)} async-done(((bf16[32,2,128,512]{3,2,1,0:T(8,128)(2,1)}), bf16[32,2,128,512]{3,2,1,0:T(8,128)(2,1)}, u32[]{:S(2)}, u32[]{:S(2)}) %all-to-all-start.1) | async-done | bytes 8388640 | tf_op jit(solution)/shard_map/all_to_all | solution.py:140
  180.4 12.4 %fusion.91 = (f32[4,8,128]{2,1,0:T(8,128)S(1)}, f32[4,8,128,896]{3,2,1,0:T(8,128)}) fusion(pred[4,128,896]{2,1,0:T(8,128)(4,1)S(1)} %copy-done.23, bf16[4,896,8,32]{1,3,2,0:T(8,128)(2,1)} %bitcast.124, bf16[4,128,8,32]{1,0,3,2:T(4,128)(2,1)S(1)} %reshape.392), kind=kOutput, calls=%fused_computation.135 | convolution fusion | flops 491783040 | bytes 17252352 | tf_op jit(solution)/shard_map/while/body/eval_jaxpr/sub | solution.py:42
  192.8 7.9 %fusion.47 = bf16[4,128,8,32]{1,3,2,0:T(8,128)(2,1)S(1)} fusion(bf16[4,896,8,32]{1,3,2,0:T(8,128)(2,1)S(1)} %bitcast.115, f32[4,8,128,896]{3,2,1,0:T(8,128)} %get-tuple-element.116, f32[4,8,128]{2,1,0:T(8,128)S(1)} %get-tuple-element.115), kind=kOutput, calls=%fused_computation.56 | convolution fusion | flops 242352128 | bytes 16793600 | tf_op jit(solution)/shard_map/while/body/eval_jaxpr/ghqk,gkhd->gqhd/dot_general | solution.py:46
  209.1 8.3 %fusion.29 = f32[4,896,8,32]{1,3,2,0:T(8,128)} fusion(bf16[4,128,8,32]{1,0,3,2:T(4,128)(2,1)S(1)} %reshape.395, f32[4,8,128,896]{3,2,1,0:T(8,128)} %get-tuple-element.116, f32[4,8,128]{2,1,0:T(8,128)S(1)} %get-tuple-element.115), kind=kOutput, calls=%fused_computation.38 | convolution fusion | flops 242221056 | bytes 18628608 | tf_op jit(solution)/shard_map/while/body/eval_jaxpr/ghqk,gqhd->gkhd/dot_general | solution.py:59
  217.4 7.2 %fusion.63 = f32[4,8,128,896]{3,2,1,0:T(8,128)} fusion(bf16[4,896,8,32]{1,3,2,0:T(8,128)(2,1)S(1)} %bitcast.116, bf16[4,128,8,32]{1,0,3,2:T(4,128)(2,1)S(1)} %reshape.395), kind=kOutput, calls=%fused_computation.83 | convolution fusion | flops 234881024 | bytes 16777216 | tf_op jit(solution)/shard_map/while/body/eval_jaxpr/gqhd,gkhd->ghqk/dot_general | solution.py:56
  229.4 33.0 %fusion.32 = f32[4,896,8,32]{1,3,2,0:T(8,128)} fusion(f32[4,8,128,896]{3,2,1,0:T(8,128)} %fusion.63, bf16[4,128,8,32]{1,0,3,2:T(4,128)(2,1)S(1)} %copy-done.26, f32[4,8,128,896]{3,2,1,0:T(8,128)} %get-tuple-element.116, f32[4,8,128]{2,1,0:T(8,128)S(1)} %get-tuple-element.115), kind=kOutput, calls=%fused_computation.39 | convolution fusion | flops 260576128 | bytes 33308672 | tf_op jit(solution)/shard_map/while/body/eval_jaxpr/ghqk,gqhd->gkhd/dot_general | solution.py:65
  277.3 5.2 copy.131
  282.6 7.9 %broadcast_in_dim.111 = f32[64,128,512]{2,1,0:T(8,128)} broadcast(f32[]{:T(128)} %constant.56.clone.1), dimensions={} | broadcast | bytes 16777220 | tf_op jit(solution)/shard_map/broadcast_in_dim | solution.py:191
  290.4 9.7 %scatter_fusion.1 = f32[64,128,512]{2,1,0:T(8,128)} fusion(f32[64,128,512]{2,1,0:T(8,128)} %broadcast_in_dim.111, s32[16]{0:T(128)S(1)} %fusion.79, f32[16,128,512]{2,1,0:T(8,128)} %bitcast.110), kind=kCustom, calls=%fused_computation.4 | custom fusion | flops 1048576 | bytes 12582976 | tf_op jit(solution)/shard_map/while/body/eval_jaxpr/scatter-add | solution.py:184
  300.1 9.0 %convert_element_type.122 = bf16[64,128,512]{2,1,0:T(8,128)(2,1)} convert(f32[64,128,512]{2,1,0:T(8,128)} %scatter_fusion.1) | non-fusion elementwise | flops 4194304 | bytes 25165824 | tf_op jit(solution)/shard_map/convert_element_type | solution.py:201
  309.1 5.1 all-to-all-start.2
  315.3 6.0 slice.51
  321.4 5.1 copy.130
  328.9 8.9 %scatter_fusion = f32[16,128,512]{2,1,0:T(8,128)} fusion(f32[16,128,512]{2,1,0:T(8,128)} %broadcast_in_dim.110, s32[12]{0:T(128)S(1)} %fusion.77, f32[12,128,512]{2,1,0:T(8,128)} %bitcast.112), kind=kCustom, calls=%fused_computation.3 | custom fusion | flops 786432 | bytes 9437232 | tf_op jit(solution)/shard_map/while/body/eval_jaxpr/scatter-add | solution.py:181
  342.5 77.6 %all-to-all-done.2 = bf16[32,2,128,512]{3,2,1,0:T(8,128)(2,1)} async-done(((bf16[32,2,128,512]{3,2,1,0:T(8,128)(2,1)}), bf16[32,2,128,512]{3,2,1,0:T(8,128)(2,1)}, u32[]{:S(2)}, u32[]{:S(2)}) %all-to-all-start.2) | async-done | bytes 8388640 | tf_op jit(solution)/shard_map/all_to_all | solution.py:202
  420.1 11.5 %bitcast_convert_fusion = f32[64,128,512]{2,1,0:T(8,128)} fusion(bf16[32,2,128,512]{3,2,1,0:T(8,128)(2,1)} %all-to-all-done.2), kind=kLoop, calls=%fused_computation.15 | loop fusion | flops 4194304 | bytes 25165824 | tf_op jit(solution)/shard_map/convert_element_type | solution.py:212
  431.6 36.2 %scatter_fusion.2 = f32[16,128,512]{2,1,0:T(8,128)} fusion(f32[16,128,512]{2,1,0:T(8,128)} %convert_convert_fusion, s32[64]{0:T(128)S(1)} %fusion.78, f32[64,128,512]{2,1,0:T(8,128)} %bitcast_convert_fusion), kind=kCustom, calls=%fused_computation.5 | custom fusion | flops 4194304 | bytes 50331904 | tf_op jit(solution)/shard_map/scatter-add | solution.py:212
  471.7 33.4 %fusion.50 = bf16[4,128,8,32]{1,3,2,0:T(8,128)(2,1)S(1)} fusion(bf16[4,896,8,32]{1,3,2,0:T(8,128)(2,1)} %bitcast.125, f32[4,8,128,896]{3,2,1,0:T(8,128)} %fusion.63, f32[4,8,128,896]{3,2,1,0:T(8,128)} %get-tuple-element.116, f32[4,8,128]{2,1,0:T(8,128)S(1)} %get-tuple-element.115), kind=kOutput, calls=%fused_computation.58 | convolution fusion | flops 260707200 | bytes 31473664 | tf_op jit(solution)/shard_map/while/body/eval_jaxpr/ghqk,gkhd->gqhd/dot_general | solution.py:62
  516.6 148.8 %all-reduce.3.cloned.1.call-done = (f32[256,256]{0,1:T(8,128)}, f32[256,256]{0,1:T(8,128)}, f32[256,256]{0,1:T(8,128)}, f32[256,256]{0,1:T(8,128)}, f32[256,1024]{1,0:T(8,128)}, /*index=5*/f32[1024,256]{1,0:T(8,128)}) async-done(((f32[256,256]{0,1:T(8,128)}, f32[256,256]{0,1:T(8,128)}, f32[256,256]{0,1:T(8,128)}, f32[256,256]{0,1:T(8,128)}, f32[256,1024]{1,0:T(8,128)}, /*index=5*/f32[1024,256]{1,0:T(8,128)}), ...) | async-done | bytes 3145744 | tf_op jit(solution)/shard_map/psum | solution.py:222
  (171 shorter events, 98.8 us)
Async XLA Ops:
  7.2 194.8 %copy-start = (bf16[1024,256]{1,0:T(8,128)(2,1)S(1)}, bf16[1024,256]{1,0:T(8,128)(2,1)}, u32[]{:S(2)}) copy-start(bf16[1024,256]{1,0:T(8,128)(2,1)} %param.20) | copy-start | bytes 1572868
  7.2 38.2 %all-gather.2.cloned.1.call-start = ((), (), s32[]{:S(2)}) async-start(), calls=%async_computation.4 | async-start | bytes 2621440 | tf_op jit(solution)/shard_map/all_gather | solution.py:137
  14.5 15.7 %all-to-all-start = ((s32[32,1,2]{2,1,0:T(1,128)}), s32[32,1,2]{2,1,0:T(1,128)S(1)}, u32[]{:S(2)}, u32[]{:S(2)}) async-start(s32[32,1,2]{2,1,0:T(1,128)} %bitcast.5), calls=%async_computation | async-start | bytes 32768 | tf_op jit(solution)/shard_map/all_to_all | solution.py:132
  53.7 7.6 %copy-start.5 = (bf16[512,256]{1,0:T(8,128)(2,1)S(1)}, bf16[512,256]{1,0:T(8,128)(2,1)}, u32[]{:S(2)}) copy-start(bf16[512,256]{1,0:T(8,128)(2,1)} %param.14) | copy-start | bytes 786436
  53.7 8.4 %copy-start.28 = (s32[4,4]{1,0:T(4,128)S(1)}, s32[4,4]{1,0:T(4,128)}, u32[]{:S(2)}) copy-start(s32[4,4]{1,0:T(4,128)} %param.25) | copy-start | bytes 196
  53.7 9.7 %copy-start.24 = (bf16[512,256]{1,0:T(8,128)(2,1)S(1)}, bf16[512,256]{1,0:T(8,128)(2,1)}, u32[]{:S(2)}) copy-start(bf16[512,256]{1,0:T(8,128)(2,1)} %param.27) | copy-start | bytes 786436
  53.7 9.8 %copy-start.21 = (bf16[256,256]{1,0:T(8,128)(2,1)S(1)}, bf16[256,256]{1,0:T(8,128)(2,1)}, u32[]{:S(2)}) copy-start(bf16[256,256]{1,0:T(8,128)(2,1)} %param.15) | copy-start | bytes 393220
  53.8 113.4 %all-to-all-start.1 = ((bf16[32,2,128,512]{3,2,1,0:T(8,128)(2,1)}), bf16[32,2,128,512]{3,2,1,0:T(8,128)(2,1)}, u32[]{:S(2)}, u32[]{:S(2)}) async-start(bf16[32,2,128,512]{3,2,1,0:T(8,128)(2,1)} %bitcast.109), calls=%async_computation.1 | async-start | bytes 16777216 | tf_op jit(solution)/shard_map/all_to_all | solution.py:140
  64.0 116.3 %copy-start.25 = (bf16[4,128,8,32]{1,0,3,2:T(4,128)(2,1)}, bf16[4,128,8,32]{1,0,3,2:T(4,128)(2,1)S(1)}, u32[]{:S(2)}) copy-start(bf16[4,128,8,32]{1,0,3,2:T(4,128)(2,1)S(1)} %reshape.392) | copy-start | bytes 786436
  64.0 8.2 %copy-start.31 = (s32[16]{0:T(128)S(1)}, s32[16]{0:T(128)}, u32[]{:S(2)}) copy-start(s32[16]{0:T(128)} %reshape.421) | copy-start | bytes 196
  64.0 8.2 %copy-start.33 = (s32[16,1]{0,1:T(1,128)S(1)}, s32[16,1]{0,1:T(1,128)}, u32[]{:S(2)}) copy-start(s32[16,1]{0,1:T(1,128)} %reshape.399) | copy-start | bytes 196
  64.1 8.3 %copy-start.27 = (s32[1024]{0:T(1024)S(1)}, s32[1024]{0:T(1024)}, u32[]{:S(2)}) copy-start(s32[1024]{0:T(1024)} %get-tuple-element.124) | copy-start | bytes 12292
  180.4 12.4 %copy-start.4 = (bf16[4,896,256]{1,2,0:T(8,128)(2,1)S(1)}, bf16[4,896,256]{1,2,0:T(8,128)(2,1)}, u32[]{:S(2)}) copy-start(bf16[4,896,256]{1,2,0:T(8,128)(2,1)} %copy.115) | copy-start | bytes 5505028
  192.8 8.2 %copy-start.18 = (bf16[512,256]{0,1:T(8,128)(2,1)S(1)}, bf16[512,256]{0,1:T(8,128)(2,1)}, u32[]{:S(2)}) copy-start(bf16[512,256]{0,1:T(8,128)(2,1)} %copy.107) | copy-start | bytes 786436
  192.8 8.2 %copy-start.19 = (bf16[256,256]{1,0:T(8,128)(2,1)S(1)}, bf16[256,256]{1,0:T(8,128)(2,1)}, u32[]{:S(2)}) copy-start(bf16[256,256]{1,0:T(8,128)(2,1)} %param.18) | copy-start | bytes 393220
  192.8 8.6 %copy-start.32 = (f32[256]{0:T(256)S(1)}, f32[256]{0:T(256)}, u32[]{:S(2)}) copy-start(f32[256]{0:T(256)} %param.21) | copy-start | bytes 3076
  192.8 8.7 %copy-start.20 = (bf16[256,1024]{1,0:T(8,128)(2,1)S(1)}, bf16[256,1024]{1,0:T(8,128)(2,1)}, u32[]{:S(2)}) copy-start(bf16[256,1024]{1,0:T(8,128)(2,1)} %param.19) | copy-start | bytes 1572868
  309.1 111.0 %all-to-all-start.2 = ((bf16[32,2,128,512]{3,2,1,0:T(8,128)(2,1)}), bf16[32,2,128,512]{3,2,1,0:T(8,128)(2,1)}, u32[]{:S(2)}, u32[]{:S(2)}) async-start(bf16[32,2,128,512]{3,2,1,0:T(8,128)(2,1)} %bitcast.108), calls=%async_computation.2 | async-start | bytes 16777216 | tf_op jit(solution)/shard_map/all_to_all | solution.py:202
  314.2 197.7 %reduce-scatter.2.cloned.1.call-start = ((), (), s32[]{:S(2)}) async-start(), calls=%async_computation.5 | async-start | bytes 2621440 | tf_op jit(solution)/shard_map/reduce_scatter | solution.py:214
  471.6 33.8 %copy-start.6 = (bf16[512,256]{1,0:T(8,128)(2,1)S(1)}, bf16[512,256]{1,0:T(8,128)(2,1)}, u32[]{:S(2)}) copy-start(bf16[512,256]{1,0:T(8,128)(2,1)} %param.14) | copy-start | bytes 786436
  471.6 193.8 %all-reduce.3.cloned.1.call-start = ((), (), s32[]{:S(2)}) async-start(), calls=%async_computation.6 | async-start | bytes 6291456 | tf_op jit(solution)/shard_map/psum | solution.py:222
  665.4 7.5 %copy-start.17 = (f32[256,1024]{1,0:T(8,128)S(1)}, f32[256,1024]{1,0:T(8,128)}, u32[]{:S(2)}) copy-start(f32[256,1024]{1,0:T(8,128)} %get-tuple-element.103) | copy-start | bytes 3145732
  665.4 8.5 %copy-start.16 = (f32[1024,256]{1,0:T(8,128)S(1)}, f32[1024,256]{1,0:T(8,128)}, u32[]{:S(2)}) copy-start(f32[1024,256]{1,0:T(8,128)} %get-tuple-element.104) | copy-start | bytes 3145732
  667.4 7.6 %copy-start.1 = (bf16[1024,256]{1,0:T(8,128)(2,1)S(1)}, bf16[1024,256]{1,0:T(8,128)(2,1)}, u32[]{:S(2)}) copy-start(bf16[1024,256]{1,0:T(8,128)(2,1)} %param.20) | copy-start | bytes 1572868
  (16 other events, 52.2 us)
Sparse Core Ops, SparseCore 0:
  12.1 33.2 all-gather.1
  471.7 25.1 reduce-scatter.1
  514.4 150.9 all-reduce.2
where the time goes:
time: 691 us; the launch traced here: 682 us
  waiting for transfers between devices  340 us (49%)
  matrix products  118 us (17%)
  other arithmetic  98.6 us (14%)
  local copies, waits for them, and re-layouts  89.7 us (13%)
  starting transfers between devices  21.2 us (3%)
  between operations  14.6 us (2%)
    psum x1, waiting for transfers between devices, on_device(): lax.psum((query_sum, pair_sum[:, :width], pair_sum[:, width:], out_sum, e...  149 us
    all_to_all x1, waiting for transfers between devices, on_device(): lax.all_to_all(part_pairs[wanted], 'dom', split_axis=0, concat_axis=0, ti...  93 us
    all_to_all x1, waiting for transfers between devices, on_device(): lax.all_to_all(far_low.reshape(dom_count, capacity, block_len, pair_width...  77.6 us
    scatter-add x1, other arithmetic, on_device(): combined = near_low.astype(jnp.float32).at[wanted_flat].add(returned.resh...  36.2 us
    dot_general x1, matrix products, attend_back(): jnp.einsum('ghqk,gkhd->gqhd', d_scores, key_heads, preferred_element_type...  33.4 us
    dot_general x1, matrix products, attend_back(): jnp.einsum('ghqk,gqhd->gkhd', d_scores, query_heads, preferred_element_ty...  33 us
    unnamed x79, local copies, waits for them, and re-layouts  15.2 us
    all_gather x1, waiting for transfers between devices, on_device(): lax.all_gather(own_pairs, 'node', axis=0, tiled=True)  14.3 us
  transfers between devices with their start and end apart: 6, of which 5 were waited for; matrix products, arithmetic and copies ran while one was open for 13% of the time, Pallas kernels for 0%

commit v1 on v0

v1 whole, which is shorter than its diff:
```python
import functools
import math

import jax
import jax.numpy as jnp
from jax import lax
from jax.experimental import pallas as pl
from jax.experimental.pallas import tpu as pltpu
from jax.sharding import PartitionSpec as P

HEADS = 8
EPSILON = 1e-05
MESH = pl.DeviceIdType.MESH
F32 = jnp.float32
BF16 = jnp.bfloat16
NEG = -1e30
VMEM_LIMIT = 56 << 20

D = 256
BLK = 128
TILES = 7
NEAR = 3
ROWS = 4
PART = 16
KEYS = TILES * BLK
N_DOM = 32
N_NODE = 4

_GROUPS = [
    [(2, 2)],
    [(2, 1), (2, 3)],
    [(1, 2), (3, 2)],
    [(1, 1), (3, 3)],
    [(1, 3), (3, 1)],
    [(2, 0), (0, 2)],
    [(1, 0), (3, 0), (0, 1), (0, 3)],
]
OFFSETS = [(a, b, c) for group in _GROUPS for c in range(2) for a, b in group] + [(0, 0, 1)]


def dom_peer(dom, offset, sign=1):
    core = lax.rem(dom, 2)
    y = lax.rem(dom // 2, 4)
    z = dom // 8
    dz, dy, dc = offset
    return (
        lax.rem(z + (dz if sign > 0 else 4 - dz), 4) * 8
        + lax.rem(y + (dy if sign > 0 else 4 - dy), 4) * 2
        + lax.rem(core + dc, 2)
    )


def nt(a, b):
    return lax.dot_general(a, b, (((1,), (1,)), ((), ())), preferred_element_type=F32)


def tn(a, b):
    return lax.dot_general(a, b, (((0,), (0,)), ((), ())), preferred_element_type=F32)


def nn(a, b):
    return jnp.dot(a, b, preferred_element_type=F32)


def exchange_kernel(
    feat_ref, ids_ref, mask_ref, part_ref, far_ref, wanted_ref, bias_ref,
    send_buf, own_buf, ids_smem, near_send, near_recv, id_send, id_recv, far_send, far_recv, local_sem,
):
    dom = lax.axis_index("dom")
    node = lax.axis_index("node")
    barrier = pltpu.get_barrier_semaphore()
    for offset in OFFSETS:
        pl.semaphore_signal(barrier, inc=1, device_id=(dom_peer(dom, offset), node), device_id_type=MESH)
    for step in range(1, N_NODE):
        pl.semaphore_signal(
            barrier, inc=1, device_id=(dom, lax.rem(node + step, N_NODE)), device_id_type=MESH
        )
    pl.semaphore_wait(barrier, len(OFFSETS) + N_NODE - 1)

    near_copies = []
    for step in range(1, N_NODE):
        copy = pltpu.make_async_remote_copy(
            src_ref=feat_ref, dst_ref=part_ref.at[pl.ds(node * ROWS, ROWS)],
            send_sem=near_send.at[step - 1], recv_sem=near_recv.at[step - 1],
            device_id=(dom, lax.rem(node + step, N_NODE)), device_id_type=MESH,
        )
        copy.start()
        near_copies.append(copy)
    id_copies = []
    for index, offset in enumerate(OFFSETS):
        peer = dom_peer(dom, offset)
        copy = pltpu.make_async_remote_copy(
            src_ref=ids_ref.at[peer], dst_ref=wanted_ref.at[dom],
            send_sem=id_send.at[index], recv_sem=id_recv.at[index],
            device_id=(peer, node), device_id_type=MESH,
        )
        copy.start()
        id_copies.append(copy)
    part_ref[pl.ds(node * ROWS, ROWS)] = feat_ref[...]
    wanted_ref[dom] = ids_ref[dom]
    for copy in id_copies:
        copy.wait()
    to_smem = pltpu.make_async_copy(wanted_ref, ids_smem, local_sem.at[0])
    to_smem.start()
    to_smem.wait()
    for copy in near_copies:
        copy.wait()

    far_copies = []
    for index, offset in enumerate(OFFSETS):
        peer = dom_peer(dom, offset)
        for slot in range(2):
            send_buf[index, slot] = part_ref[ids_smem[peer, 0, slot]]
        copy = pltpu.make_async_remote_copy(
            src_ref=send_buf.at[index], dst_ref=far_ref.at[dom],
            send_sem=far_send.at[index], recv_sem=far_recv.at[index],
            device_id=(peer, node), device_id_type=MESH,
        )
        copy.start()
        far_copies.append(copy)
    for slot in range(2):
        own_buf[slot] = part_ref[ids_smem[dom, 0, slot]]
    own_copy = pltpu.make_async_copy(own_buf, far_ref.at[dom], local_sem.at[1])
    own_copy.start()

    def to_bias(row, carry):
        start = pl.multiple_of(row * BLK, BLK)
        diagonal = lax.broadcasted_iota(jnp.int32, (BLK, BLK), 0) == lax.broadcasted_iota(
            jnp.int32, (BLK, BLK), 1
        )
        for tile in range(TILES):
            allowed = mask_ref[pl.ds(start, BLK), tile, :] > 0
            if tile == 0:
                allowed = jnp.logical_or(allowed, diagonal)
            bias_ref[pl.ds(start, BLK), tile * BLK : (tile + 1) * BLK] = jnp.where(
                allowed, 0.0, NEG
            ).astype(BF16)
        return carry

    lax.fori_loop(0, ROWS, to_bias, 0)
    own_copy.wait()
    for copy in far_copies:
        copy.wait()


def layer_kernel(
    local_ref, slot_ref, feat_ref, part_ref, far_ref, bias_ref, d_out_ref,
    wq_ref, wk_ref, wv_ref, wo_ref, we_ref, wr_ref, gain_a_ref, gain_f_ref, hm_ref,
    out_ref, back_ref, near_ref, rows_ref, grads_ref,
    fs, ks, vs, qs, ps, mixed, d_mixed, resid_grad, pair_acc, query_acc, expand_acc, reduce_acc, out_acc, sems,
):
    node = lax.axis_index("node")
    scale = 1.0 / math.sqrt(D // HEADS)
    log2e = math.log2(math.e)
    copies = []
    for row in range(ROWS):
        for tile in range(TILES - NEAR):
            copy = pltpu.make_async_copy(
                far_ref.at[slot_ref[row, tile]],
                fs.at[row, pl.ds((NEAR + tile) * BLK, BLK)],
                sems.at[row * (TILES - NEAR) + tile],
            )
            copy.start()
            copies.append(copy)
    for row in range(ROWS):
        fs[row, 0:BLK] = feat_ref[row * BLK : (row + 1) * BLK]
        for tile in range(NEAR - 1):
            fs[row, (tile + 1) * BLK : (tile + 2) * BLK] = part_ref[local_ref[row, tile]]
    back_ref[...] = jnp.zeros(back_ref.shape, BF16)
    near_ref[...] = jnp.zeros(near_ref.shape, F32)
    pair_acc[...] = jnp.zeros(pair_acc.shape, F32)
    query_acc[...] = jnp.zeros(query_acc.shape, F32)
    expand_acc[...] = jnp.zeros(expand_acc.shape, F32)
    reduce_acc[...] = jnp.zeros(reduce_acc.shape, F32)
    out_acc[...] = jnp.zeros(out_acc.shape, F32)
    qs[...] = nn(feat_ref[...], wq_ref[...]).astype(BF16)
    for copy in copies:
        copy.wait()

    head_low = [hm_ref[h : h + 1, :].astype(BF16) for h in range(HEADS)]
    head_f32 = [hm_ref[h : h + 1, :] for h in range(HEADS)]

    def forward(row, carry):
        start = pl.multiple_of(row * BLK, BLK)
        tile_rows = fs[row]
        keys = nn(tile_rows, wk_ref[...]).astype(BF16)
        ks[row] = keys
        values = nn(tile_rows, wv_ref[...]).astype(BF16)
        vs[row] = values
        query = qs[pl.ds(start, BLK), :]
        bias = bias_ref[pl.ds(start, BLK), :].astype(F32)
        total = jnp.zeros((BLK, D), F32)
        for pair in range(HEADS // 2):
            both = jnp.concatenate([query * head_low[2 * pair], query * head_low[2 * pair + 1]], 0)
            scores = nt(both, keys) * (scale * log2e)
            for half in range(2):
                mine = scores[half * BLK : (half + 1) * BLK] + bias
                top = jnp.max(mine, -1, keepdims=True)
                weight = jnp.exp2(mine - top)
                norm = 1.0 / jnp.sum(weight, -1, keepdims=True)
                ps[row, (2 * pair + half) * BLK : (2 * pair + half + 1) * BLK, :] = (weight * norm).astype(BF16)
            got = nn(ps[row, 2 * pair * BLK : (2 * pair + 2) * BLK, :], values)
            total = total + got[:BLK] * head_f32[2 * pair] + got[BLK:] * head_f32[2 * pair + 1]
        mixed[pl.ds(start, BLK), :] = total
        return carry

    lax.fori_loop(0, ROWS, forward, 0)

    chunk = 256

    def feed(step, carry):
        start = pl.multiple_of(step * chunk, chunk)
        sel = pl.ds(start, chunk)
        mixed_low = mixed[sel, :].astype(BF16)
        gain_a = gain_a_ref[...]
        gain_f = gain_f_ref[...]
        residual = feat_ref[sel, :].astype(F32) + nn(mixed_low, wo_ref[...])
        center = residual - jnp.mean(residual, -1, keepdims=True)
        rstd_a = lax.rsqrt(jnp.mean(center * center, -1, keepdims=True) + EPSILON)
        hat_a = center * rstd_a
        first_low = (hat_a * gain_a).astype(BF16)
        pre = nn(first_low, we_ref[...])
        root = math.sqrt(2.0 / math.pi)
        square = pre * pre
        tanh = jnp.tanh(root * (pre + 0.044715 * (square * pre)))
        half = 0.5 * (1.0 + tanh)
        act_low = (pre * half).astype(BF16)
        slope = half + 0.5 * pre * (1.0 - tanh * tanh) * (root * (1.0 + 3.0 * 0.044715 * square))
        second = first_low.astype(F32) + nn(act_low, wr_ref[...])
        center = second - jnp.mean(second, -1, keepdims=True)
        rstd_f = lax.rsqrt(jnp.mean(center * center, -1, keepdims=True) + EPSILON)
        hat_f = center * rstd_f
        out_ref[sel, :] = (hat_f * gain_f).astype(BF16)
        d_hat = d_out_ref[sel, :].astype(F32) * gain_f
        d_second = rstd_f * (
            d_hat - jnp.mean(d_hat, -1, keepdims=True) - hat_f * jnp.mean(d_hat * hat_f, -1, keepdims=True)
        )
        d_second_low = d_second.astype(BF16)
        reduce_acc[...] += tn(d_second_low, act_low)
        d_pre_low = (nt(d_second_low, wr_ref[...]) * slope).astype(BF16)
        expand_acc[...] += tn(first_low, d_pre_low)
        d_first = d_second + nt(d_pre_low, we_ref[...])
        d_hat = d_first * gain_a
        d_resid = rstd_a * (
            d_hat - jnp.mean(d_hat, -1, keepdims=True) - hat_a * jnp.mean(d_hat * hat_a, -1, keepdims=True)
        )
        resid_grad[sel, :] = d_resid
        d_resid_low = d_resid.astype(BF16)
        out_acc[...] += tn(mixed_low, d_resid_low)
        d_mixed[sel, :] = nt(d_resid_low, wo_ref[...]).astype(BF16)
        return carry

    lax.fori_loop(0, ROWS * BLK // chunk, feed, 0)

    first_half = lax.broadcasted_iota(jnp.int32, (64, BLK), 0) < 32

    def block_diagonal(turned, pair):
        piece = turned[64 * pair : 64 * pair + 64]
        return jnp.concatenate(
            [jnp.where(first_half, piece, 0.0), jnp.where(first_half, 0.0, piece)], 1
        ).astype(BF16)

    def backward(row, carry):
        start = pl.multiple_of(row * BLK, BLK)
        keys = ks[row]
        values = vs[row]
        query = qs[pl.ds(start, BLK), :]
        grad = d_mixed[pl.ds(start, BLK), :]
        query_t = query.astype(F32).T
        grad_t = grad.astype(F32).T
        inner_full = grad.astype(F32) * mixed[pl.ds(start, BLK), :]
        d_query = jnp.zeros((BLK, D), F32)
        key_parts = []
        value_parts = []
        for pair in range(HEADS // 2):
            both = jnp.concatenate([grad * head_low[2 * pair], grad * head_low[2 * pair + 1]], 0)
            inner = jnp.concatenate(
                [
                    jnp.sum(inner_full * head_f32[2 * pair], -1, keepdims=True),
                    jnp.sum(inner_full * head_f32[2 * pair + 1], -1, keepdims=True),
                ],
                0,
            )
            probs_low = ps[row, 2 * pair * BLK : (2 * pair + 2) * BLK, :]
            d_probs = nt(both, values)
            d_scores = (probs_low.astype(F32) * ((d_probs - inner) * scale)).astype(BF16)
            got = nn(d_scores, keys)
            d_query = d_query + got[:BLK] * head_f32[2 * pair] + got[BLK:] * head_f32[2 * pair + 1]
            key_parts.append(nn(block_diagonal(query_t, pair), d_scores).astype(BF16))
            value_parts.append(nn(block_diagonal(grad_t, pair), probs_low).astype(BF16))
        d_keys_t = jnp.concatenate(key_parts, 0)
        d_values_t = jnp.concatenate(value_parts, 0)
        tile_rows = fs[row]
        pair_acc[0:D, :] += nn(d_keys_t, tile_rows)
        pair_acc[D : 2 * D, :] += nn(d_values_t, tile_rows)
        d_rows_t = nn(wk_ref[...], d_keys_t) + nn(wv_ref[...], d_values_t)
        near_ids = [node * ROWS + row, local_ref[row, 0], local_ref[row, 1]]
        for tile in range(TILES):
            piece = d_rows_t[:, tile * BLK : (tile + 1) * BLK].T
            if tile < NEAR:
                near_ref[near_ids[tile]] += piece
            else:
                back_ref[slot_ref[row, tile - NEAR]] = piece.astype(BF16)
        d_query_low = d_query.astype(BF16)
        query_acc[...] += tn(tile_rows[:BLK], d_query_low)
        rows_ref[pl.ds(start, BLK), :] = resid_grad[pl.ds(start, BLK), :] + nt(d_query_low, wq_ref[...])
        return carry

    lax.fori_loop(0, ROWS, backward, 0)

    place = 0
    for acc in (query_acc, pair_acc, out_acc, expand_acc, reduce_acc):
        for top in range(0, acc.shape[0], D):
            for left in range(0, acc.shape[1], BLK):
                grads_ref[place : place + D, :] = acc[top : top + D, left : left + BLK].astype(BF16)
                place += D


LINE = 8
PLANE = 16
LINE_ROWS = 6144 // LINE
PLANE_ROWS = LINE_ROWS // PLANE


def return_kernel(
    wanted_ref, back_ref, near_ref, grads_ref,
    own_ref, cross_ref, sum_ref,
    recv, acc, cross_send, line_recv, line_sum, plane_recv, plane_sum, plane_all,
    far_send, far_recv, x_send, x_recv, ls_send, ls_recv, ps_send, ps_recv, pg_send, pg_recv, lg_send, lg_recv,
    local_sem,
):
    dom = lax.axis_index("dom")
    node = lax.axis_index("node")
    core = lax.rem(dom, 2)
    member = node * 2 + core
    spot = dom // 2

    def line_peer(step):
        other = lax.rem(member + step, LINE)
        return other, (dom - core + lax.rem(other, 2), other // 2)

    def plane_peer(step):
        other = lax.rem(spot + step, PLANE)
        return other, (other * 2 + core, node)

    barrier = pltpu.get_barrier_semaphore()
    for offset in OFFSETS:
        pl.semaphore_signal(barrier, inc=1, device_id=(dom_peer(dom, offset), node), device_id_type=MESH)
    for step in range(1, N_NODE):
        for flip in range(2):
            pl.semaphore_signal(
                barrier, inc=1,
                device_id=(dom - core + lax.rem(core + flip, 2), lax.rem(node + step, N_NODE)),
                device_id_type=MESH,
            )
    pl.semaphore_wait(barrier, len(OFFSETS) + 2 * (N_NODE - 1))

    line_copies = []
    for step in range(1, LINE):
        other, device = line_peer(step)
        copy = pltpu.make_async_remote_copy(
            src_ref=grads_ref.at[pl.ds(pl.multiple_of(other * LINE_ROWS, LINE_ROWS), LINE_ROWS)],
            dst_ref=line_recv.at[step - 1],
            send_sem=ls_send.at[step - 1], recv_sem=ls_recv.at[step - 1],
            device_id=device, device_id_type=MESH,
        )
        copy.start()
        line_copies.append(copy)
    far_copies = []
    for index, offset in enumerate(OFFSETS):
        peer = dom_peer(dom, offset)
        copy = pltpu.make_async_remote_copy(
            src_ref=back_ref.at[peer], dst_ref=recv.at[index],
            send_sem=far_send.at[index], recv_sem=far_recv.at[index],
            device_id=(peer, node), device_id_type=MESH,
        )
        copy.start()
        far_copies.append(copy)
    own_copy = pltpu.make_async_copy(back_ref.at[dom], recv.at[N_DOM - 1], local_sem)
    own_copy.start()
    acc[...] = near_ref[...]

    def combine(index, source):
        first = wanted_ref[source, 0, 0]
        second = wanted_ref[source, 0, 1]

        def add(block, carry):
            take_first = (first == block).astype(F32)
            take_second = (second == block).astype(F32)
            acc[block] += recv[index, 0].astype(F32) * take_first + recv[index, 1].astype(F32) * take_second
            return carry

        lax.fori_loop(0, PART, add, 0)

    own_copy.wait()
    combine(N_DOM - 1, dom)
    for copy in line_copies:
        copy.wait()
    mine = pl.ds(pl.multiple_of(member * LINE_ROWS, LINE_ROWS), LINE_ROWS)
    total = grads_ref[mine, :].astype(F32)
    for step in range(1, LINE):
        total = total + line_recv[step - 1].astype(F32)
    line_sum[...] = total.astype(BF16)
    plane_copies = []
    for step in range(1, PLANE):
        other, device = plane_peer(step)
        copy = pltpu.make_async_remote_copy(
            src_ref=line_sum.at[pl.ds(pl.multiple_of(other * PLANE_ROWS, PLANE_ROWS), PLANE_ROWS)],
            dst_ref=plane_recv.at[step - 1],
            send_sem=ps_send.at[step - 1], recv_sem=ps_recv.at[step - 1],
            device_id=device, device_id_type=MESH,
        )
        copy.start()
        plane_copies.append(copy)

    def take(begin, end):
        for index in range(begin, end):
            far_copies[index].wait()
            combine(index, dom_peer(dom, OFFSETS[index], -1))

    take(0, 8)
    for copy in plane_copies:
        copy.wait()
    spot_rows = pl.ds(pl.multiple_of(spot * PLANE_ROWS, PLANE_ROWS), PLANE_ROWS)
    total = line_sum[spot_rows, :].astype(F32)
    for step in range(1, PLANE):
        total = total + plane_recv[step - 1].astype(F32)
    plane_sum[...] = total.astype(BF16)
    gather_copies = []
    for step in range(1, PLANE):
        other, device = plane_peer(step)
        copy = pltpu.make_async_remote_copy(
            src_ref=plane_sum, dst_ref=plane_all.at[spot_rows],
            send_sem=pg_send.at[step - 1], recv_sem=pg_recv.at[step - 1],
            device_id=device, device_id_type=MESH,
        )
        copy.start()
        gather_copies.append(copy)
    plane_all[spot_rows, :] = plane_sum[...]
    take(8, 16)
    for copy in gather_copies:
        copy.wait()
    spread_copies = []
    for step in range(1, LINE):
        other, device = line_peer(step)
        copy = pltpu.make_async_remote_copy(
            src_ref=plane_all, dst_ref=sum_ref.at[mine],
            send_sem=lg_send.at[step - 1], recv_sem=lg_recv.at[step - 1],
            device_id=device, device_id_type=MESH,
        )
        copy.start()
        spread_copies.append(copy)
    sum_ref[mine, :] = plane_all[...]
    take(16, len(OFFSETS))

    cross_send[...] = acc[...].astype(BF16)
    cross_copies = []
    for step in range(1, N_NODE):
        other = lax.rem(node + step, N_NODE)
        copy = pltpu.make_async_remote_copy(
            src_ref=cross_send.at[pl.ds(other * ROWS, ROWS)], dst_ref=cross_ref.at[step - 1],
            send_sem=x_send.at[step - 1], recv_sem=x_recv.at[step - 1],
            device_id=(dom, other), device_id_type=MESH,
        )
        copy.start()
        cross_copies.append(copy)
    own_ref[...] = acc[pl.ds(node * ROWS, ROWS)]
    for copy in spread_copies:
        copy.wait()
    for copy in cross_copies:
        copy.wait()


def finish_kernel(factor, rows_ref, own_ref, cross_ref, sum_ref, dx_ref, gq, gk, gv, go, ge, gr):
    for row in range(ROWS):
        total = rows_ref[row * BLK : (row + 1) * BLK, :] + own_ref[row]
        for step in range(N_NODE - 1):
            total = total + cross_ref[step, row].astype(F32)
        dx_ref[row * BLK : (row + 1) * BLK, :] = total.astype(BF16)

    def piece(index):
        return sum_ref[index * D : (index + 1) * D, :].astype(F32) * factor

    for half in range(2):
        span = slice(half * BLK, (half + 1) * BLK)
        gq[:, span] = piece(half)
        gk[span, :] = piece(2 + half).T
        gv[span, :] = piece(4 + half).T
        go[:, span] = piece(6 + half)
    for part in range(8):
        span = slice(part * BLK, (part + 1) * BLK)
        ge[:, span] = piece(8 + part)
        gr[span, :] = piece(16 + part).T


def vmem(shape, dtype):
    return pltpu.VMEM(shape, dtype)


IN_VMEM = pl.BlockSpec(memory_space=pltpu.VMEM)
IN_SMEM = pl.BlockSpec(memory_space=pltpu.SMEM)
ANYWHERE = pl.BlockSpec(memory_space=pl.ANY)


def on_device(
    features, w_query, w_key, w_value, w_out, w_expand, w_reduce, gain_attn, gain_ffn,
    tile_mask, local_block, remote_slot, remote_block, d_out,
):
    rows = features.shape[0]
    dma = pltpu.SemaphoreType.DMA
    peers = len(OFFSETS)
    ids = jnp.pad(remote_block.reshape(N_DOM, 1, 2), ((0, 0), (0, 0), (0, BLK - 2)))
    part, far, wanted, bias = pl.pallas_call(
        exchange_kernel,
        out_shape=(
            jax.ShapeDtypeStruct((PART, BLK, D), BF16),
            jax.ShapeDtypeStruct((N_DOM, 2, BLK, D), BF16),
            jax.ShapeDtypeStruct((N_DOM, 1, BLK), jnp.int32),
            jax.ShapeDtypeStruct((rows, KEYS), BF16),
        ),
        in_specs=[IN_VMEM] * 3,
        out_specs=(IN_VMEM, ANYWHERE, IN_VMEM, IN_VMEM),
        scratch_shapes=[
            vmem((peers, 2, BLK, D), BF16), vmem((2, BLK, D), BF16), pltpu.SMEM((N_DOM, 1, BLK), jnp.int32),
            dma((N_NODE - 1,)), dma((N_NODE - 1,)), dma((peers,)), dma((peers,)), dma((peers,)), dma((peers,)),
            dma((2,)),
        ],
        compiler_params=pltpu.CompilerParams(
            collective_id=1, has_side_effects=True, vmem_limit_bytes=VMEM_LIMIT
        ),
        name="exchange",
    )(features.reshape(ROWS, BLK, D), ids, tile_mask)

    lanes = jnp.arange(D)[None, :] // (D // HEADS) == jnp.arange(HEADS)[:, None]
    output, back, near, d_rows, grads = pl.pallas_call(
        layer_kernel,
        out_shape=(
            jax.ShapeDtypeStruct((rows, D), BF16),
            jax.ShapeDtypeStruct((2 * N_DOM, BLK, D), BF16),
            jax.ShapeDtypeStruct((PART, BLK, D), F32),
            jax.ShapeDtypeStruct((rows, D), F32),
            jax.ShapeDtypeStruct((6144, BLK), BF16),
        ),
        in_specs=[IN_SMEM, IN_SMEM, IN_VMEM, IN_VMEM, ANYWHERE] + [IN_VMEM] * 11,
        out_specs=(IN_VMEM,) * 5,
        scratch_shapes=[
            vmem((ROWS, KEYS, D), BF16), vmem((ROWS, KEYS, D), BF16), vmem((ROWS, KEYS, D), BF16),
            vmem((rows, D), BF16), vmem((ROWS, HEADS * BLK, KEYS), BF16), vmem((rows, D), F32),
            vmem((rows, D), BF16), vmem((rows, D), F32), vmem((2 * D, D), F32), vmem((D, D), F32),
            vmem((D, 4 * D), F32), vmem((D, 4 * D), F32), vmem((D, D), F32), dma((16,)),
        ],
        compiler_params=pltpu.CompilerParams(vmem_limit_bytes=VMEM_LIMIT),
        name="layer",
    )(
        local_block, remote_slot, features, part, far.reshape(2 * N_DOM, BLK, D), bias, d_out,
        w_query, w_key, w_value, w_out, w_expand, w_reduce, gain_attn.reshape(1, D), gain_ffn.reshape(1, D),
        lanes.astype(F32),
    )

    own, cross, summed = pl.pallas_call(
        return_kernel,
        out_shape=(
            jax.ShapeDtypeStruct((ROWS, BLK, D), F32),
            jax.ShapeDtypeStruct((N_NODE - 1, ROWS, BLK, D), BF16),
            jax.ShapeDtypeStruct((6144, BLK), BF16),
        ),
        in_specs=[IN_SMEM, ANYWHERE, IN_VMEM, IN_VMEM],
        out_specs=(IN_VMEM,) * 3,
        scratch_shapes=[
            vmem((N_DOM, 2, BLK, D), BF16), vmem((PART, BLK, D), F32), vmem((PART, BLK, D), BF16),
            vmem((LINE - 1, LINE_ROWS, BLK), BF16), vmem((LINE_ROWS, BLK), BF16),
            vmem((PLANE - 1, PLANE_ROWS, BLK), BF16), vmem((PLANE_ROWS, BLK), BF16), vmem((LINE_ROWS, BLK), BF16),
            dma((peers,)), dma((peers,)), dma((N_NODE - 1,)), dma((N_NODE - 1,)),
            dma((LINE - 1,)), dma((LINE - 1,)), dma((PLANE - 1,)), dma((PLANE - 1,)),
            dma((PLANE - 1,)), dma((PLANE - 1,)), dma((LINE - 1,)), dma((LINE - 1,)), dma,
        ],
        compiler_params=pltpu.CompilerParams(
            collective_id=2, has_side_effects=True, vmem_limit_bytes=VMEM_LIMIT
        ),
        name="give_back",
    )(wanted, back.reshape(N_DOM, 2, BLK, D), near, grads)

    factor = 1.0 / math.sqrt(rows * N_DOM * N_NODE)
    finished = pl.pallas_call(
        functools.partial(finish_kernel, factor),
        out_shape=(
            jax.ShapeDtypeStruct((rows, D), BF16),
            jax.ShapeDtypeStruct((D, D), F32),
            jax.ShapeDtypeStruct((D, D), F32),
            jax.ShapeDtypeStruct((D, D), F32),
            jax.ShapeDtypeStruct((D, D), F32),
            jax.ShapeDtypeStruct((D, 4 * D), F32),
            jax.ShapeDtypeStruct((4 * D, D), F32),
        ),
        in_specs=[IN_VMEM] * 4,
        out_specs=(IN_VMEM,) * 7,
        compiler_params=pltpu.CompilerParams(vmem_limit_bytes=VMEM_LIMIT),
        name="finish",
    )(d_rows, own, cross, summed)
    return (output,) + tuple(finished)


def solution(mesh):
    split = P(("dom", "node"), None)
    placed = (
        (split,) + (P(),) * 8 + (P(("dom", "node"), None, None), split, split, P("dom", "node", None), split)
    )
    return jax.shard_map(
        on_device, mesh=mesh, in_specs=placed, out_specs=(split, split) + (P(),) * 6, check_vma=False
    )
```

time: 691 us -> 231 us (0.33); the launches traced: 682 us -> 230 us
  waiting for transfers between devices: 340 us -> 0 us
  Pallas kernels: 0 us -> 221 us
  matrix products: 118 us -> 0 us
  other arithmetic: 98.6 us -> 1.92 us
  local copies, waits for them, and re-layouts: 89.7 us -> 6.49 us
  starting transfers between devices: 21.2 us -> 0 us
  between operations: 14.6 us -> 0.67 us
    pallas_call x0 -> x4, Pallas kernels: none -> 221 us  [the longest x1 106 us: on_device(): pl.pallas_call(return_kernel, out_shape=(jax.ShapeDtypeStruct((ROWS, BLK,...]
    all_to_all x3 -> x0, waiting for transfers between devices: 177 us -> none  [the longest x1 93 us: on_device(): lax.all_to_all(part_pairs[wanted], 'dom', split_axis=0, concat_axis=0, ti...]
    psum x1 -> x0, waiting for transfers between devices: 149 us -> none  [on_device(): lax.psum((query_sum, pair_sum[:, :width], pair_sum[:, width:], out_sum, e...]
    dot_general x20 -> x0, matrix products: 105 us -> none  [the longest x1 33.4 us: attend_back(): jnp.einsum('ghqk,gkhd->gqhd', d_scores, key_heads, preferred_element_type...]
    scatter-add x3 -> x0, other arithmetic: 54.8 us -> none  [the longest x1 36.2 us: on_device(): combined = near_low.astype(jnp.float32).at[wanted_flat].add(returned.resh...]
    slice x9 -> x0, local copies, waits for them, and re-layouts: 29.3 us -> none  [the longest x2 11.1 us: backward_group(): d_pairs[:, :near_tiles].reshape(-1, block_len, pair_width)]
    convert_element_type x6 -> x1, other arithmetic: 29.1 us -> 0.6 us  [on_device(): lanes.astype(F32)]
    all_to_all x3 -> x0, starting transfers between devices: 21.1 us -> none  [the longest x1 8.42 us: on_device(): lax.all_to_all(remote_block.reshape(dom_count, capacity), 'dom', split_ax...]
  transfers between devices with their start and end apart: 6 -> 0, of which waited for: 5 -> 0; matrix products, arithmetic and copies ran while one was open for 13% -> 0% of each run, Pallas kernels for 0% -> 0%
where the time goes in v1:
time: 231 us; the launch traced here: 230 us
  Pallas kernels  221 us (96%)
  local copies, waits for them, and re-layouts  6.49 us (3%)
    pallas_call x1, Pallas kernels, on_device(): pl.pallas_call(return_kernel, out_shape=(jax.ShapeDtypeStruct((ROWS, BLK,...  106 us
    pallas_call x1, Pallas kernels, on_device(): pl.pallas_call(exchange_kernel, out_shape=(jax.ShapeDtypeStruct((PART, BL...  79 us
    pallas_call x1, Pallas kernels, on_device(): pl.pallas_call(layer_kernel, out_shape=(jax.ShapeDtypeStruct((rows, D), B...  32.3 us
    unnamed x3, local copies, waits for them, and re-layouts  5.77 us

profile of v1, /device:TPU:0, one launch (start us, length us, event | category | flops | bytes accessed | tf_op | source)
XLA Modules:
  0.0 230.4 jit_solution(2230398040940348604)
XLA Ops:
  0.6 0.5 broadcast.41
  1.1 1.3 reduce.3
  2.5 1.3 copy.27.local_ref
  3.8 0.6 fusion.hm_ref
  4.4 0.1 reshape.72
  4.5 0.6 pad.4.ids_ref
  5.1 3.9 %copy.26.mask_ref = s32[512,7,128]{2,1,0:T(8,128)} copy(s32[512,7,128]{2,0,1:T(8,128)} %param.23) | data formatting | bytes 3670016 | tf_op args[9]
  9.1 79.0 %exchange.1 = (bf16[16,128,256]{2,1,0:T(8,128)(2,1)}, bf16[32,2,128,256]{3,2,1,0:T(8,128)(2,1)}, s32[32,1,128]{2,1,0:T(1,128)}, bf16[512,896]{1,0:T(8,128)(2,1)}) custom-call(bf16[4,128,256]{2,1,0:T(8,128)(2,1)} %bitcast.8, s32[32,1,128]{2,1,0:T(1,128)} %pad.4.ids_ref, s32[512,7,128]{2,1,0:T(8,128)} %copy.26.mask_ref), custom_call_target="tpu_custom_call" | custom-call | tf_op jit(solution)/shard_map/exchange/pallas_call | solution.py:513
  88.0 32.3 %layer.1 = (bf16[512,256]{1,0:T(8,128)(2,1)}, bf16[64,128,256]{2,1,0:T(8,128)(2,1)}, f32[16,128,256]{2,1,0:T(8,128)}, f32[512,256]{1,0:T(8,128)}, bf16[6144,128]{1,0:T(8,128)(2,1)}) custom-call(s32[4,2]{1,0:T(4,128)} %copy.27.local_ref, s32[4,4]{1,0:T(4,128)} %slot_ref.1, bf16[512,256]{1,0:T(8,128)(2,1)} %feat_ref.1, ...), custom_call_target="tpu_custom_call" | custom-call | tf_op jit(solution)/shard_map/layer/pallas_call | solution.py:535
  120.3 105.9 %give_back.1 = (f32[4,128,256]{2,1,0:T(8,128)}, bf16[3,4,128,256]{3,2,1,0:T(8,128)(2,1)}, bf16[6144,128]{1,0:T(8,128)(2,1)}) custom-call(s32[32,1,128]{2,1,0:T(1,128)} %get-tuple-element.32.wanted_ref, bf16[32,2,128,256]{3,2,1,0:T(8,128)(2,1)} %bitcast.7, f32[16,128,256]{2,1,0:T(8,128)} %get-tuple-element.34.near_ref, ...), custom_call_target="tpu_custom_call" | custom-call | tf_op jit(solution)/shard_map/give_back/pallas_call | solution.py:560
  226.3 4.1 %finish.1 = (bf16[512,256]{1,0:T(8,128)(2,1)}, f32[256,256]{1,0:T(8,128)}, f32[256,256]{1,0:T(8,128)}, f32[256,256]{1,0:T(8,128)}, f32[256,256]{1,0:T(8,128)}, /*index=5*/f32[256,1024]{1,0:T(8,128)}, f32[1024,256]{1,0:T(8,128)}) custom-call(f32[512,256]{1,0:T(8,128)} %get-tuple-element.31.rows_ref, f32[4,128,256]{2,1,0:T(8,128)} %get-tuple-element.36.own_ref, ...), custom_call_target="tpu_custom_call" | custom-call | tf_op jit(solution)/shard_map/finish/pallas_call | solution.py:584
  (1 shorter events, 0.0 us)

commit v2 on v1

v2 whole, which is shorter than its diff:
```python
import functools
import math

import jax
import jax.numpy as jnp
from jax import lax
from jax.experimental import pallas as pl
from jax.experimental.pallas import tpu as pltpu
from jax.sharding import PartitionSpec as P

HEADS = 8
EPSILON = 1e-05
MESH = pl.DeviceIdType.MESH
F32 = jnp.float32
BF16 = jnp.bfloat16
NEG = -1e30
VMEM_LIMIT = 56 << 20

D = 256
BLK = 128
TILES = 7
NEAR = 3
ROWS = 4
PART = 16
KEYS = TILES * BLK
N_DOM = 32
N_NODE = 4
CHUNKS = 2
SPAN = BLK // (2 * CHUNKS)

_GROUPS = [
    [(2, 2)],
    [(2, 1), (2, 3)],
    [(1, 2), (3, 2)],
    [(1, 1), (3, 3)],
    [(1, 3), (3, 1)],
    [(2, 0), (0, 2)],
    [(1, 0), (3, 0), (0, 1), (0, 3)],
]
OFFSETS = [(a, b, c) for group in _GROUPS for c in range(2) for a, b in group] + [(0, 0, 1)]


def dom_peer(dom, offset, sign=1):
    core = lax.rem(dom, 2)
    y = lax.rem(dom // 2, 4)
    z = dom // 8
    dz, dy, dc = offset
    return (
        lax.rem(z + (dz if sign > 0 else 4 - dz), 4) * 8
        + lax.rem(y + (dy if sign > 0 else 4 - dy), 4) * 2
        + lax.rem(core + dc, 2)
    )


def nt(a, b):
    return lax.dot_general(a, b, (((1,), (1,)), ((), ())), preferred_element_type=F32)


def tn(a, b):
    return lax.dot_general(a, b, (((0,), (0,)), ((), ())), preferred_element_type=F32)


def nn(a, b):
    return jnp.dot(a, b, preferred_element_type=F32)


def place():
    dom = lax.axis_index("dom")
    return dom // 8, lax.rem(dom // 2, 4), lax.rem(dom, 2), lax.axis_index("node")


def device(z, y, core, node):
    return (z * 8 + y * 2 + core, node)


def four(value):
    return lax.rem(value, 4)


def two(value):
    return lax.rem(value, 2)


def plane_peers(z, y, core):
    peers = [(z, y, two(core + 1))]
    for step in range(1, 4):
        for flip in range(2):
            peers.append((four(z + step), y, two(core + flip)))
            peers.append((z, four(y + step), two(core + flip)))
    return peers


def first_phase(chunk, sources, relays, sends, recvs):
    z, y, core, node = place()
    copies = []
    for step in range(1, 4):
        for half in range(2):
            target = four((z, y)[half] + step)
            copy = pltpu.make_async_remote_copy(
                src_ref=sources[half].at[chunk, pl.ds(target * 8, 8)],
                dst_ref=relays[half].at[chunk, step - 1],
                send_sem=sends.at[chunk, half, step - 1], recv_sem=recvs.at[chunk, half, step - 1],
                device_id=(device(target, y, core, node), device(z, target, core, node))[half],
                device_id_type=MESH,
            )
            copy.start()
            copies.append((half, step, copy))
    return copies


def second_phase(chunk, half, group, sources, relays, lands, sends, recvs):
    z, y, core, node = place()
    copies = []
    for step in range(4):
        for flip in range(2):
            if step == 0 and flip == 0:
                continue
            target = four((y, z)[half] + step)
            side = two(core + flip)
            if group == 0:
                source = sources[half].at[chunk, (z, y)[half] * 8 + target * 2 + side]
            else:
                source = relays[half].at[chunk, group - 1, target * 2 + side]
            copy = pltpu.make_async_remote_copy(
                src_ref=source, dst_ref=lands[half].at[chunk, group, step, flip],
                send_sem=sends.at[chunk, half, group, step, flip],
                recv_sem=recvs.at[chunk, half, group, step, flip],
                device_id=(device(z, target, side, node), device(target, y, side, node))[half],
                device_id_type=MESH,
            )
            copy.start()
            copies.append(copy)
    return copies


def origin(half, group, step, flip):
    z, y, core, node = place()
    far, near = 4 - group, 4 - step
    if half == 0:
        return four(z + far) * 8 + four(y + near) * 2 + two(core + flip)
    return four(z + near) * 8 + four(y + far) * 2 + two(core + flip)


def exchange_kernel(
    feat_ref, table_ref, mask_ref, part_0, part_1, land_a, land_b, wanted_ref, bias_ref,
    ids, stage_a, stage_b, relay_a, relay_b, ids_smem,
    near_send, near_recv, id_send, id_recv, send1, recv1, send2, recv2, own_sem, local_sem,
):
    dom = lax.axis_index("dom")
    z, y, core, node = place()
    stages, relays, lands = (stage_a, stage_b), (relay_a, relay_b), (land_a, land_b)
    parts = (part_0, part_1)
    barrier = pltpu.get_barrier_semaphore()
    for offset in OFFSETS:
        pl.semaphore_signal(barrier, inc=1, device_id=(dom_peer(dom, offset), node), device_id_type=MESH)
    for step in range(1, N_NODE):
        pl.semaphore_signal(
            barrier, inc=1, device_id=(dom, lax.rem(node + step, N_NODE)), device_id_type=MESH
        )
    lane = lax.broadcasted_iota(jnp.int32, (1, BLK), 1)
    for peer in range(N_DOM):
        ids[peer] = jnp.where(
            lane == 0, table_ref[0, 2 * peer], jnp.where(lane == 1, table_ref[0, 2 * peer + 1], 0)
        )
    pl.semaphore_wait(barrier, len(OFFSETS) + N_NODE - 1)

    id_copies = []
    for index, offset in enumerate(OFFSETS):
        peer = dom_peer(dom, offset)
        copy = pltpu.make_async_remote_copy(
            src_ref=ids.at[peer], dst_ref=wanted_ref.at[dom],
            send_sem=id_send.at[index], recv_sem=id_recv.at[index],
            device_id=(peer, node), device_id_type=MESH,
        )
        copy.start()
        id_copies.append(copy)
    near_copies = []
    for chunk in range(CHUNKS):
        for step in range(1, N_NODE):
            copy = pltpu.make_async_remote_copy(
                src_ref=feat_ref.at[:, pl.ds(chunk * 2 * SPAN, 2 * SPAN)],
                dst_ref=parts[chunk].at[pl.ds(node * ROWS, ROWS)],
                send_sem=near_send.at[chunk, step - 1], recv_sem=near_recv.at[chunk, step - 1],
                device_id=(dom, lax.rem(node + step, N_NODE)), device_id_type=MESH,
            )
            copy.start()
            near_copies.append(copy)
    for chunk in range(CHUNKS):
        parts[chunk][pl.ds(node * ROWS, ROWS)] = feat_ref[:, chunk * 2 * SPAN : (chunk + 1) * 2 * SPAN]
    wanted_ref[dom] = ids[dom]
    for copy in id_copies:
        copy.wait()
    to_smem = pltpu.make_async_copy(wanted_ref, ids_smem, local_sem)
    to_smem.start()
    to_smem.wait()

    def stage(chunk):
        def body(peer, carry):
            turned = lax.rem(peer // 2, 4) * 8 + (peer // 8) * 2 + lax.rem(peer, 2)
            for slot in range(2):
                block = ids_smem[peer, 0, slot]
                stage_a[chunk, peer, slot] = parts[chunk][block, 0:SPAN]
                stage_b[chunk, turned, slot] = parts[chunk][block, SPAN : 2 * SPAN]
            return carry

        lax.fori_loop(0, N_DOM, body, 0)

    def keep(chunk, half, group):
        if group == 0:
            source = stages[half].at[chunk, (dom, y * 8 + z * 2 + core)[half]]
        else:
            source = relays[half].at[chunk, group - 1, (y, z)[half] * 2 + core]
        copy = pltpu.make_async_copy(
            source, lands[half].at[chunk, group, 0, 0], own_sem.at[chunk, half, group]
        )
        copy.start()
        return copy

    first = []
    second = []
    kept = []
    for chunk in range(CHUNKS):
        for copy in near_copies[chunk * (N_NODE - 1) : (chunk + 1) * (N_NODE - 1)]:
            copy.wait()
        stage(chunk)
        first.append(first_phase(chunk, stages, relays, send1, recv1))
        for half in range(2):
            second += second_phase(chunk, half, 0, stages, relays, lands, send2, recv2)
            kept.append(keep(chunk, half, 0))

    def to_bias(row, carry):
        start = pl.multiple_of(row * BLK, BLK)
        diagonal = lax.broadcasted_iota(jnp.int32, (BLK, BLK), 0) == lax.broadcasted_iota(
            jnp.int32, (BLK, BLK), 1
        )
        for tile in range(TILES):
            allowed = mask_ref[tile, pl.ds(start, BLK), :] > 0
            if tile == 0:
                allowed = jnp.logical_or(allowed, diagonal)
            bias_ref[pl.ds(start, BLK), tile * BLK : (tile + 1) * BLK] = jnp.where(
                allowed, 0.0, NEG
            ).astype(BF16)
        return carry

    lax.fori_loop(0, ROWS, to_bias, 0)
    for chunk in range(CHUNKS):
        for half, step, copy in first[chunk]:
            copy.wait()
            second += second_phase(chunk, half, step, stages, relays, lands, send2, recv2)
            kept.append(keep(chunk, half, step))
    for copy in kept:
        copy.wait()
    for copy in second:
        copy.wait()


def layer_kernel(
    local_ref, slot_ref, feat_ref, part_0, part_1, land_a, land_b, bias_ref, d_out_ref,
    wq_ref, wk_ref, wv_ref, wo_ref, we_ref, wr_ref, gain_a_ref, gain_f_ref,
    out_ref, back_a, back_b, near_ref, rows_ref, grads_ref,
    fs, ks, vs, qs, ps, mixed, d_mixed, resid_grad, pair_acc, query_acc, expand_acc, reduce_acc, out_acc, sems,
):
    scale = 1.0 / math.sqrt(D // HEADS)
    log2e = math.log2(math.e)
    here_z, here_y, here_core, node = place()
    copies = []
    for row in range(ROWS):
        for tile in range(TILES - NEAR):
            slot = slot_ref[row, tile]
            asked = slot // 2
            dz = four(here_z + 4 - asked // 8)
            dy = four(here_y + 4 - four(asked // 2))
            dc = two(here_core + two(asked))
            for chunk in range(CHUNKS):
                for half in range(2):
                    group, step = ((dz, dy), (dy, dz))[half]
                    copy = pltpu.make_async_copy(
                        (land_a, land_b)[half].at[chunk, group, step, dc, two(slot)],
                        fs.at[row, pl.ds((NEAR + tile) * BLK + (2 * chunk + half) * SPAN, SPAN)],
                        sems.at[row * (TILES - NEAR) + tile, chunk, half],
                    )
                    copy.start()
                    copies.append(copy)
    for row in range(ROWS):
        fs[row, 0:BLK] = feat_ref[row * BLK : (row + 1) * BLK]
        for tile in range(NEAR - 1):
            for chunk, part_ref in enumerate((part_0, part_1)):
                top = (tile + 1) * BLK + chunk * 2 * SPAN
                fs[row, top : top + 2 * SPAN] = part_ref[local_ref[tile, row]]
    back_a[...] = jnp.zeros(back_a.shape, BF16)
    back_b[...] = jnp.zeros(back_b.shape, BF16)
    near_ref[...] = jnp.zeros(near_ref.shape, F32)
    pair_acc[...] = jnp.zeros(pair_acc.shape, F32)
    query_acc[...] = jnp.zeros(query_acc.shape, F32)
    expand_acc[...] = jnp.zeros(expand_acc.shape, F32)
    reduce_acc[...] = jnp.zeros(reduce_acc.shape, F32)
    out_acc[...] = jnp.zeros(out_acc.shape, F32)
    qs[...] = nn(feat_ref[...], wq_ref[...]).astype(BF16)
    for copy in copies:
        copy.wait()

    lane_head = lax.broadcasted_iota(jnp.int32, (1, D), 1) // (D // HEADS)
    head_f32 = [(lane_head == h).astype(F32) for h in range(HEADS)]
    head_low = [mask.astype(BF16) for mask in head_f32]

    def forward(row, carry):
        start = pl.multiple_of(row * BLK, BLK)
        tile_rows = fs[row]
        keys = nn(tile_rows, wk_ref[...]).astype(BF16)
        ks[row] = keys
        values = nn(tile_rows, wv_ref[...]).astype(BF16)
        vs[row] = values
        query = qs[pl.ds(start, BLK), :]
        bias = bias_ref[pl.ds(start, BLK), :].astype(F32)
        total = jnp.zeros((BLK, D), F32)
        for pair in range(HEADS // 2):
            both = jnp.concatenate([query * head_low[2 * pair], query * head_low[2 * pair + 1]], 0)
            scores = nt(both, keys) * (scale * log2e)
            for half in range(2):
                mine = scores[half * BLK : (half + 1) * BLK] + bias
                top = jnp.max(mine, -1, keepdims=True)
                weight = jnp.exp2(mine - top)
                norm = 1.0 / jnp.sum(weight, -1, keepdims=True)
                ps[row, (2 * pair + half) * BLK : (2 * pair + half + 1) * BLK, :] = (weight * norm).astype(BF16)
            got = nn(ps[row, 2 * pair * BLK : (2 * pair + 2) * BLK, :], values)
            total = total + got[:BLK] * head_f32[2 * pair] + got[BLK:] * head_f32[2 * pair + 1]
        mixed[pl.ds(start, BLK), :] = total
        return carry

    lax.fori_loop(0, ROWS, forward, 0)

    chunk = 256

    def feed(step, carry):
        start = pl.multiple_of(step * chunk, chunk)
        sel = pl.ds(start, chunk)
        mixed_low = mixed[sel, :].astype(BF16)
        gain_a = gain_a_ref[...]
        gain_f = gain_f_ref[...]
        residual = feat_ref[sel, :].astype(F32) + nn(mixed_low, wo_ref[...])
        center = residual - jnp.mean(residual, -1, keepdims=True)
        rstd_a = lax.rsqrt(jnp.mean(center * center, -1, keepdims=True) + EPSILON)
        hat_a = center * rstd_a
        first_low = (hat_a * gain_a).astype(BF16)
        pre = nn(first_low, we_ref[...])
        root = math.sqrt(2.0 / math.pi)
        square = pre * pre
        tanh = jnp.tanh(root * (pre + 0.044715 * (square * pre)))
        half = 0.5 * (1.0 + tanh)
        act_low = (pre * half).astype(BF16)
        slope = half + 0.5 * pre * (1.0 - tanh * tanh) * (root * (1.0 + 3.0 * 0.044715 * square))
        second = first_low.astype(F32) + nn(act_low, wr_ref[...])
        center = second - jnp.mean(second, -1, keepdims=True)
        rstd_f = lax.rsqrt(jnp.mean(center * center, -1, keepdims=True) + EPSILON)
        hat_f = center * rstd_f
        out_ref[sel, :] = (hat_f * gain_f).astype(BF16)
        d_hat = d_out_ref[sel, :].astype(F32) * gain_f
        d_second = rstd_f * (
            d_hat - jnp.mean(d_hat, -1, keepdims=True) - hat_f * jnp.mean(d_hat * hat_f, -1, keepdims=True)
        )
        d_second_low = d_second.astype(BF16)
        reduce_acc[...] += tn(d_second_low, act_low)
        d_pre_low = (nt(d_second_low, wr_ref[...]) * slope).astype(BF16)
        expand_acc[...] += tn(first_low, d_pre_low)
        d_first = d_second + nt(d_pre_low, we_ref[...])
        d_hat = d_first * gain_a
        d_resid = rstd_a * (
            d_hat - jnp.mean(d_hat, -1, keepdims=True) - hat_a * jnp.mean(d_hat * hat_a, -1, keepdims=True)
        )
        resid_grad[sel, :] = d_resid
        d_resid_low = d_resid.astype(BF16)
        out_acc[...] += tn(mixed_low, d_resid_low)
        d_mixed[sel, :] = nt(d_resid_low, wo_ref[...]).astype(BF16)
        return carry

    lax.fori_loop(0, ROWS * BLK // chunk, feed, 0)

    first_half = lax.broadcasted_iota(jnp.int32, (64, BLK), 0) < 32

    def block_diagonal(turned, pair):
        piece = turned[64 * pair : 64 * pair + 64]
        return jnp.concatenate(
            [jnp.where(first_half, piece, 0.0), jnp.where(first_half, 0.0, piece)], 1
        ).astype(BF16)

    def backward(row, carry):
        start = pl.multiple_of(row * BLK, BLK)
        keys = ks[row]
        values = vs[row]
        query = qs[pl.ds(start, BLK), :]
        grad = d_mixed[pl.ds(start, BLK), :]
        query_t = query.astype(F32).T
        grad_t = grad.astype(F32).T
        inner_full = grad.astype(F32) * mixed[pl.ds(start, BLK), :]
        d_query = jnp.zeros((BLK, D), F32)
        key_parts = []
        value_parts = []
        for pair in range(HEADS // 2):
            both = jnp.concatenate([grad * head_low[2 * pair], grad * head_low[2 * pair + 1]], 0)
            inner = jnp.concatenate(
                [
                    jnp.sum(inner_full * head_f32[2 * pair], -1, keepdims=True),
                    jnp.sum(inner_full * head_f32[2 * pair + 1], -1, keepdims=True),
                ],
                0,
            )
            probs_low = ps[row, 2 * pair * BLK : (2 * pair + 2) * BLK, :]
            d_probs = nt(both, values)
            d_scores = (probs_low.astype(F32) * ((d_probs - inner) * scale)).astype(BF16)
            got = nn(d_scores, keys)
            d_query = d_query + got[:BLK] * head_f32[2 * pair] + got[BLK:] * head_f32[2 * pair + 1]
            key_parts.append(nn(block_diagonal(query_t, pair), d_scores).astype(BF16))
            value_parts.append(nn(block_diagonal(grad_t, pair), probs_low).astype(BF16))
        d_keys_t = jnp.concatenate(key_parts, 0)
        d_values_t = jnp.concatenate(value_parts, 0)
        tile_rows = fs[row]
        pair_acc[0:D, :] += nn(d_keys_t, tile_rows)
        pair_acc[D : 2 * D, :] += nn(d_values_t, tile_rows)
        d_rows_t = nn(wk_ref[...], d_keys_t) + nn(wv_ref[...], d_values_t)
        near_ids = [node * ROWS + row, local_ref[0, row], local_ref[1, row]]
        for tile in range(TILES):
            piece = d_rows_t[:, tile * BLK : (tile + 1) * BLK].T
            if tile < NEAR:
                near_ref[near_ids[tile]] += piece
            else:
                piece = piece.astype(BF16)
                slot = slot_ref[row, tile - NEAR]
                asked = slot // 2
                turned = four(asked // 2) * 8 + (asked // 8) * 2 + two(asked)
                for chunk in range(CHUNKS):
                    top = 2 * chunk * SPAN
                    back_a[chunk, asked, two(slot)] = piece[top : top + SPAN]
                    back_b[chunk, turned, two(slot)] = piece[top + SPAN : top + 2 * SPAN]
        d_query_low = d_query.astype(BF16)
        query_acc[...] += tn(tile_rows[:BLK], d_query_low)
        rows_ref[pl.ds(start, BLK), :] = resid_grad[pl.ds(start, BLK), :] + nt(d_query_low, wq_ref[...])
        return carry

    lax.fori_loop(0, ROWS, backward, 0)

    spot = 0
    for acc in (query_acc, pair_acc, out_acc, expand_acc, reduce_acc):
        for top in range(0, acc.shape[0], D):
            for left in range(0, acc.shape[1], BLK):
                grads_ref[spot : spot + D, :] = acc[top : top + D, left : left + BLK].astype(BF16)
                spot += D


SUM_ROWS = 6144
CORE_ROWS = SUM_ROWS // 2
X_ROWS = CORE_ROWS // 4
Z_ROWS = X_ROWS // 4
Y_ROWS = Z_ROWS // 4


def rows_at(index, size):
    return pl.ds(pl.multiple_of(index * size, size), size)


def return_kernel(
    wanted_ref, back_a, back_b, near_ref, grads_ref,
    own_ref, cross_ref, sum_ref,
    relay_a, relay_b, land_a, land_b, acc, chosen, cross_send,
    core_recv, core_sum, x_recv, x_sum, z_recv, z_sum, y_recv, y_sum, z_all, x_all,
    send1, recv1, send2, recv2, own_sem, cross_sems, core_sems, x_sems, z_sems, y_sems,
):
    dom = lax.axis_index("dom")
    z, y, core, node = place()
    sources, relays, lands = (back_a, back_b), (relay_a, relay_b), (land_a, land_b)

    barrier = pltpu.get_barrier_semaphore()
    peers = [device(*peer, node) for peer in plane_peers(z, y, core)]
    peers += [(dom, four(node + step)) for step in range(1, N_NODE)]
    for peer in peers:
        pl.semaphore_signal(barrier, inc=1, device_id=peer, device_id_type=MESH)
    pl.semaphore_wait(barrier, len(peers))

    def push(src, dst, sems, key, target):
        copy = pltpu.make_async_remote_copy(
            src_ref=src, dst_ref=dst, send_sem=sems.at[(0,) + key], recv_sem=sems.at[(1,) + key],
            device_id=target, device_id_type=MESH,
        )
        copy.start()
        return copy

    sibling = device(z, y, two(core + 1), node)
    axes = [
        (node, lambda other: device(z, y, core, other)),
        (z, lambda other: device(other, y, core, node)),
        (y, lambda other: device(z, other, core, node)),
    ]

    def scatter(axis, src, dst, sems, size):
        index, target = axes[axis]
        copies = []
        for step in range(1, 4):
            other = four(index + step)
            copies.append(push(src.at[rows_at(other, size)], dst.at[step - 1], sems, (0, step - 1), target(other)))
        return copies

    def gather(axis, src, dst, sems, size):
        index, target = axes[axis]
        mine = rows_at(index, size)
        copies = []
        for step in range(1, 4):
            copies.append(push(src, dst.at[mine], sems, (1, step - 1), target(four(index + step))))
        dst[mine, :] = src[...]
        return copies

    def finish(copies):
        for copy in copies:
            copy.wait()

    def add_up(axis, src, recv, out, size):
        total = src[rows_at(axes[axis][0], size), :].astype(F32)
        for step in range(3):
            total = total + recv[step].astype(F32)
        out[...] = total.astype(BF16)

    core_mine = rows_at(core, CORE_ROWS)
    core_copy = push(grads_ref.at[rows_at(two(core + 1), CORE_ROWS)], core_recv, core_sems, (0,), sibling)
    first = []
    second = {}
    kept = {}

    def keep(chunk, half):
        copy = pltpu.make_async_copy(
            sources[half].at[chunk, (dom, y * 8 + z * 2 + core)[half]],
            lands[half].at[chunk, 0, 0, 0], own_sem.at[chunk, half],
        )
        copy.start()
        return copy

    for chunk in range(CHUNKS):
        first.append(first_phase(chunk, sources, relays, send1, recv1))
        for half in range(2):
            second[chunk, half, 0] = second_phase(chunk, half, 0, sources, relays, lands, send2, recv2)
            kept[chunk, half] = keep(chunk, half)

    core_copy.wait()
    core_sum[...] = (grads_ref[core_mine, :].astype(F32) + core_recv[...].astype(F32)).astype(BF16)
    x_copies = scatter(0, core_sum, x_recv, x_sems, X_ROWS)

    block_of = lax.broadcasted_iota(jnp.int32, (256, 256), 0) // 16
    same_row = lax.rem(lax.broadcasted_iota(jnp.int32, (256, 256), 0), 16) == lax.rem(
        lax.broadcasted_iota(jnp.int32, (256, 256), 1), 16
    )
    slot_of = lax.broadcasted_iota(jnp.int32, (1, 256), 1) // 16
    for half in range(2):
        for group in range(4):
            names = jnp.zeros((1, 256), jnp.int32)
            for step in range(4):
                for flip in range(2):
                    source = origin(half, group, step, flip)
                    for slot in range(2):
                        names = jnp.where(
                            slot_of == step * 4 + flip * 2 + slot, wanted_ref[source, 0, slot], names
                        )
            chosen[half, group] = jnp.logical_and(names == block_of, same_row).astype(F32).astype(BF16)

    def forward(chunk):
        for half, step, copy in first[chunk]:
            copy.wait()
            second[chunk, half, step] = second_phase(chunk, half, step, sources, relays, lands, send2, recv2)
            lands[half][chunk, step, 0, 0] = relays[half][chunk, step - 1, (y, z)[half] * 2 + core]

    def combine(chunk, group):
        for half in range(2):
            finish(second[chunk, half, group])
            if group == 0:
                kept[chunk, half].wait()
            for top in range(0, SPAN, 16):
                rows = slice((2 * chunk + half) * SPAN + top, (2 * chunk + half) * SPAN + top + 16)
                arrived = lands[half][chunk, group, :, :, :, top : top + 16, :].reshape(256, D)
                added = nn(chosen[half, group], arrived).reshape(PART, 16, D)
                if group == 0:
                    acc[:, rows, :] = near_ref[:, rows, :] + added
                else:
                    acc[:, rows, :] += added

    def cross(chunk):
        rows = slice(2 * chunk * SPAN, 2 * (chunk + 1) * SPAN)
        cross_send[chunk] = acc[:, rows, :].astype(BF16)
        copies = []
        for step in range(1, N_NODE):
            other = four(node + step)
            copies.append(
                push(
                    cross_send.at[chunk, pl.ds(other * ROWS, ROWS)], cross_ref.at[step - 1, chunk],
                    cross_sems, (chunk, step - 1), (dom, other),
                )
            )
        return copies

    forward(0)
    finish(x_copies)
    add_up(0, core_sum, x_recv, x_sum, X_ROWS)
    z_copies = scatter(1, x_sum, z_recv, z_sems, Z_ROWS)
    for chunk in range(1, CHUNKS):
        forward(chunk)
    finish(z_copies)
    add_up(1, x_sum, z_recv, z_sum, Z_ROWS)
    y_copies = scatter(2, z_sum, y_recv, y_sems, Y_ROWS)
    combine(0, 0)
    finish(y_copies)
    add_up(2, z_sum, y_recv, y_sum, Y_ROWS)
    y_copies = gather(2, y_sum, z_all, y_sems, Y_ROWS)
    combine(0, 1)
    finish(y_copies)
    z_copies = gather(1, z_all, x_all, z_sems, Z_ROWS)
    combine(0, 2)
    finish(z_copies)
    my_part = sum_ref.at[core_mine]
    x_copies = gather(0, x_all, my_part, x_sems, X_ROWS)
    combine(0, 3)
    crossing = cross(0)
    finish(x_copies)
    core_copy = push(my_part, my_part, core_sems, (1,), sibling)
    for chunk in range(1, CHUNKS):
        for group in range(4):
            combine(chunk, group)
        crossing += cross(chunk)
    own_ref[...] = acc[pl.ds(node * ROWS, ROWS)]
    core_copy.wait()
    finish(crossing)


def finish_kernel(factor, rows_ref, own_ref, cross_ref, sum_ref, dx_ref, gq, gk, gv, go, ge, gr):
    for row in range(ROWS):
        for chunk in range(CHUNKS):
            rows = slice(2 * chunk * SPAN, 2 * (chunk + 1) * SPAN)
            span = slice(row * BLK + rows.start, row * BLK + rows.stop)
            total = rows_ref[span, :] + own_ref[row, rows, :]
            for step in range(N_NODE - 1):
                total = total + cross_ref[step, chunk, row].astype(F32)
            dx_ref[span, :] = total.astype(BF16)

    def piece(index):
        return sum_ref[index * D : (index + 1) * D, :].astype(F32) * factor

    for half in range(2):
        span = slice(half * BLK, (half + 1) * BLK)
        gq[:, span] = piece(half)
        gk[span, :] = piece(2 + half).T
        gv[span, :] = piece(4 + half).T
        go[:, span] = piece(6 + half)
    for part in range(8):
        span = slice(part * BLK, (part + 1) * BLK)
        ge[:, span] = piece(8 + part)
        gr[span, :] = piece(16 + part).T


def vmem(shape, dtype):
    return pltpu.VMEM(shape, dtype)


IN_VMEM = pl.BlockSpec(memory_space=pltpu.VMEM)
IN_SMEM = pl.BlockSpec(memory_space=pltpu.SMEM)
ANYWHERE = pl.BlockSpec(memory_space=pl.ANY)


def on_device(
    features, w_query, w_key, w_value, w_out, w_expand, w_reduce, gain_attn, gain_ffn,
    tile_mask, local_block, remote_slot, remote_block, d_out,
):
    rows = features.shape[0]
    dma = pltpu.SemaphoreType.DMA
    peers = len(OFFSETS)
    land = (CHUNKS, 4, 4, 2, 2, SPAN, D)
    staged = (CHUNKS, N_DOM, 2, SPAN, D)
    relay = (CHUNKS, 3, 8, 2, SPAN, D)
    phase_sems = [dma((CHUNKS, 2, 3)), dma((CHUNKS, 2, 3)), dma((CHUNKS, 2, 4, 4, 2)), dma((CHUNKS, 2, 4, 4, 2))]
    part_0, part_1, land_a, land_b, wanted, bias = pl.pallas_call(
        exchange_kernel,
        out_shape=(
            jax.ShapeDtypeStruct((PART, 2 * SPAN, D), BF16),
            jax.ShapeDtypeStruct((PART, 2 * SPAN, D), BF16),
            jax.ShapeDtypeStruct(land, BF16),
            jax.ShapeDtypeStruct(land, BF16),
            jax.ShapeDtypeStruct((N_DOM, 1, BLK), jnp.int32),
            jax.ShapeDtypeStruct((rows, KEYS), BF16),
        ),
        in_specs=[IN_VMEM, IN_SMEM, IN_VMEM],
        out_specs=(IN_VMEM, IN_VMEM, ANYWHERE, ANYWHERE, IN_VMEM, IN_VMEM),
        scratch_shapes=[
            vmem((N_DOM, 1, BLK), jnp.int32), vmem(staged, BF16), vmem(staged, BF16),
            vmem(relay, BF16), vmem(relay, BF16), pltpu.SMEM((N_DOM, 1, BLK), jnp.int32),
            dma((CHUNKS, N_NODE - 1)), dma((CHUNKS, N_NODE - 1)), dma((peers,)), dma((peers,)),
        ]
        + phase_sems
        + [dma((CHUNKS, 2, 4)), dma],
        compiler_params=pltpu.CompilerParams(
            collective_id=1, has_side_effects=True, vmem_limit_bytes=VMEM_LIMIT
        ),
        name="exchange",
    )(features.reshape(ROWS, BLK, D), remote_block.reshape(1, 2 * N_DOM), jnp.transpose(tile_mask, (1, 0, 2)))

    output, back_a, back_b, near, d_rows, grads = pl.pallas_call(
        layer_kernel,
        out_shape=(
            jax.ShapeDtypeStruct((rows, D), BF16),
            jax.ShapeDtypeStruct(staged, BF16),
            jax.ShapeDtypeStruct(staged, BF16),
            jax.ShapeDtypeStruct((PART, BLK, D), F32),
            jax.ShapeDtypeStruct((rows, D), F32),
            jax.ShapeDtypeStruct((SUM_ROWS, BLK), BF16),
        ),
        in_specs=[IN_SMEM, IN_SMEM, IN_VMEM, IN_VMEM, IN_VMEM, ANYWHERE, ANYWHERE] + [IN_VMEM] * 10,
        out_specs=(IN_VMEM,) * 6,
        scratch_shapes=[
            vmem((ROWS, KEYS, D), BF16), vmem((ROWS, KEYS, D), BF16), vmem((ROWS, KEYS, D), BF16),
            vmem((rows, D), BF16), vmem((ROWS, HEADS * BLK, KEYS), BF16), vmem((rows, D), F32),
            vmem((rows, D), BF16), vmem((rows, D), F32), vmem((2 * D, D), F32), vmem((D, D), F32),
            vmem((D, 4 * D), F32), vmem((D, 4 * D), F32), vmem((D, D), F32), dma((16, CHUNKS, 2)),
        ],
        compiler_params=pltpu.CompilerParams(vmem_limit_bytes=VMEM_LIMIT),
        name="layer",
    )(
        local_block.T, remote_slot, features, part_0, part_1, land_a, land_b, bias, d_out,
        w_query, w_key, w_value, w_out, w_expand, w_reduce, gain_attn.reshape(1, D), gain_ffn.reshape(1, D),
    )

    own, cross, summed = pl.pallas_call(
        return_kernel,
        out_shape=(
            jax.ShapeDtypeStruct((ROWS, BLK, D), F32),
            jax.ShapeDtypeStruct((N_NODE - 1, CHUNKS, ROWS, 2 * SPAN, D), BF16),
            jax.ShapeDtypeStruct((SUM_ROWS, BLK), BF16),
        ),
        in_specs=[IN_SMEM, ANYWHERE, ANYWHERE, IN_VMEM, IN_VMEM],
        out_specs=(IN_VMEM,) * 3,
        scratch_shapes=[
            vmem(relay, BF16), vmem(relay, BF16), vmem(land, BF16), vmem(land, BF16),
            vmem((PART, BLK, D), F32), vmem((2, 4, 256, 256), BF16), vmem((CHUNKS, PART, 2 * SPAN, D), BF16),
            vmem((CORE_ROWS, BLK), BF16), vmem((CORE_ROWS, BLK), BF16),
            vmem((3, X_ROWS, BLK), BF16), vmem((X_ROWS, BLK), BF16),
            vmem((3, Z_ROWS, BLK), BF16), vmem((Z_ROWS, BLK), BF16),
            vmem((3, Y_ROWS, BLK), BF16), vmem((Y_ROWS, BLK), BF16),
            vmem((Z_ROWS, BLK), BF16), vmem((X_ROWS, BLK), BF16),
        ]
        + phase_sems
        + [dma((CHUNKS, 2)), dma((2, CHUNKS, 3)), dma((2, 2)), dma((2, 2, 3)), dma((2, 2, 3)), dma((2, 2, 3))],
        compiler_params=pltpu.CompilerParams(
            collective_id=2, has_side_effects=True, vmem_limit_bytes=VMEM_LIMIT
        ),
        name="give_back",
    )(wanted, back_a, back_b, near, grads)

    factor = 1.0 / math.sqrt(rows * N_DOM * N_NODE)
    finished = pl.pallas_call(
        functools.partial(finish_kernel, factor),
        out_shape=(
            jax.ShapeDtypeStruct((rows, D), BF16),
            jax.ShapeDtypeStruct((D, D), F32),
            jax.ShapeDtypeStruct((D, D), F32),
            jax.ShapeDtypeStruct((D, D), F32),
            jax.ShapeDtypeStruct((D, D), F32),
            jax.ShapeDtypeStruct((D, 4 * D), F32),
            jax.ShapeDtypeStruct((4 * D, D), F32),
        ),
        in_specs=[IN_VMEM] * 4,
        out_specs=(IN_VMEM,) * 7,
        compiler_params=pltpu.CompilerParams(vmem_limit_bytes=VMEM_LIMIT),
        name="finish",
    )(d_rows, own, cross, summed)
    return (output,) + tuple(finished)


def solution(mesh):
    split = P(("dom", "node"), None)
    placed = (
        (split,) + (P(),) * 8 + (P(("dom", "node"), None, None), split, split, P("dom", "node", None), split)
    )
    return jax.shard_map(
        on_device, mesh=mesh, in_specs=placed, out_specs=(split, split) + (P(),) * 6, check_vma=False
    )
```

time: 231 us -> 194 us (0.84)
  Pallas kernels: 221 us -> 193 us
  local copies, waits for them, and re-layouts: 6.49 us -> 0 us
    pallas_call x1, Pallas kernels: 106 us -> 85.4 us  [on_device(): pl.pallas_call(return_kernel, out_shape=(jax.ShapeDtypeStruct((ROWS, BLK,...]
    pallas_call x1, Pallas kernels: 79 us -> 70.2 us  [on_device(): pl.pallas_call(exchange_kernel, out_shape=(jax.ShapeDtypeStruct((PART, 2...]
    unnamed x3 -> x0, local copies, waits for them, and re-layouts: 5.77 us -> none
where the time goes in v2:
time: 194 us; the launch traced here: 193 us
  Pallas kernels  193 us (99%)
    pallas_call x1, Pallas kernels, on_device(): pl.pallas_call(return_kernel, out_shape=(jax.ShapeDtypeStruct((ROWS, BLK,...  85.4 us
    pallas_call x1, Pallas kernels, on_device(): pl.pallas_call(exchange_kernel, out_shape=(jax.ShapeDtypeStruct((PART, 2...  70.2 us
    pallas_call x1, Pallas kernels, on_device(): pl.pallas_call(layer_kernel, out_shape=(jax.ShapeDtypeStruct((rows, D), B...  32.9 us
    pallas_call x1, Pallas kernels, on_device(): pl.pallas_call(functools.partial(finish_kernel, factor), out_shape=(jax.S...  4.11 us

profile of v2, /device:TPU:0, one launch (start us, length us, event | category | flops | bytes accessed | tf_op | source)
XLA Modules:
  0.0 193.3 jit_solution(11155475838405678514)
XLA Ops:
  0.6 70.2 %exchange.1 = (bf16[16,64,256]{2,1,0:T(8,128)(2,1)}, bf16[16,64,256]{2,1,0:T(8,128)(2,1)}, bf16[2,4,4,2,2,32,256]{6,5,4,3,2,1,0:T(8,128)(2,1)}, bf16[2,4,4,2,2,3...) custom-call(bf16[4,128,256]{2,1,0:T(8,128)(2,1)} %bitcast.7, s32[1,64]{1,0:T(1,128)} %bitcast.11, ...), custom_call_target="tpu_custom_call" | custom-call | tf_op jit(solution)/shard_map/exchange/pallas_call | solution.py:673
  70.9 32.9 %layer.1 = (bf16[512,256]{1,0:T(8,128)(2,1)}, bf16[2,32,2,32,256]{4,3,2,1,0:T(8,128)(2,1)}, bf16[2,32,2,32,256]{4,3,2,1,0:T(8,128)(2,1)}, f32[16,128,256]{2,1,0:...) custom-call(s32[2,4]{1,0:T(2,128)} %bitcast.8, s32[4,4]{1,0:T(4,128)} %slot_ref.1, bf16[512,256]{1,0:T(8,128)(2,1)} %feat_ref.1, ...), custom_call_target="tpu_custom_call" | custom-call | tf_op jit(solution)/shard_map/layer/pallas_call | solution.py:698
  103.7 85.4 %give_back.1 = (f32[4,128,256]{2,1,0:T(8,128)}, bf16[3,2,4,64,256]{4,3,2,1,0:T(8,128)(2,1)}, bf16[6144,128]{1,0:T(8,128)(2,1)}) custom-call(s32[32,1,128]{2,1,0:T(1,128)} %get-tuple-element.37.wanted_ref, bf16[2,32,2,32,256]{4,3,2,1,0:T(8,128)(2,1)} %get-tuple-element.38.back_a, bf16[2,32,2,32,256]{4,3,2,1,0:T(8,128)(2,1)} %get-tuple-element.39.back_b, ...), custom_call_target="tpu_custom_call" | custom-call | tf_op jit(solution)/shard_map/give_back/pallas_call | solution.py:723
  189.2 4.1 %finish.1 = (bf16[512,256]{1,0:T(8,128)(2,1)}, f32[256,256]{1,0:T(8,128)}, f32[256,256]{1,0:T(8,128)}, f32[256,256]{1,0:T(8,128)}, f32[256,256]{1,0:T(8,128)}, /*index=5*/f32[256,1024]{1,0:T(8,128)}, f32[1024,256]{1,0:T(8,128)}) custom-call(f32[512,256]{1,0:T(8,128)} %get-tuple-element.36.rows_ref, f32[4,128,256]{2,1,0:T(8,128)} %get-tuple-element.42.own_ref, ...), custom_call_target="tpu_custom_call" | custom-call | tf_op jit(solution)/shard_map/finish/pallas_call | solution.py:750

commit v3 on v2

v3 whole, which is shorter than its diff:
```python
import functools
import math

import jax
import jax.numpy as jnp
from jax import lax
from jax.experimental import pallas as pl
from jax.experimental.pallas import tpu as pltpu
from jax.sharding import PartitionSpec as P

HEADS = 8
EPSILON = 1e-05
MESH = pl.DeviceIdType.MESH
F32 = jnp.float32
BF16 = jnp.bfloat16
NEG = -1e30
VMEM_LIMIT = 60 << 20

D = 256
BLK = 128
TILES = 7
NEAR = 3
ROWS = 4
PART = 16
KEYS = TILES * BLK
FAR = ROWS * (TILES - NEAR)
N_DOM = 32
N_NODE = 4
CHUNKS = 2
SPAN = BLK // (2 * CHUNKS)

_GROUPS = [
    [(2, 2)],
    [(2, 1), (2, 3)],
    [(1, 2), (3, 2)],
    [(1, 1), (3, 3)],
    [(1, 3), (3, 1)],
    [(2, 0), (0, 2)],
    [(1, 0), (3, 0), (0, 1), (0, 3)],
]
OFFSETS = [(a, b, c) for group in _GROUPS for c in range(2) for a, b in group] + [(0, 0, 1)]


def dom_peer(dom, offset, sign=1):
    core = lax.rem(dom, 2)
    y = lax.rem(dom // 2, 4)
    z = dom // 8
    dz, dy, dc = offset
    return (
        lax.rem(z + (dz if sign > 0 else 4 - dz), 4) * 8
        + lax.rem(y + (dy if sign > 0 else 4 - dy), 4) * 2
        + lax.rem(core + dc, 2)
    )


def nt(a, b):
    return lax.dot_general(a, b, (((1,), (1,)), ((), ())), preferred_element_type=F32)


def tn(a, b):
    return lax.dot_general(a, b, (((0,), (0,)), ((), ())), preferred_element_type=F32)


def nn(a, b):
    return jnp.dot(a, b, preferred_element_type=F32)


def place():
    dom = lax.axis_index("dom")
    return dom // 8, lax.rem(dom // 2, 4), lax.rem(dom, 2), lax.axis_index("node")


def device(z, y, core, node):
    return (z * 8 + y * 2 + core, node)


def four(value):
    return lax.rem(value, 4)


def two(value):
    return lax.rem(value, 2)


def first_phase(chunk, sources, relays, sends, recvs):
    z, y, core, node = place()
    copies = []
    for step in range(1, 4):
        for half in range(2):
            target = four((z, y)[half] + step)
            copy = pltpu.make_async_remote_copy(
                src_ref=sources[half].at[chunk, pl.ds(target * 8, 8)],
                dst_ref=relays[half].at[chunk, step - 1],
                send_sem=sends.at[chunk, half, step - 1], recv_sem=recvs.at[chunk, half, step - 1],
                device_id=(device(target, y, core, node), device(z, target, core, node))[half],
                device_id_type=MESH,
            )
            copy.start()
            copies.append((half, step, copy))
    return copies


def second_phase(chunk, half, group, sources, relays, lands, sends, recvs):
    z, y, core, node = place()
    copies = []
    for step in range(4):
        for flip in range(2):
            if step == 0 and flip == 0:
                continue
            target = four((y, z)[half] + step)
            side = two(core + flip)
            if group == 0:
                source = sources[half].at[chunk, (z, y)[half] * 8 + target * 2 + side]
            else:
                source = relays[half].at[chunk, group - 1, target * 2 + side]
            copy = pltpu.make_async_remote_copy(
                src_ref=source, dst_ref=lands[half].at[chunk, group, step, flip],
                send_sem=sends.at[chunk, half, group, step, flip],
                recv_sem=recvs.at[chunk, half, group, step, flip],
                device_id=(device(z, target, side, node), device(target, y, side, node))[half],
                device_id_type=MESH,
            )
            copy.start()
            copies.append(copy)
    return copies


def origin(half, group, step, flip):
    z, y, core, node = place()
    far, near = 4 - group, 4 - step
    if half == 0:
        return four(z + far) * 8 + four(y + near) * 2 + two(core + flip)
    return four(z + near) * 8 + four(y + far) * 2 + two(core + flip)


def exchange_kernel(
    feat_ref, table_ref, slot_ref, mask_ref, part_0, part_1, land_a, land_b, wanted_ref, bias_ref, tile_ref,
    ids, stage_a, stage_b, relay_a, relay_b, ids_smem,
    near_send, near_recv, id_send, id_recv, send1, recv1, send2, recv2, own_sem, local_sem,
):
    dom = lax.axis_index("dom")
    z, y, core, node = place()
    stages, relays, lands = (stage_a, stage_b), (relay_a, relay_b), (land_a, land_b)
    parts = (part_0, part_1)
    barrier = pltpu.get_barrier_semaphore()
    for offset in OFFSETS:
        pl.semaphore_signal(barrier, inc=1, device_id=(dom_peer(dom, offset), node), device_id_type=MESH)
    for step in range(1, N_NODE):
        pl.semaphore_signal(
            barrier, inc=1, device_id=(dom, lax.rem(node + step, N_NODE)), device_id_type=MESH
        )
    lane = lax.broadcasted_iota(jnp.int32, (1, BLK), 1)
    for peer in range(N_DOM):
        ids[peer] = jnp.where(
            lane == 0, table_ref[0, 2 * peer], jnp.where(lane == 1, table_ref[0, 2 * peer + 1], 0)
        )
    pl.semaphore_wait(barrier, len(OFFSETS) + N_NODE - 1)

    id_copies = []
    for index, offset in enumerate(OFFSETS):
        peer = dom_peer(dom, offset)
        copy = pltpu.make_async_remote_copy(
            src_ref=ids.at[peer], dst_ref=wanted_ref.at[dom],
            send_sem=id_send.at[index], recv_sem=id_recv.at[index],
            device_id=(peer, node), device_id_type=MESH,
        )
        copy.start()
        id_copies.append(copy)
    near_copies = []
    for chunk in range(CHUNKS):
        for step in range(1, N_NODE):
            copy = pltpu.make_async_remote_copy(
                src_ref=feat_ref.at[:, pl.ds(chunk * 2 * SPAN, 2 * SPAN)],
                dst_ref=parts[chunk].at[pl.ds(node * ROWS, ROWS)],
                send_sem=near_send.at[chunk, step - 1], recv_sem=near_recv.at[chunk, step - 1],
                device_id=(dom, lax.rem(node + step, N_NODE)), device_id_type=MESH,
            )
            copy.start()
            near_copies.append(copy)
    for chunk in range(CHUNKS):
        parts[chunk][pl.ds(node * ROWS, ROWS)] = feat_ref[:, chunk * 2 * SPAN : (chunk + 1) * 2 * SPAN]
    wanted_ref[dom] = ids[dom]
    for copy in id_copies:
        copy.wait()
    to_smem = pltpu.make_async_copy(wanted_ref, ids_smem, local_sem)
    to_smem.start()
    to_smem.wait()

    def stage(chunk):
        def body(peer, carry):
            turned = lax.rem(peer // 2, 4) * 8 + (peer // 8) * 2 + lax.rem(peer, 2)
            for slot in range(2):
                block = ids_smem[peer, 0, slot]
                stage_a[chunk, peer, slot] = parts[chunk][block, 0:SPAN]
                stage_b[chunk, turned, slot] = parts[chunk][block, SPAN : 2 * SPAN]
            return carry

        lax.fori_loop(0, N_DOM, body, 0)

    def keep(chunk, half, group):
        if group == 0:
            source = stages[half].at[chunk, (dom, y * 8 + z * 2 + core)[half]]
        else:
            source = relays[half].at[chunk, group - 1, (y, z)[half] * 2 + core]
        copy = pltpu.make_async_copy(
            source, lands[half].at[chunk, group, 0, 0], own_sem.at[chunk, half, group]
        )
        copy.start()
        return copy

    first = []
    second = []
    kept = []
    for chunk in range(CHUNKS):
        for copy in near_copies[chunk * (N_NODE - 1) : (chunk + 1) * (N_NODE - 1)]:
            copy.wait()
        stage(chunk)
        first.append(first_phase(chunk, stages, relays, send1, recv1))
        for half in range(2):
            second += second_phase(chunk, half, 0, stages, relays, lands, send2, recv2)
            kept.append(keep(chunk, half, 0))

    def to_bias(row, carry):
        start = pl.multiple_of(row * BLK, BLK)
        diagonal = lax.broadcasted_iota(jnp.int32, (BLK, BLK), 0) == lax.broadcasted_iota(
            jnp.int32, (BLK, BLK), 1
        )
        for tile in range(TILES):
            allowed = mask_ref[tile, pl.ds(start, BLK), :] > 0
            if tile == 0:
                allowed = jnp.logical_or(allowed, diagonal)
            bias_ref[pl.ds(start, BLK), tile * BLK : (tile + 1) * BLK] = jnp.where(
                allowed, 0.0, NEG
            ).astype(BF16)
        return carry

    lax.fori_loop(0, ROWS, to_bias, 0)

    def tile_of(slot, carry):
        found = jnp.int32(FAR)
        for row in range(ROWS):
            for tile in range(TILES - NEAR):
                found = jnp.where(slot_ref[row, tile] == slot, row * (TILES - NEAR) + tile, found)
        tile_ref[0, slot] = found
        return carry

    lax.fori_loop(0, 2 * N_DOM, tile_of, 0)
    for chunk in range(CHUNKS):
        for half, step, copy in first[chunk]:
            copy.wait()
            second += second_phase(chunk, half, step, stages, relays, lands, send2, recv2)
            kept.append(keep(chunk, half, step))
    for copy in kept:
        copy.wait()
    for copy in second:
        copy.wait()


SUM_ROWS = (4096, 2048)


def rows_at(index, size):
    return pl.ds(pl.multiple_of(index * size, size), size)


def layer_kernel(
    local_ref, slot_ref, tile_ref, wanted_ref, feat_ref, part_0, part_1, far_a, far_b, bias_ref, d_out_ref,
    wq_ref, wk_ref, wv_ref, wo_ref, we_ref, wr_ref, gain_a_ref, gain_f_ref,
    out_ref, base_ref, cross_ref, sum_0, sum_1,
    fs, ks, vs, qs, ps, mixed, d_mixed, d_query, far_keys_t, far_values_t, near_keys_t, near_values_t,
    far_tiles, near_tiles, pair_acc, query_acc, expand_acc, reduce_acc, out_acc,
    grads_0, grads_1, stage_a, stage_b, relay_a, relay_b, land_a, land_b, acc, chosen, cross_send,
    core_recv_0, core_sum_0, x_recv_0, x_sum_0, spot_recv_0, spot_sum_0, x_all_0,
    core_recv_1, core_sum_1, x_recv_1, x_sum_1, spot_recv_1, spot_sum_1, x_all_1,
    send1, recv1, send2, recv2, cross_sems, core_sems, x_sems, spot_sems,
):
    dom = lax.axis_index("dom")
    z, y, core, node = place()
    sources, relays, lands = (stage_a, stage_b), (relay_a, relay_b), (land_a, land_b)
    barrier = pltpu.get_barrier_semaphore()
    peers = [(dom_peer(dom, offset), node) for offset in OFFSETS]
    peers += [(dom, four(node + step)) for step in range(1, N_NODE)]
    for peer in peers:
        pl.semaphore_signal(barrier, inc=1, device_id=peer, device_id_type=MESH)

    scale = 1.0 / math.sqrt(D // HEADS)
    log2e = math.log2(math.e)
    expand_acc[...] = jnp.zeros(expand_acc.shape, F32)
    reduce_acc[...] = jnp.zeros(reduce_acc.shape, F32)
    out_acc[...] = jnp.zeros(out_acc.shape, F32)
    qs[...] = nn(feat_ref[...], wq_ref[...]).astype(BF16)
    lane_head = lax.broadcasted_iota(jnp.int32, (1, D), 1) // (D // HEADS)
    head_f32 = [(lane_head == h).astype(F32) for h in range(HEADS)]
    head_low = [mask.astype(BF16) for mask in head_f32]

    def forward_row(row, carry):
        start = pl.multiple_of(row * BLK, BLK)
        fs[row, 0:BLK] = feat_ref[pl.ds(start, BLK), :]
        for tile in range(NEAR - 1):
            block = local_ref[tile, row]
            for chunk, part_ref in enumerate((part_0, part_1)):
                top = (tile + 1) * BLK + chunk * 2 * SPAN
                fs[row, top : top + 2 * SPAN] = part_ref[block]
        for tile in range(TILES - NEAR):
            slot = slot_ref[row, tile]
            asked = slot // 2
            dz = four(z + 4 - asked // 8)
            dy = four(y + 4 - four(asked // 2))
            dc = two(core + two(asked))
            for chunk in range(CHUNKS):
                top = (NEAR + tile) * BLK + 2 * chunk * SPAN
                fs[row, top : top + SPAN] = far_a[chunk, dz, dy, dc, two(slot)]
                fs[row, top + SPAN : top + 2 * SPAN] = far_b[chunk, dy, dz, dc, two(slot)]
        tile_rows = fs[row]
        keys = nn(tile_rows, wk_ref[...]).astype(BF16)
        ks[row] = keys
        values = nn(tile_rows, wv_ref[...]).astype(BF16)
        vs[row] = values
        query = qs[pl.ds(start, BLK), :]
        bias = bias_ref[pl.ds(start, BLK), :].astype(F32)
        total = jnp.zeros((BLK, D), F32)
        for pair in range(HEADS // 2):
            both = jnp.concatenate([query * head_low[2 * pair], query * head_low[2 * pair + 1]], 0)
            scores = nt(both, keys) * (scale * log2e)
            for half in range(2):
                mine = scores[half * BLK : (half + 1) * BLK] + bias
                top = jnp.max(mine, -1, keepdims=True)
                weight = jnp.exp2(mine - top)
                norm = 1.0 / jnp.sum(weight, -1, keepdims=True)
                ps[row, (2 * pair + half) * BLK : (2 * pair + half + 1) * BLK, :] = (weight * norm).astype(BF16)
            got = nn(ps[row, 2 * pair * BLK : (2 * pair + 2) * BLK, :], values)
            total = total + got[:BLK] * head_f32[2 * pair] + got[BLK:] * head_f32[2 * pair + 1]
        mixed[pl.ds(start, BLK), :] = total
        return carry

    lax.fori_loop(0, ROWS, forward_row, 0)

    size = 256

    def feed(step, carry):
        start = pl.multiple_of(step * size, size)
        sel = pl.ds(start, size)
        mixed_low = mixed[sel, :].astype(BF16)
        gain_a = gain_a_ref[...]
        gain_f = gain_f_ref[...]
        residual = feat_ref[sel, :].astype(F32) + nn(mixed_low, wo_ref[...])
        center = residual - jnp.mean(residual, -1, keepdims=True)
        rstd_a = lax.rsqrt(jnp.mean(center * center, -1, keepdims=True) + EPSILON)
        hat_a = center * rstd_a
        first_low = (hat_a * gain_a).astype(BF16)
        pre = nn(first_low, we_ref[...])
        root = math.sqrt(2.0 / math.pi)
        square = pre * pre
        tanh = jnp.tanh(root * (pre + 0.044715 * (square * pre)))
        half = 0.5 * (1.0 + tanh)
        act_low = (pre * half).astype(BF16)
        slope = half + 0.5 * pre * (1.0 - tanh * tanh) * (root * (1.0 + 3.0 * 0.044715 * square))
        second = first_low.astype(F32) + nn(act_low, wr_ref[...])
        center = second - jnp.mean(second, -1, keepdims=True)
        rstd_f = lax.rsqrt(jnp.mean(center * center, -1, keepdims=True) + EPSILON)
        hat_f = center * rstd_f
        out_ref[sel, :] = (hat_f * gain_f).astype(BF16)
        d_hat = d_out_ref[sel, :].astype(F32) * gain_f
        d_second = rstd_f * (
            d_hat - jnp.mean(d_hat, -1, keepdims=True) - hat_f * jnp.mean(d_hat * hat_f, -1, keepdims=True)
        )
        d_second_low = d_second.astype(BF16)
        reduce_acc[...] += tn(d_second_low, act_low)
        d_pre_low = (nt(d_second_low, wr_ref[...]) * slope).astype(BF16)
        expand_acc[...] += tn(first_low, d_pre_low)
        d_first = d_second + nt(d_pre_low, we_ref[...])
        d_hat = d_first * gain_a
        d_resid = rstd_a * (
            d_hat - jnp.mean(d_hat, -1, keepdims=True) - hat_a * jnp.mean(d_hat * hat_a, -1, keepdims=True)
        )
        base_ref[sel, :] = d_resid
        d_resid_low = d_resid.astype(BF16)
        out_acc[...] += tn(mixed_low, d_resid_low)
        d_mixed[sel, :] = nt(d_resid_low, wo_ref[...]).astype(BF16)
        return carry

    lax.fori_loop(0, ROWS * BLK // size, feed, 0)

    def pack(accs, grads):
        spot = 0
        for total in accs:
            for top in range(0, total.shape[0], D):
                for left in range(0, total.shape[1], BLK):
                    grads[spot : spot + D, :] = total[top : top + D, left : left + BLK].astype(BF16)
                    spot += D

    def push(src, dst, sems, key, target):
        copy = pltpu.make_async_remote_copy(
            src_ref=src, dst_ref=dst, send_sem=sems.at[(0,) + key], recv_sem=sems.at[(1,) + key],
            device_id=target, device_id_type=MESH,
        )
        copy.start()
        return copy

    def finish(copies):
        for copy in copies:
            copy.wait()

    spot_here = z * 4 + y
    x_line = [four(node + step) for step in range(1, 4)]
    x_line = [(other, (dom, other)) for other in x_line]
    spots = [lax.rem(spot_here + step, 16) for step in range(1, 16)]
    spots = [(other, (other * 2 + core, node)) for other in spots]
    sibling = device(z, y, two(core + 1), node)

    def reduction(number, grads, total_ref, core_recv, core_sum, x_recv, x_sum, spot_recv, spot_sum, x_all):
        core_rows = SUM_ROWS[number] // 2
        x_rows = core_rows // 4
        spot_rows = x_rows // 16
        mine = rows_at(core, core_rows)

        def scatter(members, src, dst, sems, count):
            return [
                push(src.at[rows_at(other, count)], dst.at[index], sems, (number, 0, index), target)
                for index, (other, target) in enumerate(members)
            ]

        def gather(members, own, src, dst, sems, count):
            copies = [
                push(src, dst.at[rows_at(own, count)], sems, (number, 1, index), target)
                for index, (other, target) in enumerate(members)
            ]
            dst[rows_at(own, count), :] = src[...]
            return copies

        def add_up(own, src, recv, out, count):
            total = src[rows_at(own, count), :].astype(F32)
            for index in range(recv.shape[0]):
                total = total + recv[index].astype(F32)
            out[...] = total.astype(BF16)

        copy = push(grads.at[rows_at(two(core + 1), core_rows)], core_recv, core_sems, (number, 0), sibling)
        yield
        copy.wait()
        core_sum[...] = (grads[mine, :].astype(F32) + core_recv[...].astype(F32)).astype(BF16)
        copies = scatter(x_line, core_sum, x_recv, x_sems, x_rows)
        yield
        finish(copies)
        add_up(node, core_sum, x_recv, x_sum, x_rows)
        copies = scatter(spots, x_sum, spot_recv, spot_sems, spot_rows)
        yield
        finish(copies)
        add_up(spot_here, x_sum, spot_recv, spot_sum, spot_rows)
        copies = gather(spots, spot_here, spot_sum, x_all, spot_sems, spot_rows)
        yield
        finish(copies)
        my_part = total_ref.at[mine]
        copies = gather(x_line, node, x_all, my_part, x_sems, x_rows)
        yield
        finish(copies)
        copy = push(my_part, my_part, core_sems, (number, 1), sibling)
        yield
        copy.wait()
        yield

    first_half = lax.broadcasted_iota(jnp.int32, (64, BLK), 0) < 32

    def block_diagonal(turned, pair):
        piece = turned[64 * pair : 64 * pair + 64]
        return jnp.concatenate(
            [jnp.where(first_half, piece, 0.0), jnp.where(first_half, 0.0, piece)], 1
        ).astype(BF16)

    def backward(row, begin, end):
        start = pl.multiple_of(row * BLK, BLK)
        keys = ks[row, begin:end]
        values = vs[row, begin:end]
        query = qs[pl.ds(start, BLK), :]
        grad = d_mixed[pl.ds(start, BLK), :]
        query_t = query.astype(F32).T
        grad_t = grad.astype(F32).T
        inner_full = grad.astype(F32) * mixed[pl.ds(start, BLK), :]
        query_part = jnp.zeros((BLK, D), F32)
        key_parts = []
        value_parts = []
        for pair in range(HEADS // 2):
            both = jnp.concatenate([grad * head_low[2 * pair], grad * head_low[2 * pair + 1]], 0)
            inner = jnp.concatenate(
                [
                    jnp.sum(inner_full * head_f32[2 * pair], -1, keepdims=True),
                    jnp.sum(inner_full * head_f32[2 * pair + 1], -1, keepdims=True),
                ],
                0,
            )
            probs_low = ps[row, 2 * pair * BLK : (2 * pair + 2) * BLK, begin:end]
            d_probs = nt(both, values)
            d_scores = (probs_low.astype(F32) * ((d_probs - inner) * scale)).astype(BF16)
            got = nn(d_scores, keys)
            query_part = query_part + got[:BLK] * head_f32[2 * pair] + got[BLK:] * head_f32[2 * pair + 1]
            key_parts.append(nn(block_diagonal(query_t, pair), d_scores).astype(BF16))
            value_parts.append(nn(block_diagonal(grad_t, pair), probs_low).astype(BF16))
        d_keys_t = jnp.concatenate(key_parts, 0)
        d_values_t = jnp.concatenate(value_parts, 0)
        return d_keys_t, d_values_t, nn(wk_ref[...], d_keys_t) + nn(wv_ref[...], d_values_t), query_part

    def backward_far(row, carry):
        d_keys_t, d_values_t, d_rows_t, query_part = backward(row, NEAR * BLK, KEYS)
        far_keys_t[row] = d_keys_t
        far_values_t[row] = d_values_t
        d_query[rows_at(row, BLK), :] = query_part
        for tile in range(TILES - NEAR):
            piece = d_rows_t[:, tile * BLK : (tile + 1) * BLK].T
            far_tiles[row * (TILES - NEAR) + tile] = piece.astype(BF16)
        return carry

    def backward_near(row, carry):
        d_keys_t, d_values_t, d_rows_t, query_part = backward(row, 0, NEAR * BLK)
        near_keys_t[row] = d_keys_t
        near_values_t[row] = d_values_t
        d_query[rows_at(row, BLK), :] += query_part
        for tile in range(NEAR):
            piece = d_rows_t[:, tile * BLK : (tile + 1) * BLK].T
            near_tiles[row * NEAR + tile] = piece.astype(BF16)
        return carry

    def key_grads(row, carry):
        near_rows = fs[row, : NEAR * BLK]
        far_rows = fs[row, NEAR * BLK :]
        pair_acc[0:D, :] += nn(near_keys_t[row], near_rows) + nn(far_keys_t[row], far_rows)
        pair_acc[D : 2 * D, :] += nn(near_values_t[row], near_rows) + nn(far_values_t[row], far_rows)
        return carry

    def stage(chunk):
        def body(peer, carry):
            turned = four(peer // 2) * 8 + (peer // 8) * 2 + two(peer)
            for slot in range(2):
                tile = tile_ref[0, 2 * peer + slot]
                top = 2 * chunk * SPAN
                stage_a[chunk, peer, slot] = far_tiles[tile, top : top + SPAN]
                stage_b[chunk, turned, slot] = far_tiles[tile, top + SPAN : top + 2 * SPAN]
            return carry

        lax.fori_loop(0, N_DOM, body, 0)

    block_of = lax.broadcasted_iota(jnp.int32, (256, 256), 0) // 16
    same_row = lax.rem(lax.broadcasted_iota(jnp.int32, (256, 256), 0), 16) == lax.rem(
        lax.broadcasted_iota(jnp.int32, (256, 256), 1), 16
    )
    slot_of = lax.broadcasted_iota(jnp.int32, (1, 256), 1) // 16

    def selection(values):
        names = jnp.full((1, 256), -1, jnp.int32)
        for index, value in enumerate(values):
            names = jnp.where(slot_of == index, value, names)
        return jnp.logical_and(names == block_of, same_row).astype(F32).astype(BF16)

    def relay_on(chunk):
        for half, step, copy in first[chunk]:
            copy.wait()
            second[chunk, half, step] = second_phase(chunk, half, step, sources, relays, lands, send2, recv2)
            lands[half][chunk, step, 0, 0] = relays[half][chunk, step - 1, (y, z)[half] * 2 + core]

    def combine(chunk, group):
        for half in range(2):
            finish(second[chunk, half, group])
            for top in range(0, SPAN, 16):
                rows = slice((2 * chunk + half) * SPAN + top, (2 * chunk + half) * SPAN + top + 16)
                arrived = lands[half][chunk, group, :, :, :, top : top + 16, :].reshape(256, D)
                acc[:, rows, :] += nn(chosen[half, group], arrived).reshape(PART, 16, D)

    def cross(chunk):
        rows = slice(2 * chunk * SPAN, 2 * (chunk + 1) * SPAN)
        cross_send[chunk] = acc[:, rows, :].astype(BF16)
        copies = []
        for step in range(1, N_NODE):
            other = four(node + step)
            copies.append(
                push(
                    cross_send.at[chunk, pl.ds(other * ROWS, ROWS)], cross_ref.at[step - 1, chunk],
                    cross_sems, (chunk, step - 1), (dom, other),
                )
            )
        return copies

    pack((expand_acc, reduce_acc), grads_0)
    pl.semaphore_wait(barrier, len(peers))
    wide = reduction(
        0, grads_0, sum_0, core_recv_0, core_sum_0, x_recv_0, x_sum_0, spot_recv_0, spot_sum_0, x_all_0
    )
    next(wide)
    far_tiles[FAR] = jnp.zeros((BLK, D), BF16)
    lax.fori_loop(0, 2, backward_far, 0)
    next(wide)
    lax.fori_loop(2, ROWS, backward_far, 0)

    first = []
    second = {}
    for chunk in range(CHUNKS):
        stage(chunk)
        if chunk == 0:
            next(wide)
        first.append(first_phase(chunk, sources, relays, send1, recv1))
        for half in range(2):
            second[chunk, half, 0] = second_phase(chunk, half, 0, sources, relays, lands, send2, recv2)
            lands[half][chunk, 0, 0, 0] = sources[half][chunk, (dom, y * 8 + z * 2 + core)[half]]

    near_tiles[ROWS * NEAR : PART] = jnp.zeros((PART - ROWS * NEAR, BLK, D), BF16)
    lax.fori_loop(0, ROWS, backward_near, 0)
    pair_acc[...] = jnp.zeros(pair_acc.shape, F32)
    lax.fori_loop(0, ROWS, key_grads, 0)
    d_query_low = d_query[...].astype(BF16)
    query_acc[...] = tn(feat_ref[...], d_query_low)
    pack((query_acc, pair_acc, out_acc), grads_1)
    narrow = reduction(
        1, grads_1, sum_1, core_recv_1, core_sum_1, x_recv_1, x_sum_1, spot_recv_1, spot_sum_1, x_all_1
    )
    next(narrow)
    next(wide)
    base_ref[...] += nt(d_query_low, wq_ref[...])
    next(narrow)
    relay_on(0)
    next(narrow)
    next(wide)
    near_names = []
    for row in range(ROWS):
        near_names += [node * ROWS + row, local_ref[0, row], local_ref[1, row]]
    near_chosen = selection(near_names)
    for top in range(0, BLK, 16):
        rows = slice(top, top + 16)
        acc[:, rows, :] = nn(near_chosen, near_tiles[:, rows, :].reshape(256, D)).reshape(PART, 16, D)
    for half in range(2):
        for group in range(4):
            chosen[half, group] = selection(
                [
                    wanted_ref[origin(half, group, step, flip), 0, slot]
                    for step in range(4)
                    for flip in range(2)
                    for slot in range(2)
                ]
            )
    for chunk in range(1, CHUNKS):
        relay_on(chunk)
    combine(0, 0)
    combine(0, 1)
    next(narrow)
    next(wide)
    combine(0, 2)
    combine(0, 3)
    crossing = cross(0)
    next(narrow)
    next(wide)
    for chunk in range(1, CHUNKS):
        for group in range(4):
            combine(chunk, group)
        crossing += cross(chunk)
    next(narrow)
    base_ref[...] += acc[pl.ds(node * ROWS, ROWS)].reshape(ROWS * BLK, D)
    next(narrow)
    finish(crossing)


def finish_kernel(factor, result_ref, base_ref, cross_ref, sum_0, sum_1, out_ref, dx_ref, gq, gk, gv, go, ge, gr):
    out_ref[...] = result_ref[...]
    for row in range(ROWS):
        for chunk in range(CHUNKS):
            span = slice(row * BLK + 2 * chunk * SPAN, row * BLK + 2 * (chunk + 1) * SPAN)
            total = base_ref[span, :]
            for step in range(N_NODE - 1):
                total = total + cross_ref[step, chunk, row].astype(F32)
            dx_ref[span, :] = total.astype(BF16)

    def piece(ref, index):
        return ref[index * D : (index + 1) * D, :].astype(F32) * factor

    for half in range(2):
        span = slice(half * BLK, (half + 1) * BLK)
        gq[:, span] = piece(sum_1, half)
        gk[span, :] = piece(sum_1, 2 + half).T
        gv[span, :] = piece(sum_1, 4 + half).T
        go[:, span] = piece(sum_1, 6 + half)
    for part in range(8):
        span = slice(part * BLK, (part + 1) * BLK)
        ge[:, span] = piece(sum_0, part)
        gr[span, :] = piece(sum_0, 8 + part).T


def vmem(shape, dtype):
    return pltpu.VMEM(shape, dtype)


IN_VMEM = pl.BlockSpec(memory_space=pltpu.VMEM)
IN_SMEM = pl.BlockSpec(memory_space=pltpu.SMEM)
ANYWHERE = pl.BlockSpec(memory_space=pl.ANY)


def on_device(
    features, w_query, w_key, w_value, w_out, w_expand, w_reduce, gain_attn, gain_ffn,
    tile_mask, local_block, remote_slot, remote_block, d_out,
):
    rows = features.shape[0]
    dma = pltpu.SemaphoreType.DMA
    peers = len(OFFSETS)
    land = (CHUNKS, 4, 4, 2, 2, SPAN, D)
    staged = (CHUNKS, N_DOM, 2, SPAN, D)
    relay = (CHUNKS, 3, 8, 2, SPAN, D)
    phase_sems = [dma((CHUNKS, 2, 3)), dma((CHUNKS, 2, 3)), dma((CHUNKS, 2, 4, 4, 2)), dma((CHUNKS, 2, 4, 4, 2))]
    part_0, part_1, land_a, land_b, wanted, bias, tile_of = pl.pallas_call(
        exchange_kernel,
        out_shape=(
            jax.ShapeDtypeStruct((PART, 2 * SPAN, D), BF16),
            jax.ShapeDtypeStruct((PART, 2 * SPAN, D), BF16),
            jax.ShapeDtypeStruct(land, BF16),
            jax.ShapeDtypeStruct(land, BF16),
            jax.ShapeDtypeStruct((N_DOM, 1, BLK), jnp.int32),
            jax.ShapeDtypeStruct((rows, KEYS), BF16),
            jax.ShapeDtypeStruct((1, 2 * N_DOM), jnp.int32),
        ),
        in_specs=[IN_VMEM, IN_SMEM, IN_SMEM, IN_VMEM],
        out_specs=(IN_VMEM, IN_VMEM, ANYWHERE, ANYWHERE, IN_VMEM, IN_VMEM, IN_SMEM),
        scratch_shapes=[
            vmem((N_DOM, 1, BLK), jnp.int32), vmem(staged, BF16), vmem(staged, BF16),
            vmem(relay, BF16), vmem(relay, BF16), pltpu.SMEM((N_DOM, 1, BLK), jnp.int32),
            dma((CHUNKS, N_NODE - 1)), dma((CHUNKS, N_NODE - 1)), dma((peers,)), dma((peers,)),
        ]
        + phase_sems
        + [dma((CHUNKS, 2, 4)), dma],
        compiler_params=pltpu.CompilerParams(
            collective_id=1, has_side_effects=True, vmem_limit_bytes=VMEM_LIMIT
        ),
        name="exchange",
    )(features.reshape(ROWS, BLK, D), remote_block.reshape(1, 2 * N_DOM), remote_slot, jnp.transpose(tile_mask, (1, 0, 2)))

    sum_scratch = []
    for total in SUM_ROWS:
        half, eighth, spot = total // 2, total // 8, total // 128
        sum_scratch += [
            vmem((half, BLK), BF16), vmem((half, BLK), BF16), vmem((3, eighth, BLK), BF16), vmem((eighth, BLK), BF16),
            vmem((15, spot, BLK), BF16), vmem((spot, BLK), BF16), vmem((eighth, BLK), BF16),
        ]
    result, base, cross, sum_0, sum_1 = pl.pallas_call(
        layer_kernel,
        out_shape=(
            jax.ShapeDtypeStruct((rows, D), BF16),
            jax.ShapeDtypeStruct((rows, D), F32),
            jax.ShapeDtypeStruct((N_NODE - 1, CHUNKS, ROWS, 2 * SPAN, D), BF16),
            jax.ShapeDtypeStruct((SUM_ROWS[0], BLK), BF16),
            jax.ShapeDtypeStruct((SUM_ROWS[1], BLK), BF16),
        ),
        in_specs=[IN_SMEM] * 4 + [IN_VMEM] * 15,
        out_specs=(IN_VMEM,) * 5,
        scratch_shapes=[
            vmem((ROWS, KEYS, D), BF16), vmem((ROWS, KEYS, D), BF16), vmem((ROWS, KEYS, D), BF16),
            vmem((rows, D), BF16), vmem((ROWS, HEADS * BLK, KEYS), BF16), vmem((rows, D), F32),
            vmem((rows, D), BF16), vmem((rows, D), F32),
            vmem((ROWS, D, KEYS - NEAR * BLK), BF16), vmem((ROWS, D, KEYS - NEAR * BLK), BF16),
            vmem((ROWS, D, NEAR * BLK), BF16), vmem((ROWS, D, NEAR * BLK), BF16),
            vmem((FAR + 1, BLK, D), BF16), vmem((PART, BLK, D), BF16),
            vmem((2 * D, D), F32), vmem((D, D), F32), vmem((D, 4 * D), F32), vmem((D, 4 * D), F32), vmem((D, D), F32),
            vmem((SUM_ROWS[0], BLK), BF16), vmem((SUM_ROWS[1], BLK), BF16), vmem(staged, BF16), vmem(staged, BF16),
            vmem(relay, BF16), vmem(relay, BF16), vmem(land, BF16), vmem(land, BF16),
            vmem((PART, BLK, D), F32), vmem((2, 4, 256, 256), BF16), vmem((CHUNKS, PART, 2 * SPAN, D), BF16),
        ]
        + sum_scratch
        + phase_sems
        + [dma((2, CHUNKS, 3)), dma((2, 2, 2)), dma((2, 2, 2, 3)), dma((2, 2, 2, 15))],
        compiler_params=pltpu.CompilerParams(
            collective_id=2, has_side_effects=True, vmem_limit_bytes=VMEM_LIMIT
        ),
        name="layer",
    )(
        local_block.T, remote_slot, tile_of, wanted, features, part_0, part_1, land_a, land_b, bias, d_out,
        w_query, w_key, w_value, w_out, w_expand, w_reduce, gain_attn.reshape(1, D), gain_ffn.reshape(1, D),
    )

    factor = 1.0 / math.sqrt(rows * N_DOM * N_NODE)
    return pl.pallas_call(
        functools.partial(finish_kernel, factor),
        out_shape=(
            jax.ShapeDtypeStruct((rows, D), BF16),
            jax.ShapeDtypeStruct((rows, D), BF16),
            jax.ShapeDtypeStruct((D, D), F32),
            jax.ShapeDtypeStruct((D, D), F32),
            jax.ShapeDtypeStruct((D, D), F32),
            jax.ShapeDtypeStruct((D, D), F32),
            jax.ShapeDtypeStruct((D, 4 * D), F32),
            jax.ShapeDtypeStruct((4 * D, D), F32),
        ),
        in_specs=[IN_VMEM] * 5,
        out_specs=(IN_VMEM,) * 8,
        compiler_params=pltpu.CompilerParams(vmem_limit_bytes=VMEM_LIMIT),
        name="finish",
    )(result, base, cross, sum_0, sum_1)


def solution(mesh):
    split = P(("dom", "node"), None)
    placed = (
        (split,) + (P(),) * 8 + (P(("dom", "node"), None, None), split, split, P("dom", "node", None), split)
    )
    return jax.shard_map(
        on_device, mesh=mesh, in_specs=placed, out_specs=(split, split) + (P(),) * 6, check_vma=False
    )
```

time: 194 us -> 174 us (0.90)
  Pallas kernels: 193 us -> 173 us
    pallas_call x1 -> x0, Pallas kernels: 85.4 us -> none  [on_device(): pl.pallas_call(return_kernel, out_shape=(jax.ShapeDtypeStruct((ROWS, BLK,...]
    pallas_call x1, Pallas kernels: 32.9 us -> 99 us  [on_device(): pl.pallas_call(layer_kernel, out_shape=(jax.ShapeDtypeStruct((rows, D), B...]
where the time goes in v3:
time: 174 us
  Pallas kernels  173 us (99%)
    pallas_call x1, Pallas kernels, on_device(): pl.pallas_call(layer_kernel, out_shape=(jax.ShapeDtypeStruct((rows, D), B...  99 us
    pallas_call x1, Pallas kernels, on_device(): pl.pallas_call(exchange_kernel, out_shape=(jax.ShapeDtypeStruct((PART, 2...  70.2 us
    pallas_call x1, Pallas kernels, on_device(): pl.pallas_call(functools.partial(finish_kernel, factor), out_shape=(jax.S...  4.06 us

profile of v3, /device:TPU:0, one launch (start us, length us, event | category | flops | bytes accessed | tf_op | source)
XLA Modules:
  0.0 174.0 jit_solution(14677226084446109485)
XLA Ops:
  0.6 70.2 %exchange.1 = (bf16[16,64,256]{2,1,0:T(8,128)(2,1)}, bf16[16,64,256]{2,1,0:T(8,128)(2,1)}, bf16[2,4,4,2,2,32,256]{6,5,4,3,2,1,0:T(8,128)(2,1)}, bf16[2,4,4,2,2,3...) custom-call(bf16[4,128,256]{2,1,0:T(8,128)(2,1)} %bitcast.7, ...), custom_call_target="tpu_custom_call" | custom-call | tf_op jit(solution)/shard_map/exchange/pallas_call | solution.py:702
  70.8 99.0 %layer.1 = (bf16[512,256]{1,0:T(8,128)(2,1)}, f32[512,256]{1,0:T(8,128)}, bf16[3,2,4,64,256]{4,3,2,1,0:T(8,128)(2,1)}, bf16[4096,128]{1,0:T(8,128)(2,1)}, bf16[2048,128]{1,0:T(8,128)(2,1)}) custom-call(s32[2,4]{1,0:T(2,128)} %bitcast.8, s32[4,4]{1,0:T(4,128)} %slot_ref.3, s32[1,64]{1,0:T(1,128)} %get-tuple-element.20.tile_ref, ...), custom_call_target="tpu_custom_call" | custom-call | tf_op jit(solution)/shard_map/layer/pallas_call | solution.py:735
  169.9 4.1 %finish.1 = (bf16[512,256]{1,0:T(8,128)(2,1)}, bf16[512,256]{1,0:T(8,128)(2,1)}, f32[256,256]{1,0:T(8,128)}, f32[256,256]{1,0:T(8,128)}, f32[256,256]{1,0:T(8,12...) custom-call(bf16[512,256]{1,0:T(8,128)(2,1)} %get-tuple-element.27.result_ref, ...), custom_call_target="tpu_custom_call" | custom-call | tf_op jit(solution)/shard_map/finish/pallas_call | solution.py:771

commit v4 on v3

--- a/solution.py
+++ b/solution.py
@@ -133,92 +133,139 @@
     return four(z + near) * 8 + four(y + far) * 2 + two(core + flip)
 
 
+def dom_at(half, along, across, side):
+    first, other = ((along, across), (across, along))[half]
+    return first * 8 + other * 2 + side
+
+
 def exchange_kernel(
-    feat_ref, table_ref, slot_ref, mask_ref, part_0, part_1, land_a, land_b, wanted_ref, bias_ref, tile_ref,
-    ids, stage_a, stage_b, relay_a, relay_b, ids_smem,
-    near_send, near_recv, id_send, id_recv, send1, recv1, send2, recv2, own_sem, local_sem,
+    feat_ref, table_ref, slot_ref, mask_ref,
+    part_0, part_a, part_b, land_a, land_b, wanted_ref, bias_ref, tile_ref,
+    row_ref, stage_a, stage_b, relay_a, relay_b, ids_smem, held_a1, held_a2, held_a3, held_b1, held_b2, held_b3,
+    near_send, near_recv, id_send, id_recv, send1, recv1, send2, recv2, line_send, line_recv, x_send, x_recv,
+    own_sem, local_sem,
 ):
     dom = lax.axis_index("dom")
     z, y, core, node = place()
+    axis = (z, y)
     stages, relays, lands = (stage_a, stage_b), (relay_a, relay_b), (land_a, land_b)
-    parts = (part_0, part_1)
+    held = ((part_a, held_a1, held_a2, held_a3), (part_b, held_b1, held_b2, held_b3))
     barrier = pltpu.get_barrier_semaphore()
     for offset in OFFSETS:
         pl.semaphore_signal(barrier, inc=1, device_id=(dom_peer(dom, offset), node), device_id_type=MESH)
-    for step in range(1, N_NODE):
-        pl.semaphore_signal(
-            barrier, inc=1, device_id=(dom, lax.rem(node + step, N_NODE)), device_id_type=MESH
-        )
-    lane = lax.broadcasted_iota(jnp.int32, (1, BLK), 1)
-    for peer in range(N_DOM):
-        ids[peer] = jnp.where(
-            lane == 0, table_ref[0, 2 * peer], jnp.where(lane == 1, table_ref[0, 2 * peer + 1], 0)
-        )
+    x_line = [(dom, four(node + step)) for step in range(1, N_NODE)]
+    for target in x_line:
+        pl.semaphore_signal(barrier, inc=1, device_id=target, device_id_type=MESH)
+    row_ref[:, 0 : 2 * N_DOM] = table_ref[...]
+    mine = pl.ds(node * ROWS, ROWS)
+    part_0[mine] = feat_ref[:, 0 : 2 * SPAN]
+    for half in range(2):
+        held[half][0][mine] = feat_ref[:, (2 + half) * SPAN : (3 + half) * SPAN]
     pl.semaphore_wait(barrier, len(OFFSETS) + N_NODE - 1)
 
-    id_copies = []
-    for index, offset in enumerate(OFFSETS):
-        peer = dom_peer(dom, offset)
+    def push(src, dst, send, recv, target):
         copy = pltpu.make_async_remote_copy(
-            src_ref=ids.at[peer], dst_ref=wanted_ref.at[dom],
-            send_sem=id_send.at[index], recv_sem=id_recv.at[index],
-            device_id=(peer, node), device_id_type=MESH,
+            src_ref=src, dst_ref=dst, send_sem=send, recv_sem=recv, device_id=target, device_id_type=MESH
         )
         copy.start()
-        id_copies.append(copy)
-    near_copies = []
-    for chunk in range(CHUNKS):
-        for step in range(1, N_NODE):
-            copy = pltpu.make_async_remote_copy(
-                src_ref=feat_ref.at[:, pl.ds(chunk * 2 * SPAN, 2 * SPAN)],
-                dst_ref=parts[chunk].at[pl.ds(node * ROWS, ROWS)],
-                send_sem=near_send.at[chunk, step - 1], recv_sem=near_recv.at[chunk, step - 1],
-                device_id=(dom, lax.rem(node + step, N_NODE)), device_id_type=MESH,
+        return copy
+
+    id_copies = [
+        push(row_ref, wanted_ref.at[dom], id_send.at[index], id_recv.at[index], (dom_peer(dom, offset), node))
+        for index, offset in enumerate(OFFSETS)
+    ]
+    near_copies = [
+        push(
+            feat_ref.at[:, pl.ds(0, 2 * SPAN)], part_0.at[mine], near_send.at[index], near_recv.at[index], target
+        )
+        for index, target in enumerate(x_line)
+    ]
+    line_copies = []
+    for step in range(1, 4):
+        for half in range(2):
+            target = (device(four(z + step), y, core, node), device(z, four(y + step), core, node))[half]
+            copy = push(
+                feat_ref.at[:, pl.ds((2 + half) * SPAN, SPAN)], held[half][step].at[mine],
+                line_send.at[half, step - 1], line_recv.at[half, step - 1], target,
             )
-            copy.start()
-            near_copies.append(copy)
-    for chunk in range(CHUNKS):
-        parts[chunk][pl.ds(node * ROWS, ROWS)] = feat_ref[:, chunk * 2 * SPAN : (chunk + 1) * 2 * SPAN]
-    wanted_ref[dom] = ids[dom]
+            line_copies.append((half, step, copy))
+    x_copies = {}
+
+    def spread(half, group):
+        if group == 0:
+            source = feat_ref.at[:, pl.ds((2 + half) * SPAN, SPAN)]
+        else:
+            source = held[half][group].at[mine]
+        x_copies[half, group] = [
+            push(
+                source, held[half][group].at[mine],
+                x_send.at[half, group, index], x_recv.at[half, group, index], target,
+            )
+            for index, target in enumerate(x_line)
+        ]
+
+    for half in range(2):
+        spread(half, 0)
+    wanted_ref[dom] = row_ref[...]
     for copy in id_copies:
         copy.wait()
     to_smem = pltpu.make_async_copy(wanted_ref, ids_smem, local_sem)
     to_smem.start()
     to_smem.wait()
 
-    def stage(chunk):
-        def body(peer, carry):
-            turned = lax.rem(peer // 2, 4) * 8 + (peer // 8) * 2 + lax.rem(peer, 2)
+    def stage(peer, carry):
+        turned = four(peer // 2) * 8 + (peer // 8) * 2 + two(peer)
+        for slot in range(2):
+            block = ids_smem[peer, 0, 2 * dom + slot]
+            stage_a[0, peer, slot] = part_0[block, 0:SPAN]
+            stage_b[0, turned, slot] = part_0[block, SPAN : 2 * SPAN]
+        return carry
+
+    def pick(half, group):
+        owner = dom_at(half, four(axis[half] + 4 - group), axis[1 - half], core)
+
+        def body(index, carry):
+            asker = dom_at(half, axis[half], index // 2, two(index))
             for slot in range(2):
-                block = ids_smem[peer, 0, slot]
-                stage_a[chunk, peer, slot] = parts[chunk][block, 0:SPAN]
-                stage_b[chunk, turned, slot] = parts[chunk][block, SPAN : 2 * SPAN]
+                block = ids_smem[asker, 0, 2 * owner + slot]
+                rows = held[half][group][block]
+                if group == 0:
+                    stages[half][1, axis[half] * 8 + index, slot] = rows
+                else:
+                    relays[half][1, group - 1, index, slot] = rows
             return carry
 
-        lax.fori_loop(0, N_DOM, body, 0)
-
-    def keep(chunk, half, group):
+        lax.fori_loop(0, 8, body, 0)
+
+    second = []
+    kept = []
+
+    def deliver(chunk, half, group):
+        second.extend(second_phase(chunk, half, group, stages, relays, lands, send2, recv2))
         if group == 0:
-            source = stages[half].at[chunk, (dom, y * 8 + z * 2 + core)[half]]
+            source = stages[half].at[chunk, axis[half] * 8 + axis[1 - half] * 2 + core]
         else:
-            source = relays[half].at[chunk, group - 1, (y, z)[half] * 2 + core]
+            source = relays[half].at[chunk, group - 1, axis[1 - half] * 2 + core]
         copy = pltpu.make_async_copy(
             source, lands[half].at[chunk, group, 0, 0], own_sem.at[chunk, half, group]
         )
         copy.start()
-        return copy
-
-    first = []
-    second = []
-    kept = []
-    for chunk in range(CHUNKS):
-        for copy in near_copies[chunk * (N_NODE - 1) : (chunk + 1) * (N_NODE - 1)]:
+        kept.append(copy)
+
+    for copy in near_copies:
+        copy.wait()
+    lax.fori_loop(0, N_DOM, stage, 0)
+    first = first_phase(0, stages, relays, send1, recv1)
+    for half in range(2):
+        deliver(0, half, 0)
+    for half, step, copy in line_copies:
+        copy.wait()
+        spread(half, step)
+    for half in range(2):
+        for copy in x_copies[half, 0]:
             copy.wait()
-        stage(chunk)
-        first.append(first_phase(chunk, stages, relays, send1, recv1))
-        for half in range(2):
-            second += second_phase(chunk, half, 0, stages, relays, lands, send2, recv2)
-            kept.append(keep(chunk, half, 0))
+        pick(half, 0)
+        deliver(1, half, 0)
 
     def to_bias(row, carry):
         start = pl.multiple_of(row * BLK, BLK)
@@ -245,11 +292,15 @@
         return carry
 
     lax.fori_loop(0, 2 * N_DOM, tile_of, 0)
-    for chunk in range(CHUNKS):
-        for half, step, copy in first[chunk]:
-            copy.wait()
-            second += second_phase(chunk, half, step, stages, relays, lands, send2, recv2)
-            kept.append(keep(chunk, half, step))
+    for half, step, copy in first:
+        copy.wait()
+        deliver(0, half, step)
+    for group in range(1, 4):
+        for half in range(2):
+            for copy in x_copies[half, group]:
+                copy.wait()
+            pick(half, group)
+            deliver(1, half, group)
     for copy in kept:
         copy.wait()
     for copy in second:
@@ -264,7 +315,7 @@
 
 
 def layer_kernel(
-    local_ref, slot_ref, tile_ref, wanted_ref, feat_ref, part_0, part_1, far_a, far_b, bias_ref, d_out_ref,
+    local_ref, slot_ref, tile_ref, wanted_ref, feat_ref, part_0, part_a, part_b, far_a, far_b, bias_ref, d_out_ref,
     wq_ref, wk_ref, wv_ref, wo_ref, we_ref, wr_ref, gain_a_ref, gain_f_ref,
     out_ref, base_ref, cross_ref, sum_0, sum_1,
     fs, ks, vs, qs, ps, mixed, d_mixed, d_query, far_keys_t, far_values_t, near_keys_t, near_values_t,
@@ -298,9 +349,10 @@
         fs[row, 0:BLK] = feat_ref[pl.ds(start, BLK), :]
         for tile in range(NEAR - 1):
             block = local_ref[tile, row]
-            for chunk, part_ref in enumerate((part_0, part_1)):
-                top = (tile + 1) * BLK + chunk * 2 * SPAN
-                fs[row, top : top + 2 * SPAN] = part_ref[block]
+            top = (tile + 1) * BLK
+            fs[row, top : top + 2 * SPAN] = part_0[block]
+            fs[row, top + 2 * SPAN : top + 3 * SPAN] = part_a[block]
+            fs[row, top + 3 * SPAN : top + 4 * SPAN] = part_b[block]
         for tile in range(TILES - NEAR):
             slot = slot_ref[row, tile]
             asked = slot // 2
@@ -627,7 +679,7 @@
         for group in range(4):
             chosen[half, group] = selection(
                 [
-                    wanted_ref[origin(half, group, step, flip), 0, slot]
+                    wanted_ref[origin(half, group, step, flip), 0, 2 * dom + slot]
                     for step in range(4)
                     for flip in range(2)
                     for slot in range(2)
@@ -699,26 +751,28 @@
     staged = (CHUNKS, N_DOM, 2, SPAN, D)
     relay = (CHUNKS, 3, 8, 2, SPAN, D)
     phase_sems = [dma((CHUNKS, 2, 3)), dma((CHUNKS, 2, 3)), dma((CHUNKS, 2, 4, 4, 2)), dma((CHUNKS, 2, 4, 4, 2))]
-    part_0, part_1, land_a, land_b, wanted, bias, tile_of = pl.pallas_call(
+    part_0, part_a, part_b, land_a, land_b, wanted, bias, tile_of = pl.pallas_call(
         exchange_kernel,
         out_shape=(
             jax.ShapeDtypeStruct((PART, 2 * SPAN, D), BF16),
-            jax.ShapeDtypeStruct((PART, 2 * SPAN, D), BF16),
+            jax.ShapeDtypeStruct((PART, SPAN, D), BF16),
+            jax.ShapeDtypeStruct((PART, SPAN, D), BF16),
             jax.ShapeDtypeStruct(land, BF16),
             jax.ShapeDtypeStruct(land, BF16),
             jax.ShapeDtypeStruct((N_DOM, 1, BLK), jnp.int32),
             jax.ShapeDtypeStruct((rows, KEYS), BF16),
             jax.ShapeDtypeStruct((1, 2 * N_DOM), jnp.int32),
         ),
-        in_specs=[IN_VMEM, IN_SMEM, IN_SMEM, IN_VMEM],
-        out_specs=(IN_VMEM, IN_VMEM, ANYWHERE, ANYWHERE, IN_VMEM, IN_VMEM, IN_SMEM),
+        in_specs=[IN_VMEM, IN_VMEM, IN_SMEM, IN_VMEM],
+        out_specs=(IN_VMEM, IN_VMEM, IN_VMEM, ANYWHERE, ANYWHERE, IN_VMEM, IN_VMEM, IN_SMEM),
         scratch_shapes=[
-            vmem((N_DOM, 1, BLK), jnp.int32), vmem(staged, BF16), vmem(staged, BF16),
+            vmem((1, BLK), jnp.int32), vmem(staged, BF16), vmem(staged, BF16),
             vmem(relay, BF16), vmem(relay, BF16), pltpu.SMEM((N_DOM, 1, BLK), jnp.int32),
-            dma((CHUNKS, N_NODE - 1)), dma((CHUNKS, N_NODE - 1)), dma((peers,)), dma((peers,)),
         ]
+        + [vmem((PART, SPAN, D), BF16)] * 6
+        + [dma((N_NODE - 1,)), dma((N_NODE - 1,)), dma((peers,)), dma((peers,))]
         + phase_sems
-        + [dma((CHUNKS, 2, 4)), dma],
+        + [dma((2, 3)), dma((2, 3)), dma((2, 4, 3)), dma((2, 4, 3)), dma((CHUNKS, 2, 4)), dma],
         compiler_params=pltpu.CompilerParams(
             collective_id=1, has_side_effects=True, vmem_limit_bytes=VMEM_LIMIT
         ),
@@ -741,7 +795,7 @@
             jax.ShapeDtypeStruct((SUM_ROWS[0], BLK), BF16),
             jax.ShapeDtypeStruct((SUM_ROWS[1], BLK), BF16),
         ),
-        in_specs=[IN_SMEM] * 4 + [IN_VMEM] * 15,
+        in_specs=[IN_SMEM] * 4 + [IN_VMEM] * 16,
         out_specs=(IN_VMEM,) * 5,
         scratch_shapes=[
             vmem((ROWS, KEYS, D), BF16), vmem((ROWS, KEYS, D), BF16), vmem((ROWS, KEYS, D), BF16),
@@ -763,7 +817,7 @@
         ),
         name="layer",
     )(
-        local_block.T, remote_slot, tile_of, wanted, features, part_0, part_1, land_a, land_b, bias, d_out,
+        local_block.T, remote_slot, tile_of, wanted, features, part_0, part_a, part_b, land_a, land_b, bias, d_out,
         w_query, w_key, w_value, w_out, w_expand, w_reduce, gain_attn.reshape(1, D), gain_ffn.reshape(1, D),
     )
 

time: 174 us -> 163 us (0.937)
  Pallas kernels: 173 us -> 163 us
    pallas_call x1, Pallas kernels: 70.2 us -> 59.5 us  [on_device(): pl.pallas_call(exchange_kernel, out_shape=(jax.ShapeDtypeStruct((PART, 2...]
where the time goes in v4:
time: 163 us
  Pallas kernels  163 us (100%)
    pallas_call x1, Pallas kernels, on_device(): pl.pallas_call(layer_kernel, out_shape=(jax.ShapeDtypeStruct((rows, D), B...  99 us
    pallas_call x1, Pallas kernels, on_device(): pl.pallas_call(exchange_kernel, out_shape=(jax.ShapeDtypeStruct((PART, 2...  59.5 us
    pallas_call x1, Pallas kernels, on_device(): pl.pallas_call(functools.partial(finish_kernel, factor), out_shape=(jax.S...  4.06 us

profile of v4, /device:TPU:0, one launch (start us, length us, event | category | flops | bytes accessed | tf_op | source)
XLA Modules:
  0.0 163.3 jit_solution(7557967619847508517)
XLA Ops:
  0.6 59.5 %exchange.1 = (bf16[16,64,256]{2,1,0:T(8,128)(2,1)}, bf16[16,32,256]{2,1,0:T(8,128)(2,1)}, bf16[16,32,256]{2,1,0:T(8,128)(2,1)}, bf16[2,4,4,2,2,32,256]{6,5,4,3,...) custom-call(bf16[4,128,256]{2,1,0:T(8,128)(2,1)} %bitcast.7, ...), custom_call_target="tpu_custom_call" | custom-call | tf_op jit(solution)/shard_map/exchange/pallas_call | solution.py:754
  60.2 99.0 %layer.1 = (bf16[512,256]{1,0:T(8,128)(2,1)}, f32[512,256]{1,0:T(8,128)}, bf16[3,2,4,64,256]{4,3,2,1,0:T(8,128)(2,1)}, bf16[4096,128]{1,0:T(8,128)(2,1)}, bf16[2048,128]{1,0:T(8,128)(2,1)}) custom-call(s32[2,4]{1,0:T(2,128)} %bitcast.8, s32[4,4]{1,0:T(4,128)} %slot_ref.3, s32[1,64]{1,0:T(1,128)} %get-tuple-element.21.tile_ref, ...), custom_call_target="tpu_custom_call" | custom-call | tf_op jit(solution)/shard_map/layer/pallas_call | solution.py:789
  159.2 4.1 %finish.1 = (bf16[512,256]{1,0:T(8,128)(2,1)}, bf16[512,256]{1,0:T(8,128)(2,1)}, f32[256,256]{1,0:T(8,128)}, f32[256,256]{1,0:T(8,128)}, f32[256,256]{1,0:T(8,12...) custom-call(bf16[512,256]{1,0:T(8,128)(2,1)} %get-tuple-element.29.result_ref, ...), custom_call_target="tpu_custom_call" | custom-call | tf_op jit(solution)/shard_map/finish/pallas_call | solution.py:825

commit v5 on v4

--- a/solution.py
+++ b/solution.py
@@ -14,7 +14,7 @@
 F32 = jnp.float32
 BF16 = jnp.bfloat16
 NEG = -1e30
-VMEM_LIMIT = 60 << 20
+VMEM_LIMIT = 62 << 20
 
 D = 256
 BLK = 128
@@ -320,14 +320,17 @@
     out_ref, base_ref, cross_ref, sum_0, sum_1,
     fs, ks, vs, qs, ps, mixed, d_mixed, d_query, far_keys_t, far_values_t, near_keys_t, near_values_t,
     far_tiles, near_tiles, pair_acc, query_acc, expand_acc, reduce_acc, out_acc,
-    grads_0, grads_1, stage_a, stage_b, relay_a, relay_b, land_a, land_b, acc, chosen, cross_send,
+    grads_0, grads_1, stage_a, stage_b, relay_a, relay_b, land_a, land_b, acc, near_acc, chosen, cross_send,
+    plane_a, plane_b, plane_land, line_send, line_land, axis_send, axis_land, axis_own,
     core_recv_0, core_sum_0, x_recv_0, x_sum_0, spot_recv_0, spot_sum_0, x_all_0,
     core_recv_1, core_sum_1, x_recv_1, x_sum_1, spot_recv_1, spot_sum_1, x_all_1,
-    send1, recv1, send2, recv2, cross_sems, core_sems, x_sems, spot_sems,
+    send1, recv1, send2, recv2, plane_sems, line_sems, axis_sems, cross_sems, core_sems, x_sems, spot_sems,
 ):
     dom = lax.axis_index("dom")
     z, y, core, node = place()
+    axis = (z, y)
     sources, relays, lands = (stage_a, stage_b), (relay_a, relay_b), (land_a, land_b)
+    planes = (plane_a, plane_b)
     barrier = pltpu.get_barrier_semaphore()
     peers = [(dom_peer(dom, offset), node) for offset in OFFSETS]
     peers += [(dom, four(node + step)) for step in range(1, N_NODE)]
@@ -577,17 +580,92 @@
         pair_acc[D : 2 * D, :] += nn(near_values_t[row], near_rows) + nn(far_values_t[row], far_rows)
         return carry
 
-    def stage(chunk):
-        def body(peer, carry):
-            turned = four(peer // 2) * 8 + (peer // 8) * 2 + two(peer)
-            for slot in range(2):
-                tile = tile_ref[0, 2 * peer + slot]
-                top = 2 * chunk * SPAN
-                stage_a[chunk, peer, slot] = far_tiles[tile, top : top + SPAN]
-                stage_b[chunk, turned, slot] = far_tiles[tile, top + SPAN : top + 2 * SPAN]
-            return carry
-
-        lax.fori_loop(0, N_DOM, body, 0)
+    def stage_early(peer, carry):
+        peer_z, peer_y, side = peer // 8, four(peer // 2), two(peer)
+        for slot in range(2):
+            tile = tile_ref[0, 2 * peer + slot]
+            plane_a[peer_y * 2 + side, peer_z, slot] = far_tiles[tile, 2 * SPAN : 3 * SPAN]
+            plane_b[peer_z * 2 + side, peer_y, slot] = far_tiles[tile, 3 * SPAN : 4 * SPAN]
+        return carry
+
+    def stage_late(peer, carry):
+        turned = four(peer // 2) * 8 + (peer // 8) * 2 + two(peer)
+        for slot in range(2):
+            tile = tile_ref[0, 2 * peer + slot]
+            stage_a[0, peer, slot] = far_tiles[tile, 0:SPAN]
+            stage_b[0, turned, slot] = far_tiles[tile, SPAN : 2 * SPAN]
+        return carry
+
+    def send_early(half):
+        copies = []
+        for step in range(4):
+            for flip in range(2):
+                target = four(axis[1 - half] + step)
+                side = two(core + flip)
+                if step == 0 and flip == 0:
+                    plane_land[half, 0, 0] = planes[half][target * 2 + side]
+                    continue
+                copies.append(
+                    push(
+                        planes[half].at[target * 2 + side], plane_land.at[half, step, flip],
+                        plane_sems, (half, step, flip), (dom_at(half, axis[half], target, side), node),
+                    )
+                )
+        return copies
+
+    def sum_early(half):
+        finish(early[half])
+        for ahead in range(4):
+            place_there = four(axis[half] + ahead)
+            owner = dom_at(half, place_there, axis[1 - half], core)
+            names = []
+            for step in range(4):
+                for flip in range(2):
+                    asker = dom_at(half, axis[half], four(axis[1 - half] + 4 - step), two(core + flip))
+                    names += [wanted_ref[asker, 0, 2 * owner + slot] for slot in range(2)]
+            chosen[half, ahead] = selection(names)
+            for top in range(0, SPAN, 16):
+                arrived = plane_land[half, :, :, place_there, :, top : top + 16, :].reshape(256, D)
+                total = nn(chosen[half, ahead], arrived).reshape(PART, 16, D)
+                if ahead == 0:
+                    total = total + near_acc[:, half * SPAN + top : half * SPAN + top + 16, :]
+                line_send[half, ahead, :, top : top + 16, :] = total.astype(BF16)
+        return [
+            push(
+                line_send.at[half, :, pl.ds(other * ROWS, ROWS)], line_land.at[half, index],
+                line_sems, (half, index), target,
+            )
+            for index, (other, target) in enumerate(x_line)
+        ]
+
+    def turn_early(half):
+        finish(lined[half])
+        copies = []
+        for ahead in range(4):
+            total = line_send[half, ahead, pl.ds(node * ROWS, ROWS)].astype(F32)
+            for index in range(3):
+                total = total + line_land[half, index, ahead].astype(F32)
+            if ahead == 0:
+                axis_own[half] = total
+            else:
+                axis_send[half, ahead - 1] = total.astype(BF16)
+                there = four(axis[half] + ahead)
+                copies.append(
+                    push(
+                        axis_send.at[half, ahead - 1], axis_land.at[half, ahead - 1],
+                        axis_sems, (half, ahead - 1), (dom_at(half, there, axis[1 - half], core), node),
+                    )
+                )
+        return copies
+
+    def end_early(half):
+        finish(turned_copies[half])
+        for row in range(ROWS):
+            total = axis_own[half, row]
+            for index in range(3):
+                total = total + axis_land[half, index, row].astype(F32)
+            top = row * BLK + (2 + half) * SPAN
+            base_ref[top : top + SPAN, :] += total
 
     block_of = lax.broadcasted_iota(jnp.int32, (256, 256), 0) // 16
     same_row = lax.rem(lax.broadcasted_iota(jnp.int32, (256, 256), 0), 16) == lax.rem(
@@ -601,30 +679,36 @@
             names = jnp.where(slot_of == index, value, names)
         return jnp.logical_and(names == block_of, same_row).astype(F32).astype(BF16)
 
-    def relay_on(chunk):
-        for half, step, copy in first[chunk]:
+    def relay_on(arrivals):
+        for half, step, copy in arrivals:
             copy.wait()
-            second[chunk, half, step] = second_phase(chunk, half, step, sources, relays, lands, send2, recv2)
-            lands[half][chunk, step, 0, 0] = relays[half][chunk, step - 1, (y, z)[half] * 2 + core]
-
-    def combine(chunk, group):
+            second[half, step] = second_phase(0, half, step, sources, relays, lands, send2, recv2)
+            lands[half][0, step, 0, 0] = relays[half][0, step - 1, (y, z)[half] * 2 + core]
+
+    def combine(group):
         for half in range(2):
-            finish(second[chunk, half, group])
+            finish(second[half, group])
+            names = [
+                wanted_ref[origin(half, group, step, flip), 0, 2 * dom + slot]
+                for step in range(4)
+                for flip in range(2)
+                for slot in range(2)
+            ]
+            chosen[half, group] = selection(names)
             for top in range(0, SPAN, 16):
-                rows = slice((2 * chunk + half) * SPAN + top, (2 * chunk + half) * SPAN + top + 16)
-                arrived = lands[half][chunk, group, :, :, :, top : top + 16, :].reshape(256, D)
+                rows = slice(half * SPAN + top, half * SPAN + top + 16)
+                arrived = lands[half][0, group, :, :, :, top : top + 16, :].reshape(256, D)
                 acc[:, rows, :] += nn(chosen[half, group], arrived).reshape(PART, 16, D)
 
-    def cross(chunk):
-        rows = slice(2 * chunk * SPAN, 2 * (chunk + 1) * SPAN)
-        cross_send[chunk] = acc[:, rows, :].astype(BF16)
+    def cross():
+        cross_send[...] = acc[...].astype(BF16)
         copies = []
         for step in range(1, N_NODE):
             other = four(node + step)
             copies.append(
                 push(
-                    cross_send.at[chunk, pl.ds(other * ROWS, ROWS)], cross_ref.at[step - 1, chunk],
-                    cross_sems, (chunk, step - 1), (dom, other),
+                    cross_send.at[pl.ds(other * ROWS, ROWS)], cross_ref.at[step - 1],
+                    cross_sems, (step - 1,), (dom, other),
                 )
             )
         return copies
@@ -640,16 +724,15 @@
     next(wide)
     lax.fori_loop(2, ROWS, backward_far, 0)
 
-    first = []
+    lax.fori_loop(0, N_DOM, stage_early, 0)
+    early = [send_early(half) for half in range(2)]
+    next(wide)
+    lax.fori_loop(0, N_DOM, stage_late, 0)
+    first = first_phase(0, sources, relays, send1, recv1)
     second = {}
-    for chunk in range(CHUNKS):
-        stage(chunk)
-        if chunk == 0:
-            next(wide)
-        first.append(first_phase(chunk, sources, relays, send1, recv1))
-        for half in range(2):
-            second[chunk, half, 0] = second_phase(chunk, half, 0, sources, relays, lands, send2, recv2)
-            lands[half][chunk, 0, 0, 0] = sources[half][chunk, (dom, y * 8 + z * 2 + core)[half]]
+    for half in range(2):
+        second[half, 0] = second_phase(0, half, 0, sources, relays, lands, send2, recv2)
+        lands[half][0, 0, 0, 0] = sources[half][0, (dom, y * 8 + z * 2 + core)[half]]
 
     near_tiles[ROWS * NEAR : PART] = jnp.zeros((PART - ROWS * NEAR, BLK, D), BF16)
     lax.fori_loop(0, ROWS, backward_near, 0)
@@ -662,46 +745,39 @@
         1, grads_1, sum_1, core_recv_1, core_sum_1, x_recv_1, x_sum_1, spot_recv_1, spot_sum_1, x_all_1
     )
     next(narrow)
-    next(wide)
-    base_ref[...] += nt(d_query_low, wq_ref[...])
-    next(narrow)
-    relay_on(0)
-    next(narrow)
-    next(wide)
     near_names = []
     for row in range(ROWS):
         near_names += [node * ROWS + row, local_ref[0, row], local_ref[1, row]]
     near_chosen = selection(near_names)
     for top in range(0, BLK, 16):
-        rows = slice(top, top + 16)
-        acc[:, rows, :] = nn(near_chosen, near_tiles[:, rows, :].reshape(256, D)).reshape(PART, 16, D)
-    for half in range(2):
-        for group in range(4):
-            chosen[half, group] = selection(
-                [
-                    wanted_ref[origin(half, group, step, flip), 0, 2 * dom + slot]
-                    for step in range(4)
-                    for flip in range(2)
-                    for slot in range(2)
-                ]
-            )
-    for chunk in range(1, CHUNKS):
-        relay_on(chunk)
-    combine(0, 0)
-    combine(0, 1)
+        total = nn(near_chosen, near_tiles[:, top : top + 16, :].reshape(256, D)).reshape(PART, 16, D)
+        if top < 2 * SPAN:
+            acc[:, top : top + 16, :] = total
+        else:
+            near_acc[:, top - 2 * SPAN : top - 2 * SPAN + 16, :] = total
     next(narrow)
     next(wide)
-    combine(0, 2)
-    combine(0, 3)
-    crossing = cross(0)
+    lined = [sum_early(half) for half in range(2)]
+    base_ref[...] += nt(d_query_low, wq_ref[...])
+    next(narrow)
+    relay_on(first[:3])
     next(narrow)
     next(wide)
-    for chunk in range(1, CHUNKS):
-        for group in range(4):
-            combine(chunk, group)
-        crossing += cross(chunk)
+    relay_on(first[3:])
+    combine(0)
+    combine(1)
+    turned_copies = [turn_early(half) for half in range(2)]
     next(narrow)
-    base_ref[...] += acc[pl.ds(node * ROWS, ROWS)].reshape(ROWS * BLK, D)
+    next(wide)
+    combine(2)
+    combine(3)
+    crossing = cross()
+    next(narrow)
+    next(wide)
+    for half in range(2):
+        end_early(half)
+    for row in range(ROWS):
+        base_ref[row * BLK : row * BLK + 2 * SPAN, :] += acc[node * ROWS + row]
     next(narrow)
     finish(crossing)
 
@@ -709,12 +785,13 @@
 def finish_kernel(factor, result_ref, base_ref, cross_ref, sum_0, sum_1, out_ref, dx_ref, gq, gk, gv, go, ge, gr):
     out_ref[...] = result_ref[...]
     for row in range(ROWS):
-        for chunk in range(CHUNKS):
-            span = slice(row * BLK + 2 * chunk * SPAN, row * BLK + 2 * (chunk + 1) * SPAN)
-            total = base_ref[span, :]
-            for step in range(N_NODE - 1):
-                total = total + cross_ref[step, chunk, row].astype(F32)
-            dx_ref[span, :] = total.astype(BF16)
+        span = slice(row * BLK, row * BLK + 2 * SPAN)
+        total = base_ref[span, :]
+        for step in range(N_NODE - 1):
+            total = total + cross_ref[step, row].astype(F32)
+        dx_ref[span, :] = total.astype(BF16)
+        span = slice(row * BLK + 2 * SPAN, (row + 1) * BLK)
+        dx_ref[span, :] = base_ref[span, :].astype(BF16)
 
     def piece(ref, index):
         return ref[index * D : (index + 1) * D, :].astype(F32) * factor
@@ -791,7 +868,7 @@
         out_shape=(
             jax.ShapeDtypeStruct((rows, D), BF16),
             jax.ShapeDtypeStruct((rows, D), F32),
-            jax.ShapeDtypeStruct((N_NODE - 1, CHUNKS, ROWS, 2 * SPAN, D), BF16),
+            jax.ShapeDtypeStruct((N_NODE - 1, ROWS, 2 * SPAN, D), BF16),
             jax.ShapeDtypeStruct((SUM_ROWS[0], BLK), BF16),
             jax.ShapeDtypeStruct((SUM_ROWS[1], BLK), BF16),
         ),
@@ -805,13 +882,19 @@
             vmem((ROWS, D, NEAR * BLK), BF16), vmem((ROWS, D, NEAR * BLK), BF16),
             vmem((FAR + 1, BLK, D), BF16), vmem((PART, BLK, D), BF16),
             vmem((2 * D, D), F32), vmem((D, D), F32), vmem((D, 4 * D), F32), vmem((D, 4 * D), F32), vmem((D, D), F32),
-            vmem((SUM_ROWS[0], BLK), BF16), vmem((SUM_ROWS[1], BLK), BF16), vmem(staged, BF16), vmem(staged, BF16),
-            vmem(relay, BF16), vmem(relay, BF16), vmem(land, BF16), vmem(land, BF16),
-            vmem((PART, BLK, D), F32), vmem((2, 4, 256, 256), BF16), vmem((CHUNKS, PART, 2 * SPAN, D), BF16),
+            vmem((SUM_ROWS[0], BLK), BF16), vmem((SUM_ROWS[1], BLK), BF16),
+            vmem((1,) + staged[1:], BF16), vmem((1,) + staged[1:], BF16),
+            vmem((1,) + relay[1:], BF16), vmem((1,) + relay[1:], BF16),
+            vmem((1,) + land[1:], BF16), vmem((1,) + land[1:], BF16),
+            vmem((PART, 2 * SPAN, D), F32), vmem((PART, 2 * SPAN, D), F32),
+            vmem((2, 4, 256, 256), BF16), vmem((PART, 2 * SPAN, D), BF16),
+            vmem((8, 4, 2, SPAN, D), BF16), vmem((8, 4, 2, SPAN, D), BF16), vmem((2, 4, 2, 4, 2, SPAN, D), BF16),
+            vmem((2, 4, PART, SPAN, D), BF16), vmem((2, 3, 4, ROWS, SPAN, D), BF16),
+            vmem((2, 3, ROWS, SPAN, D), BF16), vmem((2, 3, ROWS, SPAN, D), BF16), vmem((2, ROWS, SPAN, D), F32),
         ]
         + sum_scratch
-        + phase_sems
-        + [dma((2, CHUNKS, 3)), dma((2, 2, 2)), dma((2, 2, 2, 3)), dma((2, 2, 2, 15))],
+        + [dma((1, 2, 3)), dma((1, 2, 3)), dma((1, 2, 4, 4, 2)), dma((1, 2, 4, 4, 2))]
+        + [dma((2, 2, 4, 2)), dma((2, 2, 3)), dma((2, 2, 3)), dma((2, 3)), dma((2, 2, 2)), dma((2, 2, 2, 3)), dma((2, 2, 2, 15))],
         compiler_params=pltpu.CompilerParams(
             collective_id=2, has_side_effects=True, vmem_limit_bytes=VMEM_LIMIT
         ),

time: 163 us -> 153 us (0.939)
  Pallas kernels: 163 us -> 153 us
    pallas_call x1, Pallas kernels: 99 us -> 89.2 us  [on_device(): pl.pallas_call(layer_kernel, out_shape=(jax.ShapeDtypeStruct((rows, D), B...]
where the time goes in v5:
time: 153 us
  Pallas kernels  153 us (100%)
    pallas_call x1, Pallas kernels, on_device(): pl.pallas_call(layer_kernel, out_shape=(jax.ShapeDtypeStruct((rows, D), B...  89.2 us
    pallas_call x1, Pallas kernels, on_device(): pl.pallas_call(exchange_kernel, out_shape=(jax.ShapeDtypeStruct((PART, 2...  59.6 us
    pallas_call x1, Pallas kernels, on_device(): pl.pallas_call(functools.partial(finish_kernel, factor), out_shape=(jax.S...  3.84 us

profile of v5, /device:TPU:0, one launch (start us, length us, event | category | flops | bytes accessed | tf_op | source)
XLA Modules:
  0.0 153.3 jit_solution(8449716069957306658)
XLA Ops:
  0.6 59.6 %exchange.1 = (bf16[16,64,256]{2,1,0:T(8,128)(2,1)}, bf16[16,32,256]{2,1,0:T(8,128)(2,1)}, bf16[16,32,256]{2,1,0:T(8,128)(2,1)}, bf16[2,4,4,2,2,32,256]{6,5,4,3,...) custom-call(bf16[4,128,256]{2,1,0:T(8,128)(2,1)} %bitcast.7, ...), custom_call_target="tpu_custom_call" | custom-call | tf_op jit(solution)/shard_map/exchange/pallas_call | solution.py:831
  60.3 89.2 %layer.1 = (bf16[512,256]{1,0:T(8,128)(2,1)}, f32[512,256]{1,0:T(8,128)}, bf16[3,4,64,256]{3,2,1,0:T(8,128)(2,1)}, bf16[4096,128]{1,0:T(8,128)(2,1)}, bf16[2048,128]{1,0:T(8,128)(2,1)}) custom-call(s32[2,4]{1,0:T(2,128)} %bitcast.8, s32[4,4]{1,0:T(4,128)} %slot_ref.3, s32[1,64]{1,0:T(1,128)} %get-tuple-element.21.tile_ref, ...), custom_call_target="tpu_custom_call" | custom-call | tf_op jit(solution)/shard_map/layer/pallas_call | solution.py:866
  149.4 3.8 %finish.1 = (bf16[512,256]{1,0:T(8,128)(2,1)}, bf16[512,256]{1,0:T(8,128)(2,1)}, f32[256,256]{1,0:T(8,128)}, f32[256,256]{1,0:T(8,128)}, f32[256,256]{1,0:T(8,12...) custom-call(bf16[512,256]{1,0:T(8,128)(2,1)} %get-tuple-element.29.result_ref, ...), custom_call_target="tpu_custom_call" | custom-call | tf_op jit(solution)/shard_map/finish/pallas_call | solution.py:908

commit v6 on v5

--- a/solution.py
+++ b/solution.py
@@ -24,6 +24,8 @@
 PART = 16
 KEYS = TILES * BLK
 FAR = ROWS * (TILES - NEAR)
+EARLY = NEAR * BLK
+LATE = EARLY + (KEYS - EARLY) // 2
 N_DOM = 32
 N_NODE = 4
 CHUNKS = 2
@@ -267,18 +269,29 @@
         pick(half, 0)
         deliver(1, half, 0)
 
+    width = KEYS - NEAR * BLK
+    wanted_key = lax.broadcasted_iota(jnp.int32, (width, width), 1)
+    in_late = wanted_key // (width // 2)
+    within = lax.rem(wanted_key, width // 2)
+    old_key = within // (2 * SPAN) * BLK + lax.rem(within, 2 * SPAN) + (1 - in_late) * 2 * SPAN
+    reorder = (lax.broadcasted_iota(jnp.int32, (width, width), 0) == old_key).astype(F32).astype(BF16)
+
     def to_bias(row, carry):
         start = pl.multiple_of(row * BLK, BLK)
         diagonal = lax.broadcasted_iota(jnp.int32, (BLK, BLK), 0) == lax.broadcasted_iota(
             jnp.int32, (BLK, BLK), 1
         )
+        far = []
         for tile in range(TILES):
             allowed = mask_ref[tile, pl.ds(start, BLK), :] > 0
             if tile == 0:
                 allowed = jnp.logical_or(allowed, diagonal)
-            bias_ref[pl.ds(start, BLK), tile * BLK : (tile + 1) * BLK] = jnp.where(
-                allowed, 0.0, NEG
-            ).astype(BF16)
+            bias = jnp.where(allowed, 0.0, NEG).astype(BF16)
+            if tile < NEAR:
+                bias_ref[pl.ds(start, BLK), tile * BLK : (tile + 1) * BLK] = bias
+            else:
+                far.append(bias)
+        bias_ref[pl.ds(start, BLK), NEAR * BLK :] = nn(jnp.concatenate(far, 1), reorder).astype(BF16)
         return carry
 
     lax.fori_loop(0, ROWS, to_bias, 0)
@@ -319,11 +332,11 @@
     wq_ref, wk_ref, wv_ref, wo_ref, we_ref, wr_ref, gain_a_ref, gain_f_ref,
     out_ref, base_ref, cross_ref, sum_0, sum_1,
     fs, ks, vs, qs, ps, mixed, d_mixed, d_query, far_keys_t, far_values_t, near_keys_t, near_values_t,
-    far_tiles, near_tiles, pair_acc, query_acc, expand_acc, reduce_acc, out_acc,
+    far_early, far_late, near_tiles, pair_acc, query_acc, expand_acc, reduce_acc, out_acc,
     grads_0, grads_1, stage_a, stage_b, relay_a, relay_b, land_a, land_b, acc, near_acc, chosen, cross_send,
     plane_a, plane_b, plane_land, line_send, line_land, axis_send, axis_land, axis_own,
     core_recv_0, core_sum_0, x_recv_0, x_sum_0, spot_recv_0, spot_sum_0, x_all_0,
-    core_recv_1, core_sum_1, x_recv_1, x_sum_1, spot_recv_1, spot_sum_1, x_all_1,
+    core_recv_1, core_sum_1, spot_recv_1, spot_sum_1, x_recv_1, x_sum_1, spot_all_1,
     send1, recv1, send2, recv2, plane_sems, line_sems, axis_sems, cross_sems, core_sems, x_sems, spot_sems,
 ):
     dom = lax.axis_index("dom")
@@ -363,7 +376,7 @@
             dy = four(y + 4 - four(asked // 2))
             dc = two(core + two(asked))
             for chunk in range(CHUNKS):
-                top = (NEAR + tile) * BLK + 2 * chunk * SPAN
+                top = (EARLY, LATE)[1 - chunk] + 2 * tile * SPAN
                 fs[row, top : top + SPAN] = far_a[chunk, dz, dy, dc, two(slot)]
                 fs[row, top + SPAN : top + 2 * SPAN] = far_b[chunk, dy, dz, dc, two(slot)]
         tile_rows = fs[row]
@@ -377,13 +390,16 @@
         for pair in range(HEADS // 2):
             both = jnp.concatenate([query * head_low[2 * pair], query * head_low[2 * pair + 1]], 0)
             scores = nt(both, keys) * (scale * log2e)
+            lows = []
             for half in range(2):
                 mine = scores[half * BLK : (half + 1) * BLK] + bias
                 top = jnp.max(mine, -1, keepdims=True)
                 weight = jnp.exp2(mine - top)
                 norm = 1.0 / jnp.sum(weight, -1, keepdims=True)
-                ps[row, (2 * pair + half) * BLK : (2 * pair + half + 1) * BLK, :] = (weight * norm).astype(BF16)
-            got = nn(ps[row, 2 * pair * BLK : (2 * pair + 2) * BLK, :], values)
+                lows.append((weight * norm).astype(BF16))
+            probs_low = jnp.concatenate(lows, 0)
+            ps[row, 2 * pair * BLK : (2 * pair + 2) * BLK, :] = probs_low
+            got = nn(probs_low, values)
             total = total + got[:BLK] * head_f32[2 * pair] + got[BLK:] * head_f32[2 * pair + 1]
         mixed[pl.ds(start, BLK), :] = total
         return carry
@@ -463,19 +479,24 @@
     spots = [(other, (other * 2 + core, node)) for other in spots]
     sibling = device(z, y, two(core + 1), node)
 
-    def reduction(number, grads, total_ref, core_recv, core_sum, x_recv, x_sum, spot_recv, spot_sum, x_all):
+    def reduction(number, grads, total_ref, core_recv, core_sum, recvs, sums, near_all):
+        lines = [(x_line, node, x_sems), (spots, spot_here, spot_sems)]
+        if number == 1:
+            lines.reverse()
+        counts = [len(line[0]) + 1 for line in lines]
         core_rows = SUM_ROWS[number] // 2
-        x_rows = core_rows // 4
-        spot_rows = x_rows // 16
+        sizes = [core_rows // counts[0], core_rows // counts[0] // counts[1]]
         mine = rows_at(core, core_rows)
 
-        def scatter(members, src, dst, sems, count):
+        def scatter(line, src, dst, count):
+            members, own, sems = line
             return [
                 push(src.at[rows_at(other, count)], dst.at[index], sems, (number, 0, index), target)
                 for index, (other, target) in enumerate(members)
             ]
 
-        def gather(members, own, src, dst, sems, count):
+        def gather(line, src, dst, count):
+            members, own, sems = line
             copies = [
                 push(src, dst.at[rows_at(own, count)], sems, (number, 1, index), target)
                 for index, (other, target) in enumerate(members)
@@ -483,8 +504,8 @@
             dst[rows_at(own, count), :] = src[...]
             return copies
 
-        def add_up(own, src, recv, out, count):
-            total = src[rows_at(own, count), :].astype(F32)
+        def add_up(line, src, recv, out, count):
+            total = src[rows_at(line[1], count), :].astype(F32)
             for index in range(recv.shape[0]):
                 total = total + recv[index].astype(F32)
             out[...] = total.astype(BF16)
@@ -493,19 +514,19 @@
         yield
         copy.wait()
         core_sum[...] = (grads[mine, :].astype(F32) + core_recv[...].astype(F32)).astype(BF16)
-        copies = scatter(x_line, core_sum, x_recv, x_sems, x_rows)
+        copies = scatter(lines[0], core_sum, recvs[0], sizes[0])
         yield
         finish(copies)
-        add_up(node, core_sum, x_recv, x_sum, x_rows)
-        copies = scatter(spots, x_sum, spot_recv, spot_sems, spot_rows)
+        add_up(lines[0], core_sum, recvs[0], sums[0], sizes[0])
+        copies = scatter(lines[1], sums[0], recvs[1], sizes[1])
         yield
         finish(copies)
-        add_up(spot_here, x_sum, spot_recv, spot_sum, spot_rows)
-        copies = gather(spots, spot_here, spot_sum, x_all, spot_sems, spot_rows)
+        add_up(lines[1], sums[0], recvs[1], sums[1], sizes[1])
+        copies = gather(lines[1], sums[1], near_all, sizes[1])
         yield
         finish(copies)
         my_part = total_ref.at[mine]
-        copies = gather(x_line, node, x_all, my_part, x_sems, x_rows)
+        copies = gather(lines[0], near_all, my_part, sizes[0])
         yield
         finish(copies)
         copy = push(my_part, my_part, core_sems, (number, 1), sibling)
@@ -553,14 +574,26 @@
         d_values_t = jnp.concatenate(value_parts, 0)
         return d_keys_t, d_values_t, nn(wk_ref[...], d_keys_t) + nn(wv_ref[...], d_values_t), query_part
 
-    def backward_far(row, carry):
-        d_keys_t, d_values_t, d_rows_t, query_part = backward(row, NEAR * BLK, KEYS)
-        far_keys_t[row] = d_keys_t
-        far_values_t[row] = d_values_t
+    def keep_far(row, parts, begin, tiles):
+        d_keys_t, d_values_t, d_rows_t = parts
+        columns = slice(begin - EARLY, begin - EARLY + LATE - EARLY)
+        far_keys_t[row, :, columns] = d_keys_t
+        far_values_t[row, :, columns] = d_values_t
+        for pair in range((TILES - NEAR) // 2):
+            piece = d_rows_t[:, pair * BLK : (pair + 1) * BLK].T.astype(BF16)
+            for side in range(2):
+                tiles[row * (TILES - NEAR) + 2 * pair + side] = piece[side * 2 * SPAN : (side + 1) * 2 * SPAN]
+
+    def backward_early(row, carry):
+        *parts, query_part = backward(row, EARLY, LATE)
+        keep_far(row, parts, EARLY, far_early)
         d_query[rows_at(row, BLK), :] = query_part
-        for tile in range(TILES - NEAR):
-            piece = d_rows_t[:, tile * BLK : (tile + 1) * BLK].T
-            far_tiles[row * (TILES - NEAR) + tile] = piece.astype(BF16)
+        return carry
+
+    def backward_late(row, carry):
+        *parts, query_part = backward(row, LATE, KEYS)
+        keep_far(row, parts, LATE, far_late)
+        d_query[rows_at(row, BLK), :] += query_part
         return carry
 
     def backward_near(row, carry):
@@ -584,16 +617,16 @@
         peer_z, peer_y, side = peer // 8, four(peer // 2), two(peer)
         for slot in range(2):
             tile = tile_ref[0, 2 * peer + slot]
-            plane_a[peer_y * 2 + side, peer_z, slot] = far_tiles[tile, 2 * SPAN : 3 * SPAN]
-            plane_b[peer_z * 2 + side, peer_y, slot] = far_tiles[tile, 3 * SPAN : 4 * SPAN]
+            plane_a[peer_y * 2 + side, peer_z, slot] = far_early[tile, 0:SPAN]
+            plane_b[peer_z * 2 + side, peer_y, slot] = far_early[tile, SPAN : 2 * SPAN]
         return carry
 
     def stage_late(peer, carry):
         turned = four(peer // 2) * 8 + (peer // 8) * 2 + two(peer)
         for slot in range(2):
             tile = tile_ref[0, 2 * peer + slot]
-            stage_a[0, peer, slot] = far_tiles[tile, 0:SPAN]
-            stage_b[0, turned, slot] = far_tiles[tile, SPAN : 2 * SPAN]
+            stage_a[0, peer, slot] = far_late[tile, 0:SPAN]
+            stage_b[0, turned, slot] = far_late[tile, SPAN : 2 * SPAN]
         return carry
 
     def send_early(half):
@@ -716,18 +749,18 @@
     pack((expand_acc, reduce_acc), grads_0)
     pl.semaphore_wait(barrier, len(peers))
     wide = reduction(
-        0, grads_0, sum_0, core_recv_0, core_sum_0, x_recv_0, x_sum_0, spot_recv_0, spot_sum_0, x_all_0
+        0, grads_0, sum_0, core_recv_0, core_sum_0, (x_recv_0, spot_recv_0), (x_sum_0, spot_sum_0), x_all_0
     )
     next(wide)
-    far_tiles[FAR] = jnp.zeros((BLK, D), BF16)
-    lax.fori_loop(0, 2, backward_far, 0)
+    for tiles in (far_early, far_late):
+        tiles[FAR] = jnp.zeros((2 * SPAN, D), BF16)
+    lax.fori_loop(0, ROWS, backward_early, 0)
     next(wide)
-    lax.fori_loop(2, ROWS, backward_far, 0)
-
     lax.fori_loop(0, N_DOM, stage_early, 0)
     early = [send_early(half) for half in range(2)]
+    lax.fori_loop(0, ROWS, backward_late, 0)
+    lax.fori_loop(0, N_DOM, stage_late, 0)
     next(wide)
-    lax.fori_loop(0, N_DOM, stage_late, 0)
     first = first_phase(0, sources, relays, send1, recv1)
     second = {}
     for half in range(2):
@@ -736,15 +769,6 @@
 
     near_tiles[ROWS * NEAR : PART] = jnp.zeros((PART - ROWS * NEAR, BLK, D), BF16)
     lax.fori_loop(0, ROWS, backward_near, 0)
-    pair_acc[...] = jnp.zeros(pair_acc.shape, F32)
-    lax.fori_loop(0, ROWS, key_grads, 0)
-    d_query_low = d_query[...].astype(BF16)
-    query_acc[...] = tn(feat_ref[...], d_query_low)
-    pack((query_acc, pair_acc, out_acc), grads_1)
-    narrow = reduction(
-        1, grads_1, sum_1, core_recv_1, core_sum_1, x_recv_1, x_sum_1, spot_recv_1, spot_sum_1, x_all_1
-    )
-    next(narrow)
     near_names = []
     for row in range(ROWS):
         near_names += [node * ROWS + row, local_ref[0, row], local_ref[1, row]]
@@ -755,9 +779,17 @@
             acc[:, top : top + 16, :] = total
         else:
             near_acc[:, top - 2 * SPAN : top - 2 * SPAN + 16, :] = total
+    lined = [sum_early(half) for half in range(2)]
+    next(wide)
+    pair_acc[...] = jnp.zeros(pair_acc.shape, F32)
+    lax.fori_loop(0, ROWS, key_grads, 0)
+    d_query_low = d_query[...].astype(BF16)
+    query_acc[...] = tn(feat_ref[...], d_query_low)
+    pack((query_acc, pair_acc, out_acc), grads_1)
+    narrow = reduction(
+        1, grads_1, sum_1, core_recv_1, core_sum_1, (spot_recv_1, x_recv_1), (spot_sum_1, x_sum_1), spot_all_1
+    )
     next(narrow)
-    next(wide)
-    lined = [sum_early(half) for half in range(2)]
     base_ref[...] += nt(d_query_low, wq_ref[...])
     next(narrow)
     relay_on(first[:3])
@@ -766,6 +798,7 @@
     relay_on(first[3:])
     combine(0)
     combine(1)
+    next(narrow)
     turned_copies = [turn_early(half) for half in range(2)]
     next(narrow)
     next(wide)
@@ -857,12 +890,13 @@
     )(features.reshape(ROWS, BLK, D), remote_block.reshape(1, 2 * N_DOM), remote_slot, jnp.transpose(tile_mask, (1, 0, 2)))
 
     sum_scratch = []
-    for total in SUM_ROWS:
-        half, eighth, spot = total // 2, total // 8, total // 128
-        sum_scratch += [
-            vmem((half, BLK), BF16), vmem((half, BLK), BF16), vmem((3, eighth, BLK), BF16), vmem((eighth, BLK), BF16),
-            vmem((15, spot, BLK), BF16), vmem((spot, BLK), BF16), vmem((eighth, BLK), BF16),
-        ]
+    for total, lines in zip(SUM_ROWS, ((4, 16), (16, 4))):
+        half = total // 2
+        sum_scratch += [vmem((half, BLK), BF16), vmem((half, BLK), BF16)]
+        for count in lines:
+            half = half // count
+            sum_scratch += [vmem((count - 1, half, BLK), BF16), vmem((half, BLK), BF16)]
+        sum_scratch.append(vmem((total // 2 // lines[0], BLK), BF16))
     result, base, cross, sum_0, sum_1 = pl.pallas_call(
         layer_kernel,
         out_shape=(
@@ -880,7 +914,7 @@
             vmem((rows, D), BF16), vmem((rows, D), F32),
             vmem((ROWS, D, KEYS - NEAR * BLK), BF16), vmem((ROWS, D, KEYS - NEAR * BLK), BF16),
             vmem((ROWS, D, NEAR * BLK), BF16), vmem((ROWS, D, NEAR * BLK), BF16),
-            vmem((FAR + 1, BLK, D), BF16), vmem((PART, BLK, D), BF16),
+            vmem((FAR + 1, 2 * SPAN, D), BF16), vmem((FAR + 1, 2 * SPAN, D), BF16), vmem((PART, BLK, D), BF16),
             vmem((2 * D, D), F32), vmem((D, D), F32), vmem((D, 4 * D), F32), vmem((D, 4 * D), F32), vmem((D, D), F32),
             vmem((SUM_ROWS[0], BLK), BF16), vmem((SUM_ROWS[1], BLK), BF16),
             vmem((1,) + staged[1:], BF16), vmem((1,) + staged[1:], BF16),

time: 153 us -> 150 us (0.980)
  Pallas kernels: 153 us -> 149 us
    pallas_call x1, Pallas kernels: 89.2 us -> 85.6 us  [on_device(): pl.pallas_call(layer_kernel, out_shape=(jax.ShapeDtypeStruct((rows, D), B...]
where the time goes in v6:
time: 150 us
  Pallas kernels  149 us (99%)
    pallas_call x1, Pallas kernels, on_device(): pl.pallas_call(layer_kernel, out_shape=(jax.ShapeDtypeStruct((rows, D), B...  85.6 us
    pallas_call x1, Pallas kernels, on_device(): pl.pallas_call(exchange_kernel, out_shape=(jax.ShapeDtypeStruct((PART, 2...  59.6 us
    pallas_call x1, Pallas kernels, on_device(): pl.pallas_call(functools.partial(finish_kernel, factor), out_shape=(jax.S...  3.84 us

profile of v6, /device:TPU:0, one launch (start us, length us, event | category | flops | bytes accessed | tf_op | source)
XLA Modules:
  0.0 149.7 jit_solution(9068836911079381545)
XLA Ops:
  0.6 59.6 %exchange.1 = (bf16[16,64,256]{2,1,0:T(8,128)(2,1)}, bf16[16,32,256]{2,1,0:T(8,128)(2,1)}, bf16[16,32,256]{2,1,0:T(8,128)(2,1)}, bf16[2,4,4,2,2,32,256]{6,5,4,3,...) custom-call(bf16[4,128,256]{2,1,0:T(8,128)(2,1)} %bitcast.7, ...), custom_call_target="tpu_custom_call" | custom-call | tf_op jit(solution)/shard_map/exchange/pallas_call | solution.py:864
  60.3 85.6 %layer.1 = (bf16[512,256]{1,0:T(8,128)(2,1)}, f32[512,256]{1,0:T(8,128)}, bf16[3,4,64,256]{3,2,1,0:T(8,128)(2,1)}, bf16[4096,128]{1,0:T(8,128)(2,1)}, bf16[2048,128]{1,0:T(8,128)(2,1)}) custom-call(s32[2,4]{1,0:T(2,128)} %bitcast.8, s32[4,4]{1,0:T(4,128)} %slot_ref.3, s32[1,64]{1,0:T(1,128)} %get-tuple-element.21.tile_ref, ...), custom_call_target="tpu_custom_call" | custom-call | tf_op jit(solution)/shard_map/layer/pallas_call | solution.py:900
  145.9 3.8 %finish.1 = (bf16[512,256]{1,0:T(8,128)(2,1)}, bf16[512,256]{1,0:T(8,128)(2,1)}, f32[256,256]{1,0:T(8,128)}, f32[256,256]{1,0:T(8,128)}, f32[256,256]{1,0:T(8,12...) custom-call(bf16[512,256]{1,0:T(8,128)(2,1)} %get-tuple-element.29.result_ref, ...), custom_call_target="tpu_custom_call" | custom-call | tf_op jit(solution)/shard_map/finish/pallas_call | solution.py:942

commit v7 on v6

--- a/solution.py
+++ b/solution.py
@@ -84,22 +84,18 @@
     return lax.rem(value, 2)
 
 
-def first_phase(chunk, sources, relays, sends, recvs):
+def first_step(chunk, half, step, sources, relays, sends, recvs):
     z, y, core, node = place()
-    copies = []
-    for step in range(1, 4):
-        for half in range(2):
-            target = four((z, y)[half] + step)
-            copy = pltpu.make_async_remote_copy(
-                src_ref=sources[half].at[chunk, pl.ds(target * 8, 8)],
-                dst_ref=relays[half].at[chunk, step - 1],
-                send_sem=sends.at[chunk, half, step - 1], recv_sem=recvs.at[chunk, half, step - 1],
-                device_id=(device(target, y, core, node), device(z, target, core, node))[half],
-                device_id_type=MESH,
-            )
-            copy.start()
-            copies.append((half, step, copy))
-    return copies
+    target = four((z, y)[half] + step)
+    copy = pltpu.make_async_remote_copy(
+        src_ref=sources[half].at[chunk, pl.ds(target * 8, 8)],
+        dst_ref=relays[half].at[chunk, step - 1],
+        send_sem=sends.at[chunk, half, step - 1], recv_sem=recvs.at[chunk, half, step - 1],
+        device_id=(device(target, y, core, node), device(z, target, core, node))[half],
+        device_id_type=MESH,
+    )
+    copy.start()
+    return half, step, copy
 
 
 def second_phase(chunk, half, group, sources, relays, lands, sends, recvs):
@@ -142,7 +138,7 @@
 
 def exchange_kernel(
     feat_ref, table_ref, slot_ref, mask_ref,
-    part_0, part_a, part_b, land_a, land_b, wanted_ref, bias_ref, tile_ref,
+    part_0, part_1, part_a, part_b, land_a, land_b, wanted_ref, bias_ref, tile_ref,
     row_ref, stage_a, stage_b, relay_a, relay_b, ids_smem, held_a1, held_a2, held_a3, held_b1, held_b2, held_b3,
     near_send, near_recv, id_send, id_recv, send1, recv1, send2, recv2, line_send, line_recv, x_send, x_recv,
     own_sem, local_sem,
@@ -160,8 +156,9 @@
         pl.semaphore_signal(barrier, inc=1, device_id=target, device_id_type=MESH)
     row_ref[:, 0 : 2 * N_DOM] = table_ref[...]
     mine = pl.ds(node * ROWS, ROWS)
-    part_0[mine] = feat_ref[:, 0 : 2 * SPAN]
+    late = (part_0, part_1)
     for half in range(2):
+        late[half][mine] = feat_ref[:, half * SPAN : (half + 1) * SPAN]
         held[half][0][mine] = feat_ref[:, (2 + half) * SPAN : (3 + half) * SPAN]
     pl.semaphore_wait(barrier, len(OFFSETS) + N_NODE - 1)
 
@@ -177,10 +174,14 @@
         for index, offset in enumerate(OFFSETS)
     ]
     near_copies = [
-        push(
-            feat_ref.at[:, pl.ds(0, 2 * SPAN)], part_0.at[mine], near_send.at[index], near_recv.at[index], target
-        )
-        for index, target in enumerate(x_line)
+        [
+            push(
+                feat_ref.at[:, pl.ds(half * SPAN, SPAN)], late[half].at[mine],
+                near_send.at[half, index], near_recv.at[half, index], target,
+            )
+            for index, target in enumerate(x_line)
+        ]
+        for half in range(2)
     ]
     line_copies = []
     for step in range(1, 4):
@@ -215,13 +216,14 @@
     to_smem.start()
     to_smem.wait()
 
-    def stage(peer, carry):
-        turned = four(peer // 2) * 8 + (peer // 8) * 2 + two(peer)
-        for slot in range(2):
-            block = ids_smem[peer, 0, 2 * dom + slot]
-            stage_a[0, peer, slot] = part_0[block, 0:SPAN]
-            stage_b[0, turned, slot] = part_0[block, SPAN : 2 * SPAN]
-        return carry
+    def stage(half, there):
+        def body(index, carry):
+            peer = dom_at(half, there, index // 2, two(index))
+            for slot in range(2):
+                stages[half][0, there * 8 + index, slot] = late[half][ids_smem[peer, 0, 2 * dom + slot]]
+            return carry
+
+        lax.fori_loop(0, 8, body, 0)
 
     def pick(half, group):
         owner = dom_at(half, four(axis[half] + 4 - group), axis[1 - half], core)
@@ -254,11 +256,15 @@
         copy.start()
         kept.append(copy)
 
-    for copy in near_copies:
-        copy.wait()
-    lax.fori_loop(0, N_DOM, stage, 0)
-    first = first_phase(0, stages, relays, send1, recv1)
+    first = []
     for half in range(2):
+        for copy in near_copies[half]:
+            copy.wait()
+        for step in range(1, 4):
+            stage(half, four(axis[half] + step))
+            first.append(first_step(0, half, step, stages, relays, send1, recv1))
+    for half in range(2):
+        stage(half, axis[half])
         deliver(0, half, 0)
     for half, step, copy in line_copies:
         copy.wait()
@@ -305,7 +311,7 @@
         return carry
 
     lax.fori_loop(0, 2 * N_DOM, tile_of, 0)
-    for half, step, copy in first:
+    for half, step, copy in (first[0], first[3], first[1], first[4], first[2], first[5]):
         copy.wait()
         deliver(0, half, step)
     for group in range(1, 4):
@@ -328,7 +334,7 @@
 
 
 def layer_kernel(
-    local_ref, slot_ref, tile_ref, wanted_ref, feat_ref, part_0, part_a, part_b, far_a, far_b, bias_ref, d_out_ref,
+    local_ref, slot_ref, tile_ref, wanted_ref, feat_ref, part_0, part_1, part_a, part_b, far_a, far_b, bias_ref, d_out_ref,
     wq_ref, wk_ref, wv_ref, wo_ref, we_ref, wr_ref, gain_a_ref, gain_f_ref,
     out_ref, base_ref, cross_ref, sum_0, sum_1,
     fs, ks, vs, qs, ps, mixed, d_mixed, d_query, far_keys_t, far_values_t, near_keys_t, near_values_t,
@@ -366,9 +372,8 @@
         for tile in range(NEAR - 1):
             block = local_ref[tile, row]
             top = (tile + 1) * BLK
-            fs[row, top : top + 2 * SPAN] = part_0[block]
-            fs[row, top + 2 * SPAN : top + 3 * SPAN] = part_a[block]
-            fs[row, top + 3 * SPAN : top + 4 * SPAN] = part_b[block]
+            for index, part_ref in enumerate((part_0, part_1, part_a, part_b)):
+                fs[row, top + index * SPAN : top + (index + 1) * SPAN] = part_ref[block]
         for tile in range(TILES - NEAR):
             slot = slot_ref[row, tile]
             asked = slot // 2
@@ -613,13 +618,15 @@
         pair_acc[D : 2 * D, :] += nn(near_values_t[row], near_rows) + nn(far_values_t[row], far_rows)
         return carry
 
-    def stage_early(peer, carry):
-        peer_z, peer_y, side = peer // 8, four(peer // 2), two(peer)
-        for slot in range(2):
-            tile = tile_ref[0, 2 * peer + slot]
-            plane_a[peer_y * 2 + side, peer_z, slot] = far_early[tile, 0:SPAN]
-            plane_b[peer_z * 2 + side, peer_y, slot] = far_early[tile, SPAN : 2 * SPAN]
-        return carry
+    def stage_early(half):
+        def body(peer, carry):
+            along, across = ((peer // 8, four(peer // 2)), (four(peer // 2), peer // 8))[half]
+            for slot in range(2):
+                tile = tile_ref[0, 2 * peer + slot]
+                planes[half][across * 2 + two(peer), along, slot] = far_early[tile, half * SPAN : (half + 1) * SPAN]
+            return carry
+
+        lax.fori_loop(0, N_DOM, body, 0)
 
     def stage_late(peer, carry):
         turned = four(peer // 2) * 8 + (peer // 8) * 2 + two(peer)
@@ -756,12 +763,16 @@
         tiles[FAR] = jnp.zeros((2 * SPAN, D), BF16)
     lax.fori_loop(0, ROWS, backward_early, 0)
     next(wide)
-    lax.fori_loop(0, N_DOM, stage_early, 0)
-    early = [send_early(half) for half in range(2)]
+    early = []
+    for half in range(2):
+        stage_early(half)
+        early.append(send_early(half))
     lax.fori_loop(0, ROWS, backward_late, 0)
     lax.fori_loop(0, N_DOM, stage_late, 0)
     next(wide)
-    first = first_phase(0, sources, relays, send1, recv1)
+    first = [
+        first_step(0, half, step, sources, relays, send1, recv1) for step in range(1, 4) for half in range(2)
+    ]
     second = {}
     for half in range(2):
         second[half, 0] = second_phase(0, half, 0, sources, relays, lands, send2, recv2)
@@ -815,9 +826,11 @@
     finish(crossing)
 
 
-def finish_kernel(factor, result_ref, base_ref, cross_ref, sum_0, sum_1, out_ref, dx_ref, gq, gk, gv, go, ge, gr):
+def finish_kernel(
+    factor, result_ref, base_ref, cross_ref, expand_ref, reduce_ref, rest_ref, out_ref, dx_ref, gq, gk, gv, go, ge, gr
+):
     out_ref[...] = result_ref[...]
-    for row in range(ROWS):
+    for row in range(ROWS // 2):
         span = slice(row * BLK, row * BLK + 2 * SPAN)
         total = base_ref[span, :]
         for step in range(N_NODE - 1):
@@ -825,20 +838,16 @@
         dx_ref[span, :] = total.astype(BF16)
         span = slice(row * BLK + 2 * SPAN, (row + 1) * BLK)
         dx_ref[span, :] = base_ref[span, :].astype(BF16)
-
-    def piece(ref, index):
-        return ref[index * D : (index + 1) * D, :].astype(F32) * factor
-
     for half in range(2):
         span = slice(half * BLK, (half + 1) * BLK)
-        gq[:, span] = piece(sum_1, half)
-        gk[span, :] = piece(sum_1, 2 + half).T
-        gv[span, :] = piece(sum_1, 4 + half).T
-        go[:, span] = piece(sum_1, 6 + half)
-    for part in range(8):
+        gq[:, span] = rest_ref[half].astype(F32) * factor
+        gk[span, :] = (rest_ref[2 + half].astype(F32) * factor).T
+        gv[span, :] = (rest_ref[4 + half].astype(F32) * factor).T
+        go[:, span] = rest_ref[6 + half].astype(F32) * factor
+    for part in range(4):
         span = slice(part * BLK, (part + 1) * BLK)
-        ge[:, span] = piece(sum_0, part)
-        gr[span, :] = piece(sum_0, 8 + part).T
+        ge[:, span] = expand_ref[part].astype(F32) * factor
+        gr[span, :] = (reduce_ref[part].astype(F32) * factor).T
 
 
 def vmem(shape, dtype):
@@ -861,10 +870,11 @@
     staged = (CHUNKS, N_DOM, 2, SPAN, D)
     relay = (CHUNKS, 3, 8, 2, SPAN, D)
     phase_sems = [dma((CHUNKS, 2, 3)), dma((CHUNKS, 2, 3)), dma((CHUNKS, 2, 4, 4, 2)), dma((CHUNKS, 2, 4, 4, 2))]
-    part_0, part_a, part_b, land_a, land_b, wanted, bias, tile_of = pl.pallas_call(
+    part_0, part_1, part_a, part_b, land_a, land_b, wanted, bias, tile_of = pl.pallas_call(
         exchange_kernel,
         out_shape=(
-            jax.ShapeDtypeStruct((PART, 2 * SPAN, D), BF16),
+            jax.ShapeDtypeStruct((PART, SPAN, D), BF16),
+            jax.ShapeDtypeStruct((PART, SPAN, D), BF16),
             jax.ShapeDtypeStruct((PART, SPAN, D), BF16),
             jax.ShapeDtypeStruct((PART, SPAN, D), BF16),
             jax.ShapeDtypeStruct(land, BF16),
@@ -874,13 +884,13 @@
             jax.ShapeDtypeStruct((1, 2 * N_DOM), jnp.int32),
         ),
         in_specs=[IN_VMEM, IN_VMEM, IN_SMEM, IN_VMEM],
-        out_specs=(IN_VMEM, IN_VMEM, IN_VMEM, ANYWHERE, ANYWHERE, IN_VMEM, IN_VMEM, IN_SMEM),
+        out_specs=(IN_VMEM,) * 4 + (ANYWHERE, ANYWHERE, IN_VMEM, IN_VMEM, IN_SMEM),
         scratch_shapes=[
             vmem((1, BLK), jnp.int32), vmem(staged, BF16), vmem(staged, BF16),
             vmem(relay, BF16), vmem(relay, BF16), pltpu.SMEM((N_DOM, 1, BLK), jnp.int32),
         ]
         + [vmem((PART, SPAN, D), BF16)] * 6
-        + [dma((N_NODE - 1,)), dma((N_NODE - 1,)), dma((peers,)), dma((peers,))]
+        + [dma((2, N_NODE - 1)), dma((2, N_NODE - 1)), dma((peers,)), dma((peers,))]
         + phase_sems
         + [dma((2, 3)), dma((2, 3)), dma((2, 4, 3)), dma((2, 4, 3)), dma((CHUNKS, 2, 4)), dma],
         compiler_params=pltpu.CompilerParams(
@@ -906,7 +916,7 @@
             jax.ShapeDtypeStruct((SUM_ROWS[0], BLK), BF16),
             jax.ShapeDtypeStruct((SUM_ROWS[1], BLK), BF16),
         ),
-        in_specs=[IN_SMEM] * 4 + [IN_VMEM] * 16,
+        in_specs=[IN_SMEM] * 4 + [IN_VMEM] * 17,
         out_specs=(IN_VMEM,) * 5,
         scratch_shapes=[
             vmem((ROWS, KEYS, D), BF16), vmem((ROWS, KEYS, D), BF16), vmem((ROWS, KEYS, D), BF16),
@@ -934,11 +944,12 @@
         ),
         name="layer",
     )(
-        local_block.T, remote_slot, tile_of, wanted, features, part_0, part_a, part_b, land_a, land_b, bias, d_out,
+        local_block.T, remote_slot, tile_of, wanted, features, part_0, part_1, part_a, part_b, land_a, land_b, bias, d_out,
         w_query, w_key, w_value, w_out, w_expand, w_reduce, gain_attn.reshape(1, D), gain_ffn.reshape(1, D),
     )
 
     factor = 1.0 / math.sqrt(rows * N_DOM * N_NODE)
+    pieces = sum_0.reshape(16, D, BLK)
     return pl.pallas_call(
         functools.partial(finish_kernel, factor),
         out_shape=(
@@ -951,11 +962,28 @@
             jax.ShapeDtypeStruct((D, 4 * D), F32),
             jax.ShapeDtypeStruct((4 * D, D), F32),
         ),
-        in_specs=[IN_VMEM] * 5,
-        out_specs=(IN_VMEM,) * 8,
+        grid=(2,),
+        in_specs=[
+            pl.BlockSpec((rows // 2, D), lambda i: (i, 0)),
+            pl.BlockSpec((rows // 2, D), lambda i: (i, 0)),
+            pl.BlockSpec((N_NODE - 1, ROWS // 2, 2 * SPAN, D), lambda i: (0, i, 0, 0)),
+            pl.BlockSpec((4, D, BLK), lambda i: (i, 0, 0)),
+            pl.BlockSpec((4, D, BLK), lambda i: (2 + i, 0, 0)),
+            pl.BlockSpec((8, BLK, BLK), lambda i: (0, i, 0)),
+        ],
+        out_specs=(
+            pl.BlockSpec((rows // 2, D), lambda i: (i, 0)),
+            pl.BlockSpec((rows // 2, D), lambda i: (i, 0)),
+            pl.BlockSpec((BLK, D), lambda i: (i, 0)),
+            pl.BlockSpec((D, BLK), lambda i: (0, i)),
+            pl.BlockSpec((D, BLK), lambda i: (0, i)),
+            pl.BlockSpec((BLK, D), lambda i: (i, 0)),
+            pl.BlockSpec((D, 2 * D), lambda i: (0, i)),
+            pl.BlockSpec((2 * D, D), lambda i: (i, 0)),
+        ),
         compiler_params=pltpu.CompilerParams(vmem_limit_bytes=VMEM_LIMIT),
         name="finish",
-    )(result, base, cross, sum_0, sum_1)
+    )(result, base, cross, pieces, pieces, sum_1.reshape(8, D, BLK))
 
 
 def solution(mesh):

time: 150 us -> 149 us (level)
  no operation moved by 1% of the time
where the time goes in v7:
time: 149 us
  Pallas kernels  148 us (99%)
    pallas_call x1, Pallas kernels, on_device(): pl.pallas_call(layer_kernel, out_shape=(jax.ShapeDtypeStruct((rows, D), B...  85.7 us
    pallas_call x1, Pallas kernels, on_device(): pl.pallas_call(exchange_kernel, out_shape=(jax.ShapeDtypeStruct((PART, SP...  58.9 us
    pallas_call x1, Pallas kernels, on_device(): pl.pallas_call(functools.partial(finish_kernel, factor), out_shape=(jax.S...  3.41 us

profile of v7, /device:TPU:0, one launch (start us, length us, event | category | flops | bytes accessed | tf_op | source)
XLA Modules:
  0.0 148.8 jit_solution(13017150616931113490)
XLA Ops:
  0.6 58.9 %exchange.1 = (bf16[16,32,256]{2,1,0:T(8,128)(2,1)}, bf16[16,32,256]{2,1,0:T(8,128)(2,1)}, bf16[16,32,256]{2,1,0:T(8,128)(2,1)}, bf16[16,32,256]{2,1,0:T(8,128)(...) custom-call(bf16[4,128,256]{2,1,0:T(8,128)(2,1)} %bitcast.11, ...), custom_call_target="tpu_custom_call" | custom-call | tf_op jit(solution)/shard_map/exchange/pallas_call | solution.py:873
  59.6 85.7 %layer.1 = (bf16[512,256]{1,0:T(8,128)(2,1)}, f32[512,256]{1,0:T(8,128)}, bf16[3,4,64,256]{3,2,1,0:T(8,128)(2,1)}, bf16[4096,128]{1,0:T(8,128)(2,1)}, bf16[2048,128]{1,0:T(8,128)(2,1)}) custom-call(s32[2,4]{1,0:T(2,128)} %bitcast.13, s32[4,4]{1,0:T(4,128)} %slot_ref.3, s32[1,64]{1,0:T(1,128)} %get-tuple-element.22.tile_ref, ...), custom_call_target="tpu_custom_call" | custom-call | tf_op jit(solution)/shard_map/layer/pallas_call | solution.py:910
  145.3 3.4 %finish.1 = (bf16[512,256]{1,0:T(8,128)(2,1)}, bf16[512,256]{1,0:T(8,128)(2,1)}, f32[256,256]{1,0:T(8,128)}, f32[256,256]{1,0:T(8,128)}, f32[256,256]{1,0:T(8,12...) custom-call(bf16[512,256]{1,0:T(8,128)(2,1)} %get-tuple-element.31.result_ref, ...), custom_call_target="tpu_custom_call" | custom-call | tf_op jit(solution)/shard_map/finish/pallas_call | solution.py:953

commit v8 on v7

--- a/solution.py
+++ b/solution.py
@@ -810,12 +810,12 @@
     combine(0)
     combine(1)
     next(narrow)
+    combine(2)
+    combine(3)
+    crossing = cross()
     turned_copies = [turn_early(half) for half in range(2)]
     next(narrow)
     next(wide)
-    combine(2)
-    combine(3)
-    crossing = cross()
     next(narrow)
     next(wide)
     for half in range(2):

time: 149 us -> 149 us (level)
  no operation moved by 1% of the time
where the time goes in v8:
time: 149 us; the launch traced here: 148 us
  Pallas kernels  147 us (99%)
    pallas_call x1, Pallas kernels, on_device(): pl.pallas_call(layer_kernel, out_shape=(jax.ShapeDtypeStruct((rows, D), B...  84.6 us
    pallas_call x1, Pallas kernels, on_device(): pl.pallas_call(exchange_kernel, out_shape=(jax.ShapeDtypeStruct((PART, SP...  58.9 us
    pallas_call x1, Pallas kernels, on_device(): pl.pallas_call(functools.partial(finish_kernel, factor), out_shape=(jax.S...  3.41 us

profile of v8, /device:TPU:0, one launch (start us, length us, event | category | flops | bytes accessed | tf_op | source)
XLA Modules:
  0.0 147.7 jit_solution(2733714801313101786)
XLA Ops:
  0.6 58.9 %exchange.1 = (bf16[16,32,256]{2,1,0:T(8,128)(2,1)}, bf16[16,32,256]{2,1,0:T(8,128)(2,1)}, bf16[16,32,256]{2,1,0:T(8,128)(2,1)}, bf16[16,32,256]{2,1,0:T(8,128)(...) custom-call(bf16[4,128,256]{2,1,0:T(8,128)(2,1)} %bitcast.11, ...), custom_call_target="tpu_custom_call" | custom-call | tf_op jit(solution)/shard_map/exchange/pallas_call | solution.py:873
  59.6 84.6 %layer.1 = (bf16[512,256]{1,0:T(8,128)(2,1)}, f32[512,256]{1,0:T(8,128)}, bf16[3,4,64,256]{3,2,1,0:T(8,128)(2,1)}, bf16[4096,128]{1,0:T(8,128)(2,1)}, bf16[2048,128]{1,0:T(8,128)(2,1)}) custom-call(s32[2,4]{1,0:T(2,128)} %bitcast.13, s32[4,4]{1,0:T(4,128)} %slot_ref.3, s32[1,64]{1,0:T(1,128)} %get-tuple-element.22.tile_ref, ...), custom_call_target="tpu_custom_call" | custom-call | tf_op jit(solution)/shard_map/layer/pallas_call | solution.py:910
  144.1 3.4 %finish.1 = (bf16[512,256]{1,0:T(8,128)(2,1)}, bf16[512,256]{1,0:T(8,128)(2,1)}, f32[256,256]{1,0:T(8,128)}, f32[256,256]{1,0:T(8,128)}, f32[256,256]{1,0:T(8,12...) custom-call(bf16[512,256]{1,0:T(8,128)(2,1)} %get-tuple-element.31.result_ref, ...), custom_call_target="tpu_custom_call" | custom-call | tf_op jit(solution)/shard_map/finish/pallas_call | solution.py:953
